TPU v7x, 32 devices: a whole 2x2x4 slice. The times are simulated.
32 devices in a mesh: shift: 4 (over x, core), rows: 8 (over z, y).
Axes of the slice: x: 2, y: 2, z: 4, core: 2. Of those that a mesh axis runs over, the one named last changes fastest.
Arguments:
- neighbours: int32 [64, 8], P('rows'), may hold values from 0 to 63, as said below
- couplings: float32 [64, 8, 128, 128], P('rows'), may hold values from -0.01953125 to 0.01953125
- eigvectors: float32 [64, 128, 128], P('rows'), may hold values from -1 to 1, as said below
- eigvalues: float32 [64, 128], P('rows'), may hold values from -2.5 to 2.5
- start_block: float32 [8192, 128], P('rows'), may hold values from -240 to 240
Outputs:
- basis: float32 [8192, 128], P('rows')
- basis_image: float32 [8192, 128], P('rows')
- projected: float32 [128, 128], replicated
Inputs may be any that keep to these rules, and one draw needn't show every extreme that they name: Each block's 8 neighbours are distinct blocks other than itself, each within 8 blocks of it. `eigvectors`: each block's matrix has orthonormal columns up to rounding.
All inputs are finite; a program needn't handle non-finite values.
Results may differ from a plain program's by a relative error of at most 0.00025.
Values sent between devices are 32-bit elements; how exact they have to be, the bound alone decides.
No kernel may reach another device: no remote copies, remote signals or barrier semaphores. Data moves between devices by JAX's collectives and lax.ppermute only.
A program may use at most 64 MiB of HBM per device.

v0:
```python
import jax
import jax.numpy as jnp
from jax import lax
from jax.sharding import PartitionSpec as P

SWEEPS = 3


radius = 1.0
damping = 0.8


def extended(block, sides, width):
    for axis, dim in sides:
        count = lax.axis_size(axis)
        forward = [(i, i + 1) for i in range(count - 1)]
        backward = [(target, source) for source, target in forward]
        low = lax.ppermute(
            lax.slice_in_dim(block, block.shape[dim] - width, None, axis=dim), axis, forward
        )
        high = lax.ppermute(lax.slice_in_dim(block, 0, width, axis=dim), axis, backward)
        block = jnp.concatenate([low, block, high], axis=dim)
    return block


def unrotate(vectors, field):
    return jnp.einsum("imn,imc->inc", vectors, field, precision=lax.Precision.HIGHEST)


def rotate(vectors, field):
    return jnp.einsum("inm,imc->inc", vectors, field, precision=lax.Precision.HIGHEST)


def shifted_inverse(vectors, values, field, real_part, imag_part):
    width = field.shape[-1] // 2
    spun = unrotate(vectors, field)
    offset = real_part - values
    denom = offset * offset + imag_part * imag_part
    scale_re = (offset / denom)[..., None]
    scale_im = (-imag_part / denom)[..., None]
    first = spun[..., :width]
    second = spun[..., width:]
    mixed = jnp.concatenate(
        [scale_re * first - scale_im * second, scale_re * second + scale_im * first], axis=-1
    )
    return rotate(vectors, mixed)


def diagonal_part(vectors, values, field):
    return rotate(vectors, values[..., None] * unrotate(vectors, field))


def coupled(near_blocks, couplings):
    return jnp.einsum("iknm,ikmc->inc", couplings, near_blocks, precision=lax.Precision.HIGHEST)


def product(left, right):
    return jnp.dot(left, right, precision=lax.Precision.HIGHEST)


def per_device(neighbours, couplings, eigvectors, eigvalues, start_block):
    blk_dev, blk = eigvalues.shape
    ncol = start_block.shape[1]
    rows_here = blk_dev * blk
    total = rows_here * lax.axis_size("rows")
    count = lax.axis_size("shift")
    angle = jnp.pi * (lax.axis_index("shift").astype(jnp.float32) + 0.5) / count
    real_part = radius * jnp.cos(angle)
    imag_part = radius * jnp.sin(angle)
    local_index = neighbours - (lax.axis_index("rows") * blk_dev - blk_dev)

    def operate_on(field, padded):
        blocks_all = padded.reshape(3 * blk_dev, blk, padded.shape[-1])
        near = blocks_all[local_index]
        return diagonal_part(eigvectors, eigvalues, field) + coupled(near, couplings)

    blocks_b = start_block.reshape(blk_dev, blk, ncol)
    rhs = jnp.concatenate([blocks_b, jnp.zeros_like(blocks_b)], axis=-1)
    iterate = damping * shifted_inverse(eigvectors, eigvalues, rhs, real_part, imag_part)
    for sweep in range(1, SWEEPS):
        first = iterate[..., :ncol]
        second = iterate[..., ncol:]
        shifted = jnp.concatenate(
            [real_part * first - imag_part * second, imag_part * first + real_part * second],
            axis=-1,
        )
        iterate_padded = extended(iterate.reshape(rows_here, 2 * ncol), (("rows", 0),), rows_here)
        resid = rhs - shifted + operate_on(iterate, iterate_padded)
        iterate = iterate + damping * shifted_inverse(
            eigvectors, eigvalues, resid, real_part, imag_part
        )
    contrib = real_part / count * iterate[..., :ncol] - imag_part / count * iterate[..., ncol:]
    contrib = contrib.reshape(rows_here, ncol)
    field = lax.psum(contrib, "shift")
    padded = extended(field, (("rows", 0),), rows_here)
    image = operate_on(field.reshape(blk_dev, blk, ncol), padded).reshape(rows_here, ncol)
    gram, moment = lax.psum((product(field.T, field), product(field.T, image)), "rows")
    gram = gram / total
    moment = moment / total
    factor = jnp.linalg.cholesky(gram)
    basis = jax.scipy.linalg.solve_triangular(factor, field.T, lower=True).T
    basis_image = jax.scipy.linalg.solve_triangular(factor, image.T, lower=True).T
    half_way = jax.scipy.linalg.solve_triangular(factor, moment, lower=True)
    projected = jax.scipy.linalg.solve_triangular(factor, half_way.T, lower=True).T
    return (basis, basis_image, projected)


def solution(mesh):
    in_specs = (
        P("rows", None),
        P("rows", None, None, None),
        P("rows", None, None),
        P("rows", None),
        P("rows", None),
    )
    out_specs = (P("rows", None), P("rows", None), P())
    return jax.shard_map(
        per_device, mesh=mesh, in_specs=in_specs, out_specs=out_specs, check_vma=False
    )
```

profile of v0, /device:TPU:0, one launch (start us, length us, event | category | flops | bytes accessed | tf_op | source)
XLA Modules:
  0.0 357.3 jit_solution(10808111391663354559)
XLA Ops:
  7.4 1.2 copy.19
  11.6 1.3 copy.22
  12.9 5.8 %collective-permute-start = (f32[1024,256]{1,0:T(8,128)}, f32[1024,256]{1,0:T(8,128)}, u32[]{:S(2)}, u32[]{:S(2)}) collective-permute-start(f32[1024,256]{1,0:T(8,128)} %bitcast.3), channel_id=1, source_target_pairs={{0,1},{1,2},{2,3},{3,4},{4,5},{5,6},{6,7},{8,9},{9,10},{10,11},{11... | collective-permute-start | bytes 3145736 | tf_op jit(solution)/shard_map/ppermute | solution.py:18
  18.7 1.3 collective-permute-start.1
  20.1 1.1 multiply_subtract_fusion.3
  23.4 39.6 %collective-permute-done = f32[1024,256]{1,0:T(8,128)} collective-permute-done((f32[1024,256]{1,0:T(8,128)}, f32[1024,256]{1,0:T(8,128)}, u32[]{:S(2)}, u32[]{:S(2)}) %collective-permute-start) | collective-permute-done | bytes 1048608 | tf_op jit(solution)/shard_map/ppermute | solution.py:18
  62.9 3.8 %pad_maximum_fusion = f32[3072,256]{1,0:T(8,128)} fusion(f32[1024,256]{1,0:T(8,128)} %collective-permute-done.1, f32[1024,256]{1,0:T(8,128)} %bitcast.3, f32[1024,256]{1,0:T(8,128)} %collective-permute-done), kind=kLoop, calls=%fused_computation.3 | loop fusion | flops 1572864 | bytes 6291456 | tf_op jit(solution)/shard_map/concatenate | solution.py:22
  66.7 6.2 %gather_fusion = f32[64,128,256]{2,1,0:T(8,128)} fusion(f32[24,128,256]{2,1,0:T(8,128)} %bitcast.127, s32[1024]{0:T(1024)S(1)} %pad_clamp_fusion), kind=kCustom, calls=%fused_computation | custom fusion | bytes 16777472 | tf_op jit(solution)/shard_map/gather | solution.py:74
  72.9 17.4 %fusion.11 = f32[8,128,256]{1,2,0:T(8,128)S(1)} fusion(f32[8,256,128]{2,1,0:T(8,128)S(1)} %fusion.42, f32[8,8,128,256]{3,2,1,0:T(8,128)} %bitcast.130, f32[8,8,128,128]{3,2,1,0:T(8,128)} %param.10, f32[8,128,128]{1,2,0:T(8,128)S(1)} %copy.19, f32[8,128,128]{1,2,0:T(8,128)} %get-tuple-element.22, f32[8,128,128]{1,2,0:T(8,128)} %get-tuple-element.21), kind=kOutput, calls=%fused_computation.26 | convolution fusion | flops 3222274048 | bytes 16252928 | tf_op jit(solution)/shard_map/iknm,ikmc->inc/dot_general | solution.py:54
  92.7 1.3 copy.25
  94.0 5.4 %collective-permute-start.2 = (f32[1024,256]{1,0:T(8,128)}, f32[1024,256]{1,0:T(8,128)}, u32[]{:S(2)}, u32[]{:S(2)}) collective-permute-start(f32[1024,256]{1,0:T(8,128)} %bitcast.11), channel_id=1, source_target_pairs={{0,1},{1,2},{2,3},{3,4},{4,5},{5,6},{6,7},{8,9},{9,10},{10,11},{11... | collective-permute-start | bytes 3145736 | tf_op jit(solution)/shard_map/ppermute | solution.py:18
  99.3 1.3 collective-permute-start.3
  100.6 1.1 multiply_subtract_fusion.1
  103.9 38.8 %collective-permute-done.2 = f32[1024,256]{1,0:T(8,128)} collective-permute-done((f32[1024,256]{1,0:T(8,128)}, f32[1024,256]{1,0:T(8,128)}, u32[]{:S(2)}, u32[]{:S(2)}) %collective-permute-start.2) | collective-permute-done | bytes 1048608 | tf_op jit(solution)/shard_map/ppermute | solution.py:18
  142.7 3.8 %pad_maximum_fusion.1 = f32[3072,256]{1,0:T(8,128)} fusion(f32[1024,256]{1,0:T(8,128)} %collective-permute-done.3, f32[1024,256]{1,0:T(8,128)} %bitcast.11, f32[1024,256]{1,0:T(8,128)} %collective-permute-done.2), kind=kLoop, calls=%fused_computation.4 | loop fusion | flops 1572864 | bytes 6291456 | tf_op jit(solution)/shard_map/concatenate | solution.py:22
  146.4 6.2 %gather_fusion.1 = f32[64,128,256]{2,1,0:T(8,128)} fusion(f32[24,128,256]{2,1,0:T(8,128)} %bitcast.128, s32[1024]{0:T(1024)S(1)} %pad_clamp_fusion), kind=kCustom, calls=%fused_computation.1 | custom fusion | bytes 16777472 | tf_op jit(solution)/shard_map/gather | solution.py:74
  152.6 17.7 %fusion.14 = f32[8,128,256]{1,2,0:T(8,128)S(1)} fusion(f32[8,256,128]{2,1,0:T(8,128)S(1)} %fusion.43, f32[8,8,128,256]{3,2,1,0:T(8,128)} %bitcast.129, f32[8,8,128,128]{3,2,1,0:T(8,128)} %param.10, f32[8,128,128]{1,2,0:T(8,128)S(1)} %copy.19, f32[8,128,128]{1,2,0:T(8,128)} %get-tuple-element.20, f32[8,128,128]{1,2,0:T(8,128)} %get-tuple-element.19), kind=kOutput, calls=%fused_computation.29 | convolution fusion | flops 3222274048 | bytes 16252928 | tf_op jit(solution)/shard_map/iknm,ikmc->inc/dot_general | solution.py:54
  171.5 1.1 fusion.6
  173.8 37.4 %all-reduce.5.cloned.1.call-done = f32[1024,128]{1,0:T(8,128)} async-done(((f32[1024,128]{1,0:T(8,128)}), f32[1024,128]{1,0:T(8,128)}) %all-reduce.5.cloned.1.call-update) | async-done | bytes 524304 | tf_op jit(solution)/shard_map/psum | solution.py:94
  211.2 3.5 collective-permute-start.4
  214.7 1.5 collective-permute-start.5
  216.2 2.8 fusion.44
  219.0 2.1 convolution_multiply_fusion.5
  221.1 1.2 fusion.45
  222.3 14.2 %collective-permute-done.4 = f32[1024,128]{1,0:T(8,128)S(1)} collective-permute-done((f32[1024,128]{1,0:T(8,128)}, f32[1024,128]{1,0:T(8,128)S(1)}, u32[]{:S(2)}, u32[]{:S(2)}) %collective-permute-start.4) | collective-permute-done | bytes 524320 | tf_op jit(solution)/shard_map/ppermute | solution.py:18
  236.6 2.8 gather_fusion.2
  239.3 7.9 %fusion.15 = f32[8,128,128]{1,2,0:T(8,128)S(1)} fusion(f32[8,128,128]{1,2,0:T(8,128)S(1)} %fusion.45, f32[8,8,128,128]{3,2,1,0:T(8,128)} %bitcast.135, f32[8,8,128,128]{3,2,1,0:T(8,128)} %param.10), kind=kOutput, calls=%fused_computation.34 | convolution fusion | flops 1610743808 | bytes 9437184 | tf_op jit(solution)/shard_map/iknm,ikmc->inc/dot_general | solution.py:54
  247.3 1.6 fusion.46
  248.9 71.0 %all-reduce.7.cloned.1.call-done = (f32[128,128]{0,1:T(8,128)}, f32[128,128]{0,1:T(8,128)}) async-done(((f32[128,128]{0,1:T(8,128)}, f32[128,128]{0,1:T(8,128)}), (f32[128,128]{0,1:T(8,128)}, f32[128,128]{0,1:T(8,128)})) %all-reduce.7.cloned.1.call-update) | async-done | bytes 131088 | tf_op jit(solution)/shard_map/psum | solution.py:97
  321.7 11.9 %cholesky.18 = f32[128,128]{1,0:T(8,128)S(1)} custom-call(f32[128,128]{1,0:T(8,128)S(1)} %fusion.32), custom_call_target="Cholesky" | custom-call | tf_op jit(solution)/shard_map/jit(cholesky)/cholesky | solution.py:100
  335.0 9.8 %custom-call.11 = f32[1,128,128]{1,2,0:T(8,128)S(1)} custom-call(f32[1,128,128]{2,1,0:T(8,128)S(1)} %fusion.27), custom_call_target="InvertDiagBlocksLowerTriangular" | custom-call | tf_op jit(solution)/shard_map/jit(_solve_triangular)/triangular_solve | solution.py:101
  344.8 1.1 convolution_bitcast_fusion.8
  (46 shorter events, 19.4 us)
Async XLA Ops:
  7.2 1.5 copy-start
  7.2 204.0 %all-reduce.5.cloned.1.call-start = ((), (), s32[]{:S(2)}) async-start(), calls=%async_computation | async-start | bytes 1048576 | tf_op jit(solution)/shard_map/psum | solution.py:94
  8.6 11.4 %copy-start.3 = (s32[8,8]{1,0:T(8,128)S(1)}, s32[8,8]{1,0:T(8,128)}, u32[]{:S(2)}) copy-start(s32[8,8]{1,0:T(8,128)} %param.9) | copy-start | bytes 772
  10.3 10.9 %copy-start.2 = (f32[8,128]{1,0:T(8,128)S(1)}, f32[8,128]{1,0:T(8,128)}, u32[]{:S(2)}) copy-start(f32[8,128]{1,0:T(8,128)} %param.12) | copy-start | bytes 12292
  12.9 50.1 %collective-permute-start = (f32[1024,256]{1,0:T(8,128)}, f32[1024,256]{1,0:T(8,128)}, u32[]{:S(2)}, u32[]{:S(2)}) collective-permute-start(f32[1024,256]{1,0:T(8,128)} %bitcast.3), channel_id=1, source_target_pairs={{0,1},{1,2},{2,3},{3,4},{4,5},{5,6},{6,7},{8,9},{9,10},{10,11},{11... | collective-permute-start | bytes 3145736 | tf_op jit(solution)/shard_map/ppermute | solution.py:18
  18.7 44.2 %collective-permute-start.1 = (f32[1024,256]{1,0:T(8,128)}, f32[1024,256]{1,0:T(8,128)}, u32[]{:S(2)}, u32[]{:S(2)}) collective-permute-start(f32[1024,256]{1,0:T(8,128)} %bitcast.3), channel_id=1, source_target_pairs={{1,0},{2,1},{3,2},{4,3},{5,4},{6,5},{7,6},{9,8},{10,9},{11,10},{12... | collective-permute-start | bytes 3145736 | tf_op jit(solution)/shard_map/ppermute | solution.py:21
  94.0 48.7 %collective-permute-start.2 = (f32[1024,256]{1,0:T(8,128)}, f32[1024,256]{1,0:T(8,128)}, u32[]{:S(2)}, u32[]{:S(2)}) collective-permute-start(f32[1024,256]{1,0:T(8,128)} %bitcast.11), channel_id=1, source_target_pairs={{0,1},{1,2},{2,3},{3,4},{4,5},{5,6},{6,7},{8,9},{9,10},{10,11},{11... | collective-permute-start | bytes 3145736 | tf_op jit(solution)/shard_map/ppermute | solution.py:18
  99.3 43.3 %collective-permute-start.3 = (f32[1024,256]{1,0:T(8,128)}, f32[1024,256]{1,0:T(8,128)}, u32[]{:S(2)}, u32[]{:S(2)}) collective-permute-start(f32[1024,256]{1,0:T(8,128)} %bitcast.11), channel_id=1, source_target_pairs={{1,0},{2,1},{3,2},{4,3},{5,4},{6,5},{7,6},{9,8},{10,9},{11,10},{12... | collective-permute-start | bytes 3145736 | tf_op jit(solution)/shard_map/ppermute | solution.py:21
  173.7 146.2 %all-reduce.7.cloned.1.call-start = ((), (), s32[]{:S(2)}) async-start(), calls=%async_computation.1 | async-start | bytes 262144 | tf_op jit(solution)/shard_map/psum | solution.py:97
  211.2 25.3 %copy-start.1 = (f32[1024,128]{1,0:T(8,128)S(1)}, f32[1024,128]{1,0:T(8,128)}, u32[]{:S(2)}) copy-start(f32[1024,128]{1,0:T(8,128)} %all-reduce.5.cloned.1.call-done) | copy-start | bytes 1572868
  211.2 25.3 %collective-permute-start.4 = (f32[1024,128]{1,0:T(8,128)}, f32[1024,128]{1,0:T(8,128)S(1)}, u32[]{:S(2)}, u32[]{:S(2)}) collective-permute-start(f32[1024,128]{1,0:T(8,128)} %all-reduce.5.cloned.1.call-done), channel_id=1, source_target_pairs={{0,1},{1,2},{2,3},{3,4},{4,5},{5,6},{6,7},{8,9},{9,10},{10,11},{11... | collective-permute-start | bytes 1572872 | tf_op jit(solution)/shard_map/ppermute | solution.py:18
  214.7 21.8 %collective-permute-start.5 = (f32[1024,128]{1,0:T(8,128)}, f32[1024,128]{1,0:T(8,128)S(1)}, u32[]{:S(2)}, u32[]{:S(2)}) collective-permute-start(f32[1024,128]{1,0:T(8,128)} %all-reduce.5.cloned.1.call-done), channel_id=1, source_target_pairs={{1,0},{2,1},{3,2},{4,3},{5,4},{6,5},{7,6},{9,8},{10,9},{11,10},{12... | collective-permute-start | bytes 1572872 | tf_op jit(solution)/shard_map/ppermute | solution.py:21
Sparse Core Ops, SparseCore 0:
  173.9 37.2 all-reduce.4
  249.1 70.8 all-reduce.6
where the time goes:
time: 362 us; the launch traced here: 357 us
  waiting for transfers between devices  201 us (56%)
  matrix products  64.1 us (18%)
  other arithmetic  35.8 us (10%)
  local copies, waits for them, and re-layouts  22.9 us (6%)
  starting transfers between devices  18.8 us (5%)
  between operations  14.7 us (4%)
    ppermute x3, waiting for transfers between devices, extended(): lax.ppermute(lax.slice_in_dim(block, block.shape[dim] - width, None, axis...  92.6 us
    psum x1, waiting for transfers between devices, per_device(): lax.psum((product(field.T, field), product(field.T, image)), 'rows')  71 us
    dot_general x3, matrix products, coupled(): jnp.einsum('iknm,ikmc->inc', couplings, near_blocks, precision=lax.Precis...  43 us
    psum x1, waiting for transfers between devices, per_device(): field = lax.psum(contrib, 'shift')  37.4 us
    gather x3, local copies, waits for them, and re-layouts, operate_on(): near = blocks_all[local_index]  15.1 us
    ppermute x3, starting transfers between devices, extended(): lax.ppermute(lax.slice_in_dim(block, block.shape[dim] - width, None, axis...  14.7 us
    another operation x3, other arithmetic, per_device(): factor = jnp.linalg.cholesky(gram)  12.6 us
    another operation x2, other arithmetic, per_device(): basis = jax.scipy.linalg.solve_triangular(factor, field.T, lower=True).T  10.5 us
  transfers between devices with their start and end apart: 8, of which 5 were waited for; matrix products, arithmetic and copies ran while one was open for 4% of the time, Pallas kernels for 0%

commit v1 on v0

v1 whole, which is shorter than its diff:
```python
import functools

import jax
import jax.numpy as jnp
import numpy as np
from jax import lax
from jax.experimental import pallas as pl
from jax.experimental.pallas import tpu as pltpu
from jax.sharding import PartitionSpec as P

RADIUS = 1.0
DAMPING = 0.8
KEEP = 1.0 - DAMPING
CHUNKS = 4
VMEM_LIMIT = 24 * 1024 * 1024
F32 = jnp.float32
BF16 = jnp.bfloat16


def split(value):
    high = value.astype(BF16)
    low = (value - high.astype(F32)).astype(BF16)
    return high, low


def dot(left, right):
    return jnp.dot(left, right, preferred_element_type=F32)


def dot_three(stacked, high, low):
    half = stacked.shape[0] // 2
    both = dot(stacked, high)
    return both[:half] + both[half:] + dot(stacked[:half], low)


def apply_three(stacked, value):
    return dot_three(stacked, *split(value))


def exact(left, right, contract):
    return lax.dot_general(
        left, right, (contract, ((), ())), precision=lax.Precision.HIGHEST,
        preferred_element_type=F32,
    )


def lane_group(shape, width):
    return lax.broadcasted_iota(jnp.int32, shape, len(shape) - 1) // width


def spread(value, group, width):
    kept = jnp.where(lane_group(value.shape, width) == group, value, 0.0)
    return fold(kept, width)


def fold(value, width):
    lanes = value.shape[-1]
    groups = lanes // width
    if groups & (groups - 1) == 0:
        step = lanes // 2
        while step >= width:
            value = value + pltpu.roll(value, step, value.ndim - 1)
            step //= 2
        return value
    total = value
    for k in range(1, groups):
        total = total + pltpu.roll(value, k * width, value.ndim - 1)
    return total


def column_of(row):
    n = row.shape[1]
    shape = (n, n)
    diagonal = lax.broadcasted_iota(jnp.int32, shape, 0) == lax.broadcasted_iota(jnp.int32, shape, 1)
    return jnp.sum(jnp.where(diagonal, jnp.broadcast_to(row, shape), 0.0), axis=1, keepdims=True)


def inverse_scale(points, energy):
    offset = points[0:1, :] - energy
    imag = points[1:2, :]
    inverse = 1.0 / (offset * offset + imag * imag)
    return offset * inverse, -(imag * inverse)


def call(kernel, out_shape, grid=None, in_specs=None, out_specs=None, scratch=(), flops=0, bytes_accessed=0):
    extra = {}
    if grid is not None:
        extra["grid"] = grid
    return pl.pallas_call(
        kernel,
        out_shape=out_shape,
        in_specs=in_specs,
        out_specs=out_specs,
        scratch_shapes=list(scratch),
        compiler_params=pltpu.CompilerParams(vmem_limit_bytes=VMEM_LIMIT),
        cost_estimate=pl.CostEstimate(flops=flops, bytes_accessed=bytes_accessed, transcendentals=0),
        **extra,
    )


VMEM = functools.partial(pl.BlockSpec, memory_space=pltpu.VMEM)
SMEM = functools.partial(pl.BlockSpec, memory_space=pltpu.SMEM)


def whole(shape):
    return pl.BlockSpec(shape, lambda i: (0,) * len(shape))


def per_device(neighbours, couplings, eigvectors, eigvalues, start_block):
    blk_dev, blk = eigvalues.shape
    nnb = neighbours.shape[1]
    ncol = start_block.shape[1]
    rows_here = blk_dev * blk
    count = lax.axis_size("shift")
    nrows = lax.axis_size("rows")
    total = rows_here * nrows
    width = ncol // count
    packs = blk_dev // count
    wide = 2 * ncol
    here = lax.axis_index("shift")
    me = lax.axis_index("rows")
    paired = nrows % 2 == 0
    halves = 2 if count % 2 == 0 else 1
    per_half = blk_dev // halves
    half_id = here % halves

    angle = np.pi * (np.arange(count, dtype=np.float64) + 0.5) / count
    table = np.zeros((8, ncol), np.float32)
    table[0] = np.repeat(RADIUS * np.cos(angle), width)
    table[1] = np.repeat(RADIUS * np.sin(angle), width)
    table[2] = table[0] / count
    table[3] = table[1] / count
    points = jnp.asarray(table)

    def swap(value):
        if paired:
            return lax.ppermute(value, "rows", [(i, i ^ 1) for i in range(nrows)])
        return lax.ppermute(value, "rows", [(i + 1, i) for i in range(nrows - 1)])

    def pass_on(value, arrived):
        if paired:
            pairs = [(i, i + 2) for i in range(0, nrows - 2, 2)] + [(i, i - 2) for i in range(3, nrows, 2)]
            return lax.ppermute(arrived, "rows", pairs)
        return lax.ppermute(value, "rows", [(i, i + 1) for i in range(nrows - 1)])

    def halo(values):
        first = [swap(v) for v in values]
        second = [pass_on(v, a) for v, a in zip(values, first)]
        return first, second

    def mate(value):
        return lax.ppermute(value, "shift", [(i, i ^ 1) for i in range(count)])

    def gather_shift(value):
        return lax.all_gather(value, "shift")

    def sum_rows(value):
        if nrows & (nrows - 1):
            return lax.psum(value, "rows")
        step = 1
        while step < nrows:
            value = value + lax.ppermute(value, "rows", [(i, i ^ step) for i in range(nrows)])
            step *= 2
        return value

    place = neighbours - (me * blk_dev - blk_dev)
    group = place // blk_dev
    partner_group = jnp.where(me % 2 == 0, 2, 0) if paired else 2
    slot = place % blk_dev + blk_dev * jnp.where(group == 1, 0, jnp.where(group == partner_group, 1, 2))
    slot = slot.astype(jnp.int32)
    position = jnp.stack([here, half_id]).astype(jnp.int32)

    mine = lax.dynamic_slice_in_dim(eigvectors, half_id * per_half, per_half, axis=0)
    cuts = 2 if per_half % 2 == 0 else 1
    sends = jnp.split(mine, cuts, axis=0)
    vec_first, vec_second = halo(sends)
    if halves == 2:
        mate_first = [mate(v) for v in vec_first]
        mate_second = [mate(v) for v in vec_second]
    else:
        mate_first, mate_second = [], []

    def prepare(pos, pts, start, vec, val, spun, packed, vec_st, vec_ts, scale):
        pts = pts[...]
        for i in range(blk_dev):
            tiled = spread(start[i * blk:(i + 1) * blk, :], pos[0], width)
            v = vec[i]
            vh, vl = split(v)
            vec_st[i, :blk, :] = vh
            vec_st[i, blk:, :] = vl
            th, tl = split(v.T)
            vec_ts[i, :blk, :] = th
            vec_ts[i, blk:, :] = tl
            turned = dot_three(jnp.concatenate([th, tl], axis=0), *split(tiled))
            spun[i] = turned
            rows = slice((i // count) * blk, (i // count + 1) * blk)
            kept = jnp.where(lane_group(turned.shape, width) == i % count, turned, 0.0)
            if i % count == 0:
                packed[rows, :] = kept
            else:
                packed[rows, :] += kept
            re, im = inverse_scale(pts, column_of(val[i:i + 1, :]))
            scale[i, :, :ncol] = re
            scale[i, :, ncol:] = im
        packed[packs * blk:, :] = val[...]

    sds = jax.ShapeDtypeStruct
    spun, packed, vec_st, vec_ts, scale = call(
        prepare,
        (
            sds((blk_dev, blk, ncol), F32),
            sds((packs * blk + blk_dev, ncol), F32),
            sds((blk_dev, 2 * blk, blk), BF16),
            sds((blk_dev, 2 * blk, blk), BF16),
            sds((blk_dev, blk, wide), F32),
        ),
        in_specs=[SMEM(), VMEM(), VMEM(), VMEM(), VMEM()],
        out_specs=[VMEM()] * 5,
        flops=6 * blk_dev * blk * blk * ncol,
        bytes_accessed=4 * 6 * blk_dev * blk * blk,
    )(position, points, start_block, eigvectors, eigvalues)

    (pack_first,), (pack_second,) = halo([packed])

    def couple(coup, spun_ref, scale_ref, vec, cst, xh, xl):
        for k in range(nnb):
            ch, cl = split(coup[0, k])
            cst[0, :blk, k * blk:(k + 1) * blk] = ch
            cst[0, blk:, k * blk:(k + 1) * blk] = cl
        b = DAMPING * spun_ref[0]
        s = scale_ref[0]
        x = apply_three(vec[0], jnp.concatenate([s[:, :ncol] * b, s[:, ncol:] * b], axis=1))
        h, l = split(x)
        xh[...] = h
        xl[...] = l

    def block_of(*shape):
        return pl.BlockSpec((1,) + shape, lambda i: (i,) + (0,) * len(shape))

    cst, own_h, own_l = call(
        couple,
        (
            sds((blk_dev, 2 * blk, nnb * blk), BF16),
            sds((rows_here, wide), BF16),
            sds((rows_here, wide), BF16),
        ),
        grid=(blk_dev,),
        in_specs=[block_of(nnb, blk, blk), block_of(blk, ncol), block_of(blk, wide), block_of(2 * blk, blk)],
        out_specs=[
            block_of(2 * blk, nnb * blk),
            pl.BlockSpec((blk, wide), lambda i: (i, 0)),
            pl.BlockSpec((blk, wide), lambda i: (i, 0)),
        ],
        flops=6 * blk_dev * blk * blk * wide,
        bytes_accessed=8 * blk_dev * nnb * blk * blk,
    )(couplings, spun, scale, vec_st)

    n_vec = halves * cuts

    def first_iterate(*refs):
        pos, pts, oh, ol = refs[:4]
        sides = [refs[4:4 + n_vec], refs[4 + n_vec:4 + 2 * n_vec]]
        packs_in = refs[4 + 2 * n_vec:6 + 2 * n_vec]
        xh, xl = refs[6 + 2 * n_vec:]
        xh[:rows_here, :] = oh[...]
        xl[:rows_here, :] = ol[...]
        pts = pts[...]
        per_cut = per_half // cuts
        for side in range(2):
            pack = packs_in[side]
            for h in range(halves):
                base = ((pos[1] + h) % halves) * per_half if halves > 1 else 0
                for c in range(cuts):
                    for j in range(per_cut):
                        b = base + c * per_cut + j
                        row0 = pl.multiple_of((b // count) * blk, blk)
                        turned = spread(pack[pl.ds(row0, blk), :], b % count, width) * DAMPING
                        re, im = inverse_scale(pts, column_of(pack[pl.ds(packs * blk + b, 1), :]))
                        v = sides[side][h * cuts + c][j]
                        vh, vl = split(v)
                        x = apply_three(
                            jnp.concatenate([vh, vl], axis=0),
                            jnp.concatenate([re * turned, im * turned], axis=1),
                        )
                        out0 = pl.multiple_of((b + blk_dev * (1 + side)) * blk, blk)
                        h1, l1 = split(x)
                        xh[pl.ds(out0, blk), :] = h1
                        xl[pl.ds(out0, blk), :] = l1

    field_shape = (sds((3 * rows_here, wide), BF16), sds((3 * rows_here, wide), BF16))
    vec_in = vec_first + mate_first + vec_second + mate_second
    one_h, one_l = call(
        first_iterate,
        field_shape,
        in_specs=[SMEM()] + [VMEM()] * (5 + len(vec_in)),
        out_specs=[VMEM()] * 2,
        flops=12 * blk_dev * blk * blk * wide,
        bytes_accessed=4 * 6 * blk_dev * blk * blk,
    )(position, points, own_h, own_l, *vec_in, pack_first, pack_second)

    def near_of(ref, slots, i):
        return jnp.concatenate(
            [ref[pl.ds(pl.multiple_of(slots[i, k] * blk, blk), blk), :] for k in range(nnb)], axis=0
        )

    def times(s, g):
        re, im = g[:, :ncol], g[:, ncol:]
        sre, sim = s[:, :ncol], s[:, ncol:]
        return jnp.concatenate([sre * re - sim * im, sre * im + sim * re], axis=1)

    def plus_real(g, b):
        return jnp.concatenate([g[:, :ncol] + b, g[:, ncol:]], axis=1)

    def second_iterate(base, slots, xh, xl, c, vec, vec_t, spun_ref, scale_ref, out, out_hat):
        i = pl.program_id(0) + base
        s = dot_three(c[0], near_of(xh, slots, i), near_of(xl, slots, i))
        g = plus_real(apply_three(vec_t[0], s), (1.0 + KEEP) * spun_ref[0])
        hat = times(scale_ref[0], DAMPING * g)
        out_hat[0] = hat
        out[0] = apply_three(vec[0], hat)

    chunks = CHUNKS if blk_dev % CHUNKS == 0 else 1
    per_chunk = blk_dev // chunks

    def shifted(base, *shape):
        return pl.BlockSpec((1,) + shape, lambda i: (i + base,) + (0,) * len(shape))

    own, own_hat = [], []
    for c in range(chunks):
        base = c * per_chunk
        out, hat = call(
            functools.partial(second_iterate, base),
            (sds((per_chunk, blk, wide), F32), sds((per_chunk, blk, wide), F32)),
            grid=(per_chunk,),
            in_specs=[
                SMEM(), whole((3 * rows_here, wide)), whole((3 * rows_here, wide)),
                shifted(base, 2 * blk, nnb * blk), shifted(base, 2 * blk, blk), shifted(base, 2 * blk, blk),
                shifted(base, blk, ncol), shifted(base, blk, wide),
            ],
            out_specs=[block_of(blk, wide), block_of(blk, wide)],
            flops=6 * per_chunk * (nnb + 2) * blk * blk * wide,
            bytes_accessed=4 * 3 * rows_here * wide + 4 * per_chunk * nnb * blk * blk,
        )(slot, one_h, one_l, cst, vec_st, vec_ts, spun, scale)
        own.append(out)
        own_hat.append(hat)

    two_first, two_second = halo(own)

    def third_iterate(*refs):
        slots, pts = refs[:2]
        fields = refs[2:2 + 3 * chunks]
        hats = refs[2 + 3 * chunks:2 + 4 * chunks]
        c, vec, vec_t, spun_ref, scale_ref, val = refs[2 + 4 * chunks:8 + 4 * chunks]
        packed_out, diag_out, xh, xl = refs[8 + 4 * chunks:]
        i = pl.program_id(0)

        @pl.when(i == 0)
        def _():
            for f, field in enumerate(fields):
                for j in range(per_chunk):
                    rows = slice((f * per_chunk + j) * blk, (f * per_chunk + j + 1) * blk)
                    h, l = split(field[j])
                    xh[rows, :] = h
                    xl[rows, :] = l
            packed_out[...] = jnp.zeros_like(packed_out)

        s = dot_three(c[0], near_of(xh, slots, i), near_of(xl, slots, i))
        g = plus_real(apply_three(vec_t[0], s), spun_ref[0])
        hat = hats[0][i % per_chunk]
        for q in range(1, chunks):
            hat = jnp.where(i // per_chunk == q, hats[q][i % per_chunk], hat)
        hat = KEEP * hat + times(scale_ref[0], DAMPING * g)
        term = pts[2:3, :] * hat[:, :ncol] - pts[3:4, :] * hat[:, ncol:]
        turned = fold(term, width)
        energy = column_of(val[pl.ds(i, 1), :])
        both = apply_three(vec[0], jnp.concatenate([turned, energy * turned], axis=1))
        diag_out[0] = both[:, ncol:]
        rows = pl.ds(pl.multiple_of((i // count) * blk, blk), blk)
        packed_out[rows, :] += jnp.where(
            lane_group((blk, ncol), width) == i % count, both[:, :ncol], 0.0
        )

    chunk_spec = whole((per_chunk, blk, wide))
    filtered, diagonal = call(
        third_iterate,
        (sds((packs * blk, ncol), F32), sds((blk_dev, blk, ncol), F32)),
        grid=(blk_dev,),
        in_specs=[SMEM(), whole(points.shape)] + [chunk_spec] * (4 * chunks) + [
            block_of(2 * blk, nnb * blk), block_of(2 * blk, blk), block_of(2 * blk, blk),
            block_of(blk, ncol), block_of(blk, wide), whole((blk_dev, blk)),
        ],
        out_specs=[whole((packs * blk, ncol)), block_of(blk, ncol)],
        scratch=[pltpu.VMEM((3 * rows_here, wide), BF16)] * 2,
        flops=6 * blk_dev * (nnb + 2) * blk * blk * wide,
        bytes_accessed=4 * 4 * rows_here * wide + 4 * blk_dev * nnb * blk * blk,
    )(slot, points, *own, *two_first, *two_second, *own_hat, cst, vec_st, vec_ts, spun, scale, eigvalues)

    (filt_first,), (filt_second,) = halo([filtered])
    filt_all = gather_shift(filtered)

    def unpacked(ref, i):
        rows = slice((i // count) * blk, (i // count + 1) * blk)
        lanes = lane_group((blk, ncol), width)
        out = jnp.zeros((blk, ncol), F32)
        for s in range(count):
            moved = ref[s, rows, :]
            turn = ((s - i % count) * width) % ncol
            if turn:
                moved = pltpu.roll(moved, turn, 1)
            out = jnp.where(lanes == s, moved, out)
        return out

    def gram_of(pieces, full, gram):
        acc = jnp.zeros((ncol, ncol), F32)
        for i in range(blk_dev):
            f = unpacked(pieces, i)
            full[i * blk:(i + 1) * blk, :] = f
            acc = acc + exact(f, f, ((0,), (0,)))
        gram[...] = acc

    full, gram = call(
        gram_of,
        (sds((rows_here, ncol), F32), sds((ncol, ncol), F32)),
        in_specs=[VMEM()], out_specs=[VMEM()] * 2,
        flops=12 * rows_here * ncol * ncol, bytes_accessed=8 * rows_here * ncol,
    )(filt_all)
    gram = sum_rows(gram)

    def image_of(slots, own_f, first_f, second_f, full_ref, c, diag, packed_out, moment, xh, xl):
        i = pl.program_id(0)

        @pl.when(i == 0)
        def _():
            for f, field in enumerate((own_f, first_f, second_f)):
                for b in range(blk_dev):
                    piece = field[(b // count) * blk:(b // count + 1) * blk, :]
                    h, l = split(spread(piece, b % count, width))
                    rows = slice((f * blk_dev + b) * blk, (f * blk_dev + b + 1) * blk)
                    xh[rows, :] = h
                    xl[rows, :] = l
            packed_out[...] = jnp.zeros_like(packed_out)
            moment[...] = jnp.zeros_like(moment)

        image = diag[0] + dot_three(c[0], near_of(xh, slots, i), near_of(xl, slots, i))
        rows = pl.ds(pl.multiple_of((i // count) * blk, blk), blk)
        lanes = lane_group((blk, ncol), width)
        packed_out[rows, :] += jnp.where(lanes == i % count, image, 0.0)
        part = exact(full_ref[...], image, ((0,), (0,)))
        span = ncol // count
        piece = jnp.zeros((span, ncol), F32)
        for s in range(count):
            piece = piece + jnp.where(
                lane_group((span, ncol), width) == s, part[s * span:(s + 1) * span, :], 0.0
            )
        moment[...] += piece

    image, moment = call(
        image_of,
        (sds((packs * blk, ncol), F32), sds((ncol // count, ncol), F32)),
        grid=(blk_dev,),
        in_specs=[SMEM()] + [whole((packs * blk, ncol))] * 3 + [
            pl.BlockSpec((blk, ncol), lambda i: (i, 0)),
            block_of(2 * blk, nnb * blk), block_of(blk, ncol),
        ],
        out_specs=[whole((packs * blk, ncol)), whole((ncol // count, ncol))],
        scratch=[pltpu.VMEM((3 * rows_here, ncol), BF16)] * 2,
        flops=6 * blk_dev * (nnb + 2) * blk * blk * ncol,
        bytes_accessed=4 * blk_dev * nnb * blk * blk,
    )(slot, filtered, filt_first, filt_second, full, cst, diagonal)

    image_all = gather_shift(image)
    moment_all = gather_shift(sum_rows(moment))

    def factor_of(gram_ref, full_ref, inverse, basis_ref):
        tiles = ncol // 8
        a = [gram_ref[t * 8:(t + 1) * 8, :] * (1.0 / total) for t in range(tiles)]
        lanes = lax.broadcasted_iota(jnp.int32, (8, ncol), 1)
        subs = lax.broadcasted_iota(jnp.int32, (8, ncol), 0)
        e = [jnp.where(lanes == subs + t * 8, 1.0, 0.0).astype(F32) for t in range(tiles)]
        for k in range(ncol):
            t, q = divmod(k, 8)
            rp = 1.0 / a[t][q:q + 1, k:k + 1]
            row = a[t][q:q + 1, :] * rp
            erow = e[t][q:q + 1, :] * rp
            for u in range(t, tiles):
                m = jnp.broadcast_to(a[u][:, k:k + 1], (8, ncol))
                if u == t:
                    m = jnp.where(subs > q, m, 0.0)
                a[u] = a[u] - m * row
                e[u] = e[u] - m * erow
        for t in range(tiles):
            pivot = jnp.sum(jnp.where(lanes == subs + t * 8, a[t], 0.0), axis=1, keepdims=True)
            inverse[t * 8:(t + 1) * 8, :] = e[t] * (1.0 / jnp.sqrt(pivot))
        basis_ref[...] = exact(full_ref[...], inverse[...], ((1,), (1,)))

    inverse, basis = call(
        factor_of,
        (sds((ncol, ncol), F32), sds((rows_here, ncol), F32)),
        in_specs=[VMEM()] * 2, out_specs=[VMEM()] * 2,
        flops=12 * rows_here * ncol * ncol, bytes_accessed=8 * rows_here * ncol,
    )(gram, full)

    def project(pieces, moments, inv_ref, image_ref, projected_ref):
        inv = inv_ref[...]
        for i in range(blk_dev):
            image_ref[i * blk:(i + 1) * blk, :] = exact(unpacked(pieces, i), inv, ((1,), (1,)))
        span = ncol // count
        lanes = lane_group((span, ncol), width)
        strips = []
        for g in range(count):
            out = jnp.zeros((span, ncol), F32)
            for s in range(count):
                moved = moments[s]
                turn = ((s - g) * width) % ncol
                if turn:
                    moved = pltpu.roll(moved, turn, 1)
                out = jnp.where(lanes == s, moved, out)
            strips.append(out)
        m = jnp.concatenate(strips, axis=0) * (1.0 / total)
        projected_ref[...] = exact(exact(inv, m, ((1,), (0,))), inv, ((1,), (1,)))

    basis_image, projected = call(
        project,
        (sds((rows_here, ncol), F32), sds((ncol, ncol), F32)),
        in_specs=[VMEM()] * 3, out_specs=[VMEM()] * 2,
        flops=12 * rows_here * ncol * ncol, bytes_accessed=8 * rows_here * ncol,
    )(image_all, moment_all, inverse)
    return (basis, basis_image, projected)


def solution(mesh):
    in_specs = (
        P("rows", None),
        P("rows", None, None, None),
        P("rows", None, None),
        P("rows", None),
        P("rows", None),
    )
    out_specs = (P("rows", None), P("rows", None), P())
    return jax.shard_map(
        per_device, mesh=mesh, in_specs=in_specs, out_specs=out_specs, check_vma=False
    )
```

time: 362 us -> 151 us (0.42); the launches traced: 357 us -> 151 us
  waiting for transfers between devices: 201 us -> 21.2 us
  matrix products: 64.1 us -> 0 us
  Pallas kernels: 0 us -> 50.2 us
  other arithmetic: 35.8 us -> 0.13 us
  starting transfers between devices: 18.8 us -> 52.7 us
  blocking collectives: 0 us -> 18.9 us
  local copies, waits for them, and re-layouts: 22.9 us -> 6.65 us
  between operations: 14.7 us -> 0.98 us
    psum x2 -> x0, waiting for transfers between devices: 108 us -> none  [the longest x1 71 us: per_device(): lax.psum((product(field.T, field), product(field.T, image)), 'rows')]
    ppermute x6 -> x26, waiting for transfers between devices: 92.6 us -> 21.2 us  [the longest x8 8.07 us: pass_on(): return lax.ppermute(arrived, 'rows', pairs)]
    dot_general x17 -> x0, matrix products: 61.4 us -> none  [the longest x3 43 us: coupled(): jnp.einsum('iknm,ikmc->inc', couplings, near_blocks, precision=lax.Precis...]
    pallas_call x0 -> x12, Pallas kernels: none -> 50.2 us  [the longest x1 12.2 us: per_device(): call(factor_of, (sds((ncol, ncol), F32), sds((rows_here, ncol), F32)), in...]
    ppermute x6 -> x26, starting transfers between devices: 18.8 us -> 52.7 us  [the longest x8 32 us: pass_on(): return lax.ppermute(arrived, 'rows', pairs)]
    another operation x5 -> x1, other arithmetic: 23 us -> 0.07 us  [per_device(): position = jnp.stack([here, half_id]).astype(jnp.int32)]
    all_gather x0 -> x3, blocking collectives: none -> 18.9 us  [gather_shift(): return lax.all_gather(value, 'shift')]
    gather x3 -> x0, local copies, waits for them, and re-layouts: 15.1 us -> none  [operate_on(): near = blocks_all[local_index]]
  transfers between devices with their start and end apart: 8 -> 26, of which waited for: 5 -> 8; matrix products, arithmetic and copies ran while one was open for 4% -> 0% of each run, Pallas kernels for 0% -> 17%
where the time goes in v1:
time: 151 us
  starting transfers between devices  52.7 us (35%)
  Pallas kernels  50.2 us (33%)
  waiting for transfers between devices  21.2 us (14%)
  blocking collectives  18.9 us (13%)
  local copies, waits for them, and re-layouts  6.65 us (4%)
    ppermute x8, starting transfers between devices, pass_on(): return lax.ppermute(arrived, 'rows', pairs)  32 us
    all_gather x3, blocking collectives, gather_shift(): return lax.all_gather(value, 'shift')  18.9 us
    pallas_call x1, Pallas kernels, per_device(): call(factor_of, (sds((ncol, ncol), F32), sds((rows_here, ncol), F32)), in...  12.2 us
    pallas_call x4, Pallas kernels, per_device(): call(functools.partial(second_iterate, base), (sds((per_chunk, blk, wide)...  9.93 us
    ppermute x6, starting transfers between devices, sum_rows(): lax.ppermute(value, 'rows', [(i, i ^ step) for i in range(nrows)])  9.8 us
    ppermute x8, starting transfers between devices, swap(): return lax.ppermute(value, 'rows', [(i, i ^ 1) for i in range(nrows)])  9.77 us
    pallas_call x1, Pallas kernels, per_device(): call(third_iterate, (sds((packs * blk, ncol), F32), sds((blk_dev, blk, nc...  9.66 us
    ppermute x8, waiting for transfers between devices, pass_on(): return lax.ppermute(arrived, 'rows', pairs)  8.07 us
  transfers between devices with their start and end apart: 26, of which 8 were waited for; matrix products, arithmetic and copies ran while one was open for 0% of the time, Pallas kernels for 17%

profile of v1, /device:TPU:0, one launch (start us, length us, event | category | flops | bytes accessed | tf_op | source)
XLA Modules:
  0.0 150.7 jit_solution(8121858660358317409)
XLA Ops:
  1.7 3.0 %collective-permute-start = (f32[2,128,128]{2,1,0:T(8,128)S(1)}, f32[2,128,128]{2,1,0:T(8,128)S(1)}, u32[]{:S(2)}, u32[]{:S(2)}) collective-permute-start(f32[2,128,128]{2,1,0:T(8,128)S(1)} %get-tuple-element.60), channel_id=1, source_target_pairs={{0,1},{1,0},{2,3},{3,2},{4,5},{5,4},{6,7},{7,6},{8,9},{9,8},{10,11... | collective-permute-start | bytes 393224 | tf_op jit(solution)/shard_map/ppermute | solution.py:137
  10.2 2.0 %collective-permute-start.8 = (f32[264,128]{1,0:T(8,128)S(1)}, f32[264,128]{1,0:T(8,128)S(1)}, u32[]{:S(2)}, u32[]{:S(2)}) collective-permute-start(f32[264,128]{1,0:T(8,128)S(1)} %get-tuple-element.36), channel_id=1, source_target_pairs={{0,1},{1,0},{2,3},{3,2},{4,5},{5,4},{6,7},{7,6},{8,9},{9,8},{10,11... | collective-permute-start | bytes 405512 | tf_op jit(solution)/shard_map/ppermute | solution.py:137
  12.2 3.5 %collective-permute-start.4 = (f32[2,128,128]{2,1,0:T(8,128)S(1)}, f32[2,128,128]{2,1,0:T(8,128)S(1)}, u32[]{:S(2)}, u32[]{:S(2)}) collective-permute-start(f32[2,128,128]{2,1,0:T(8,128)S(1)} %collective-permute-done.refs_4_), channel_id=1, source_target_pairs={{0,2},{2,4},{4,6},{3,1},{5,3},{7,5},{8,10},{10,12},{12,14},{11,9},... | collective-permute-start | bytes 393224 | tf_op jit(solution)/shard_map/ppermute | solution.py:143
  15.7 3.5 %collective-permute-start.5 = (f32[2,128,128]{2,1,0:T(8,128)S(1)}, f32[2,128,128]{2,1,0:T(8,128)S(1)}, u32[]{:S(2)}, u32[]{:S(2)}) collective-permute-start(f32[2,128,128]{2,1,0:T(8,128)S(1)} %collective-permute-done.1.refs_5_), channel_id=1, source_target_pairs={{0,2},{2,4},{4,6},{3,1},{5,3},{7,5},{8,10},{10,12},{12,14},{11,9},... | collective-permute-start | bytes 393224 | tf_op jit(solution)/shard_map/ppermute | solution.py:143
  19.2 2.2 %copy-done = f32[8,8,128,128]{3,2,1,0:T(8,128)S(1)} copy-done((f32[8,8,128,128]{3,2,1,0:T(8,128)S(1)}, f32[8,8,128,128]{3,2,1,0:T(8,128)}, u32[]{:S(2)}) %copy-start) | copy-done | bytes 4194328
  21.4 2.8 %shard_map.86 = (bf16[8,256,1024]{2,1,0:T(8,128)(2,1)S(1)}, bf16[1024,256]{1,0:T(8,128)(2,1)S(1)}, bf16[1024,256]{1,0:T(8,128)(2,1)S(1)}) custom-call(f32[8,8,128,128]{3,2,1,0:T(8,128)S(1)} %copy-done, f32[8,128,128]{2,1,0:T(8,128)S(1)} %get-tuple-element.31.spun_ref.refs_21_, f32[8,128,256]{2,1,0:T(8,128)S(1)} %get-tuple-element.32.scale_ref.refs_22_, ...), custom_call_target="tpu_custom_call" | custom-call | flops 201326592 | bytes 8388608 | tf_op jit(solution)/shard_map/pallas_call | solution.py:240
  24.8 3.5 %collective-permute-start.9 = (f32[264,128]{1,0:T(8,128)S(1)}, f32[264,128]{1,0:T(8,128)S(1)}, u32[]{:S(2)}, u32[]{:S(2)}) collective-permute-start(f32[264,128]{1,0:T(8,128)S(1)} %collective-permute-done.8.refs_12_), channel_id=1, source_target_pairs={{0,2},{2,4},{4,6},{3,1},{5,3},{7,5},{8,10},{10,12},{12,14},{11,9},... | collective-permute-start | bytes 405512 | tf_op jit(solution)/shard_map/ppermute | solution.py:143
  28.9 2.4 %collective-permute-done.9.refs_13_ = f32[264,128]{1,0:T(8,128)S(1)} collective-permute-done((f32[264,128]{1,0:T(8,128)S(1)}, f32[264,128]{1,0:T(8,128)S(1)}, u32[]{:S(2)}, u32[]{:S(2)}) %collective-permute-start.9) | collective-permute-done | bytes 135200 | tf_op jit(solution)/shard_map/ppermute | solution.py:143
  31.3 2.9 %shard_map.87 = (bf16[3072,256]{1,0:T(8,128)(2,1)S(1)}, bf16[3072,256]{1,0:T(8,128)(2,1)S(1)}) custom-call(s32[2]{0:T(128)S(1)} %pad_add_fusion.pos.refs_0_, f32[8,128]{1,0:T(8,128)S(1)} %copy-done.4, bf16[1024,256]{1,0:T(8,128)(2,1)S(1)} %get-tuple-element.34.refs_2_, bf16[1024,256]{1,0:T(8,128)(2,1)S(1)} %get-tuple-element.35.refs_3_, ...), custom_call_target="tpu_custom_call" | custom-call | flops 402653184 | bytes 3145728 | tf_op jit(solution)/shard_map/pallas_call | solution.py:292
  34.2 2.5 %shard_map.88 = (f32[2,128,256]{2,1,0:T(8,128)S(1)}, f32[2,128,256]{2,1,0:T(8,128)S(1)}) custom-call(s32[8,8]{1,0:T(8,128)S(1)} %fusion.slots.refs_0_, bf16[3072,256]{1,0:T(8,128)(2,1)S(1)} %get-tuple-element.37.xh, bf16[3072,256]{1,0:T(8,128)(2,1)S(1)} %get-tuple-element.38.xl, bf16[8,256,1024]{2,1,0:T(8,128)(2,1)S(1)} %get-tuple-element.39.c.refs_18_, ...), custom_call_target="tpu_custom_call" | custom-call | flops 503316480 | bytes 4194304 | tf_op jit(solution)/shard_map/pallas_call | solution.py:331
  36.7 2.5 %shard_map.89 = (f32[2,128,256]{2,1,0:T(8,128)S(1)}, f32[2,128,256]{2,1,0:T(8,128)S(1)}) custom-call(s32[8,8]{1,0:T(8,128)S(1)} %fusion.slots.refs_0_, bf16[3072,256]{1,0:T(8,128)(2,1)S(1)} %get-tuple-element.37.xh, bf16[3072,256]{1,0:T(8,128)(2,1)S(1)} %get-tuple-element.38.xl, bf16[8,256,1024]{2,1,0:T(8,128)(2,1)S(1)} %get-tuple-element.39.c.refs_18_, ...), custom_call_target="tpu_custom_call" | custom-call | flops 503316480 | bytes 4194304 | tf_op jit(solution)/shard_map/pallas_call | solution.py:331
  39.2 2.5 %shard_map.90 = (f32[2,128,256]{2,1,0:T(8,128)S(1)}, f32[2,128,256]{2,1,0:T(8,128)S(1)}) custom-call(s32[8,8]{1,0:T(8,128)S(1)} %fusion.slots.refs_0_, bf16[3072,256]{1,0:T(8,128)(2,1)S(1)} %get-tuple-element.37.xh, bf16[3072,256]{1,0:T(8,128)(2,1)S(1)} %get-tuple-element.38.xl, bf16[8,256,1024]{2,1,0:T(8,128)(2,1)S(1)} %get-tuple-element.39.c.refs_18_, ...), custom_call_target="tpu_custom_call" | custom-call | flops 503316480 | bytes 4194304 | tf_op jit(solution)/shard_map/pallas_call | solution.py:331
  41.7 2.5 %shard_map.91 = (f32[2,128,256]{2,1,0:T(8,128)S(1)}, f32[2,128,256]{2,1,0:T(8,128)S(1)}) custom-call(s32[8,8]{1,0:T(8,128)S(1)} %fusion.slots.refs_0_, bf16[3072,256]{1,0:T(8,128)(2,1)S(1)} %get-tuple-element.37.xh, bf16[3072,256]{1,0:T(8,128)(2,1)S(1)} %get-tuple-element.38.xl, bf16[8,256,1024]{2,1,0:T(8,128)(2,1)S(1)} %get-tuple-element.39.c.refs_18_, ...), custom_call_target="tpu_custom_call" | custom-call | flops 503316480 | bytes 4194304 | tf_op jit(solution)/shard_map/pallas_call | solution.py:331
  44.3 2.0 %collective-permute-start.11 = (f32[2,128,256]{2,1,0:T(8,128)S(1)}, f32[2,128,256]{2,1,0:T(8,128)S(1)}, u32[]{:S(2)}, u32[]{:S(2)}) collective-permute-start(f32[2,128,256]{2,1,0:T(8,128)S(1)} %get-tuple-element.42.refs_3_), channel_id=1, source_target_pairs={{0,1},{1,0},{2,3},{3,2},{4,5},{5,4},{6,7},{7,6},{8,9},{9,8},{10,11... | collective-permute-start | bytes 786440 | tf_op jit(solution)/shard_map/ppermute | solution.py:137
  48.3 5.2 %collective-permute-done.10.refs_6_ = f32[2,128,256]{2,1,0:T(8,128)S(1)} collective-permute-done((f32[2,128,256]{2,1,0:T(8,128)S(1)}, f32[2,128,256]{2,1,0:T(8,128)S(1)}, u32[]{:S(2)}, u32[]{:S(2)}) %collective-permute-start.10) | collective-permute-done | bytes 262176 | tf_op jit(solution)/shard_map/ppermute | solution.py:137
  53.5 4.4 %collective-permute-start.14 = (f32[2,128,256]{2,1,0:T(8,128)S(1)}, f32[2,128,256]{2,1,0:T(8,128)S(1)}, u32[]{:S(2)}, u32[]{:S(2)}) collective-permute-start(f32[2,128,256]{2,1,0:T(8,128)S(1)} %collective-permute-done.10.refs_6_), channel_id=1, source_target_pairs={{0,2},{2,4},{4,6},{3,1},{5,3},{7,5},{8,10},{10,12},{12,14},{11,9},... | collective-permute-start | bytes 786440 | tf_op jit(solution)/shard_map/ppermute | solution.py:143
  59.1 4.4 %collective-permute-start.15 = (f32[2,128,256]{2,1,0:T(8,128)S(1)}, f32[2,128,256]{2,1,0:T(8,128)S(1)}, u32[]{:S(2)}, u32[]{:S(2)}) collective-permute-start(f32[2,128,256]{2,1,0:T(8,128)S(1)} %collective-permute-done.11.refs_7_), channel_id=1, source_target_pairs={{0,2},{2,4},{4,6},{3,1},{5,3},{7,5},{8,10},{10,12},{12,14},{11,9},... | collective-permute-start | bytes 786440 | tf_op jit(solution)/shard_map/ppermute | solution.py:143
  64.7 4.4 %collective-permute-start.16 = (f32[2,128,256]{2,1,0:T(8,128)S(1)}, f32[2,128,256]{2,1,0:T(8,128)S(1)}, u32[]{:S(2)}, u32[]{:S(2)}) collective-permute-start(f32[2,128,256]{2,1,0:T(8,128)S(1)} %collective-permute-done.12.refs_8_), channel_id=1, source_target_pairs={{0,2},{2,4},{4,6},{3,1},{5,3},{7,5},{8,10},{10,12},{12,14},{11,9},... | collective-permute-start | bytes 786440 | tf_op jit(solution)/shard_map/ppermute | solution.py:143
  69.1 3.8 %collective-permute-start.17 = (f32[2,128,256]{2,1,0:T(8,128)S(1)}, f32[2,128,256]{2,1,0:T(8,128)S(1)}, u32[]{:S(2)}, u32[]{:S(2)}) collective-permute-start(f32[2,128,256]{2,1,0:T(8,128)S(1)} %collective-permute-done.13.refs_9_), channel_id=1, source_target_pairs={{0,2},{2,4},{4,6},{3,1},{5,3},{7,5},{8,10},{10,12},{12,14},{11,9},... | collective-permute-start | bytes 786440 | tf_op jit(solution)/shard_map/ppermute | solution.py:143
  74.6 4.0 %collective-permute-done.17.refs_13_ = f32[2,128,256]{2,1,0:T(8,128)S(1)} collective-permute-done((f32[2,128,256]{2,1,0:T(8,128)S(1)}, f32[2,128,256]{2,1,0:T(8,128)S(1)}, u32[]{:S(2)}, u32[]{:S(2)}) %collective-permute-start.17) | collective-permute-done | bytes 262176 | tf_op jit(solution)/shard_map/ppermute | solution.py:143
  78.6 9.7 %shard_map.92 = (f32[256,128]{1,0:T(8,128)S(1)}, f32[8,128,128]{2,1,0:T(8,128)S(1)}) custom-call(s32[8,8]{1,0:T(8,128)S(1)} %fusion.slots.refs_0_, f32[8,128]{1,0:T(8,128)S(1)} %copy-done.4, f32[2,128,256]{2,1,0:T(8,128)S(1)} %get-tuple-element.41.refs_2_, f32[2,128,256]{2,1,0:T(8,128)S(1)} %get-tuple-element.42.refs_3_, ...), custom_call_target="tpu_custom_call" | custom-call | flops 2013265920 | bytes 8388608 | tf_op jit(solution)/shard_map/pallas_call | solution.py:384
  88.8 7.2 %all-gather = f32[1024,128]{1,0:T(8,128)S(1)} all-gather(f32[256,128]{1,0:T(8,128)S(1)} %get-tuple-element.49.own_f), channel_id=2, replica_groups=mesh['shift'=4,'rows'=8] {'shift'}, dimensions={0}, use_global_device_ids=true | all-gather | bytes 655360 | tf_op jit(solution)/shard_map/all_gather | solution.py:155
  98.7 4.6 %collective-permute-start.22 = (f32[256,128]{1,0:T(8,128)S(1)}, f32[256,128]{1,0:T(8,128)S(1)}, u32[]{:S(2)}, u32[]{:S(2)}) collective-permute-start(f32[256,128]{1,0:T(8,128)S(1)} %collective-permute-done.21.first_f), channel_id=1, source_target_pairs={{0,2},{2,4},{4,6},{3,1},{5,3},{7,5},{8,10},{10,12},{12,14},{11,9},... | collective-permute-start | bytes 393224 | tf_op jit(solution)/shard_map/ppermute | solution.py:143
  103.8 3.8 %collective-permute-done.19 = f32[128,128]{1,0:T(8,128)S(1)} collective-permute-done((f32[128,128]{1,0:T(8,128)S(1)}, f32[128,128]{1,0:T(8,128)S(1)}, u32[]{:S(2)}, u32[]{:S(2)}) %collective-permute-start.19) | collective-permute-done | bytes 65568 | tf_op jit(solution)/shard_map/ppermute | solution.py:162
  107.9 7.8 %shard_map.95 = (f32[256,128]{1,0:T(8,128)S(1)}, f32[32,128]{1,0:T(8,128)S(1)}) custom-call(s32[8,8]{1,0:T(8,128)S(1)} %fusion.slots.refs_0_, f32[256,128]{1,0:T(8,128)S(1)} %get-tuple-element.49.own_f, f32[256,128]{1,0:T(8,128)S(1)} %collective-permute-done.21.first_f, f32[256,128]{1,0:T(8,128)S(1)} %collective-permute-done.22.second_f, ...), custom_call_target="tpu_custom_call" | custom-call | flops 1006632960 | bytes 4194304 | tf_op jit(solution)/shard_map/pallas_call | solution.py:457
  115.7 2.2 %collective-permute-start.23 = (f32[32,128]{1,0:T(8,128)S(1)}, f32[32,128]{1,0:T(8,128)S(1)}, u32[]{:S(2)}, u32[]{:S(2)}) collective-permute-start(f32[32,128]{1,0:T(8,128)S(1)} %get-tuple-element.55), channel_id=1, source_target_pairs={{0,1},{1,0},{2,3},{3,2},{4,5},{5,4},{6,7},{7,6},{8,9},{9,8},{10,11... | collective-permute-start | bytes 49160 | tf_op jit(solution)/shard_map/ppermute | solution.py:162
  119.6 2.2 %collective-permute-start.24 = (f32[32,128]{1,0:T(8,128)S(1)}, f32[32,128]{1,0:T(8,128)S(1)}, u32[]{:S(2)}, u32[]{:S(2)}) collective-permute-start(f32[32,128]{1,0:T(8,128)S(1)} %add.47), channel_id=1, source_target_pairs={{0,2},{1,3},{2,0},{3,1},{4,6},{5,7},{6,4},{7,5},{8,10},{9,11},{10,... | collective-permute-start | bytes 49160 | tf_op jit(solution)/shard_map/ppermute | solution.py:162
  121.8 12.2 %shard_map.94 = (f32[128,128]{1,0:T(8,128)S(1)}, f32[1024,128]{1,0:T(8,128)}) custom-call(f32[128,128]{1,0:T(8,128)S(1)} %add.46.gram_ref, f32[1024,128]{1,0:T(8,128)S(1)} %get-tuple-element.51.full_ref), custom_call_target="tpu_custom_call" | custom-call | flops 201326592 | bytes 1048576 | tf_op jit(solution)/shard_map/pallas_call | solution.py:496
  134.0 2.9 %collective-permute-start.25 = (f32[32,128]{1,0:T(8,128)S(1)}, f32[32,128]{1,0:T(8,128)S(1)}, u32[]{:S(2)}, u32[]{:S(2)}) collective-permute-start(f32[32,128]{1,0:T(8,128)S(1)} %add.48), channel_id=1, source_target_pairs={{0,4},{1,5},{2,6},{3,7},{4,0},{5,1},{6,2},{7,3},{8,12},{9,13},{10,... | collective-permute-start | bytes 49160 | tf_op jit(solution)/shard_map/ppermute | solution.py:162
  136.9 6.5 %all-gather.1 = f32[1024,128]{1,0:T(8,128)S(1)} all-gather(f32[256,128]{1,0:T(8,128)S(1)} %get-tuple-element.54), channel_id=3, replica_groups=mesh['shift'=4,'rows'=8] {'shift'}, dimensions={0}, use_global_device_ids=true | all-gather | bytes 655360 | tf_op jit(solution)/shard_map/all_gather | solution.py:155
  143.4 5.2 %all-gather.2 = f32[128,128]{1,0:T(8,128)S(1)} all-gather(f32[32,128]{1,0:T(8,128)S(1)} %add.49), channel_id=4, replica_groups=mesh['shift'=4,'rows'=8] {'shift'}, dimensions={0}, use_global_device_ids=true | all-gather | bytes 81920 | tf_op jit(solution)/shard_map/all_gather | solution.py:155
  148.7 2.1 %shard_map.96 = (f32[1024,128]{1,0:T(8,128)}, f32[128,128]{1,0:T(8,128)}) custom-call(f32[4,256,128]{2,1,0:T(8,128)S(1)} %bitcast.5, f32[4,32,128]{2,1,0:T(8,128)S(1)} %bitcast.7, f32[128,128]{1,0:T(8,128)S(1)} %get-tuple-element.56.inv_ref), custom_call_target="tpu_custom_call" | custom-call | flops 201326592 | bytes 1048576 | tf_op jit(solution)/shard_map/pallas_call | solution.py:522
  (60 shorter events, 19.6 us)
Async XLA Ops:
  0.6 30.7 %copy-start.4 = (f32[8,128]{1,0:T(8,128)S(1)}, f32[8,128]{1,0:T(8,128)}, u32[]{:S(2)}) copy-start(f32[8,128]{1,0:T(8,128)} %constant.61.clone.pts.refs_1_) | copy-start | bytes 12292
  0.6 28.2 %copy-start.7 = (s32[8,8]{1,0:T(8,128)S(1)}, s32[8,8]{1,0:T(8,128)}, u32[]{:S(2)}) copy-start(s32[8,8]{1,0:T(8,128)} %param.6) | copy-start | bytes 772
  1.7 10.5 %collective-permute-start = (f32[2,128,128]{2,1,0:T(8,128)S(1)}, f32[2,128,128]{2,1,0:T(8,128)S(1)}, u32[]{:S(2)}, u32[]{:S(2)}) collective-permute-start(f32[2,128,128]{2,1,0:T(8,128)S(1)} %get-tuple-element.60), channel_id=1, source_target_pairs={{0,1},{1,0},{2,3},{3,2},{4,5},{5,4},{6,7},{7,6},{8,9},{9,8},{10,11... | collective-permute-start | bytes 393224 | tf_op jit(solution)/shard_map/ppermute | solution.py:137
  4.7 11.0 %collective-permute-start.1 = (f32[2,128,128]{2,1,0:T(8,128)S(1)}, f32[2,128,128]{2,1,0:T(8,128)S(1)}, u32[]{:S(2)}, u32[]{:S(2)}) collective-permute-start(f32[2,128,128]{2,1,0:T(8,128)S(1)} %get-tuple-element.59), channel_id=1, source_target_pairs={{0,1},{1,0},{2,3},{3,2},{4,5},{5,4},{6,7},{7,6},{8,9},{9,8},{10,11... | collective-permute-start | bytes 393224 | tf_op jit(solution)/shard_map/ppermute | solution.py:137
  4.9 1.0 copy-start.1
  5.9 1.0 copy-start.2
  10.2 14.6 %collective-permute-start.8 = (f32[264,128]{1,0:T(8,128)S(1)}, f32[264,128]{1,0:T(8,128)S(1)}, u32[]{:S(2)}, u32[]{:S(2)}) collective-permute-start(f32[264,128]{1,0:T(8,128)S(1)} %get-tuple-element.36), channel_id=1, source_target_pairs={{0,1},{1,0},{2,3},{3,2},{4,5},{5,4},{6,7},{7,6},{8,9},{9,8},{10,11... | collective-permute-start | bytes 405512 | tf_op jit(solution)/shard_map/ppermute | solution.py:137
  12.2 16.1 %collective-permute-start.4 = (f32[2,128,128]{2,1,0:T(8,128)S(1)}, f32[2,128,128]{2,1,0:T(8,128)S(1)}, u32[]{:S(2)}, u32[]{:S(2)}) collective-permute-start(f32[2,128,128]{2,1,0:T(8,128)S(1)} %collective-permute-done.refs_4_), channel_id=1, source_target_pairs={{0,2},{2,4},{4,6},{3,1},{5,3},{7,5},{8,10},{10,12},{12,14},{11,9},... | collective-permute-start | bytes 393224 | tf_op jit(solution)/shard_map/ppermute | solution.py:143
  15.7 12.7 %collective-permute-start.5 = (f32[2,128,128]{2,1,0:T(8,128)S(1)}, f32[2,128,128]{2,1,0:T(8,128)S(1)}, u32[]{:S(2)}, u32[]{:S(2)}) collective-permute-start(f32[2,128,128]{2,1,0:T(8,128)S(1)} %collective-permute-done.1.refs_5_), channel_id=1, source_target_pairs={{0,2},{2,4},{4,6},{3,1},{5,3},{7,5},{8,10},{10,12},{12,14},{11,9},... | collective-permute-start | bytes 393224 | tf_op jit(solution)/shard_map/ppermute | solution.py:143
  19.2 2.2 %copy-start = (f32[8,8,128,128]{3,2,1,0:T(8,128)S(1)}, f32[8,8,128,128]{3,2,1,0:T(8,128)}, u32[]{:S(2)}) copy-start(f32[8,8,128,128]{3,2,1,0:T(8,128)} %coup.1) | copy-start | bytes 12582916
  24.2 4.7 %collective-permute-start.2 = (f32[2,128,128]{2,1,0:T(8,128)S(1)}, f32[2,128,128]{2,1,0:T(8,128)S(1)}, u32[]{:S(2)}, u32[]{:S(2)}) collective-permute-start(f32[2,128,128]{2,1,0:T(8,128)S(1)} %collective-permute-done.refs_4_), channel_id=1, source_target_pairs={{0,8},{8,0},{16,24},{24,16},{1,9},{9,1},{17,25},{25,17},{2,10},{10... | collective-permute-start | bytes 393224 | tf_op jit(solution)/shard_map/ppermute | solution.py:152
  24.3 4.6 %collective-permute-start.3 = (f32[2,128,128]{2,1,0:T(8,128)S(1)}, f32[2,128,128]{2,1,0:T(8,128)S(1)}, u32[]{:S(2)}, u32[]{:S(2)}) collective-permute-start(f32[2,128,128]{2,1,0:T(8,128)S(1)} %collective-permute-done.1.refs_5_), channel_id=1, source_target_pairs={{0,8},{8,0},{16,24},{24,16},{1,9},{9,1},{17,25},{25,17},{2,10},{10... | collective-permute-start | bytes 393224 | tf_op jit(solution)/shard_map/ppermute | solution.py:152
  24.8 6.5 %collective-permute-start.9 = (f32[264,128]{1,0:T(8,128)S(1)}, f32[264,128]{1,0:T(8,128)S(1)}, u32[]{:S(2)}, u32[]{:S(2)}) collective-permute-start(f32[264,128]{1,0:T(8,128)S(1)} %collective-permute-done.8.refs_12_), channel_id=1, source_target_pairs={{0,2},{2,4},{4,6},{3,1},{5,3},{7,5},{8,10},{10,12},{12,14},{11,9},... | collective-permute-start | bytes 405512 | tf_op jit(solution)/shard_map/ppermute | solution.py:143
  28.3 3.1 %collective-permute-start.6 = (f32[2,128,128]{2,1,0:T(8,128)S(1)}, f32[2,128,128]{2,1,0:T(8,128)S(1)}, u32[]{:S(2)}, u32[]{:S(2)}) collective-permute-start(f32[2,128,128]{2,1,0:T(8,128)S(1)} %collective-permute-done.4.refs_8_), channel_id=1, source_target_pairs={{0,8},{8,0},{16,24},{24,16},{1,9},{9,1},{17,25},{25,17},{2,10},{10... | collective-permute-start | bytes 393224 | tf_op jit(solution)/shard_map/ppermute | solution.py:152
  28.4 3.0 %collective-permute-start.7 = (f32[2,128,128]{2,1,0:T(8,128)S(1)}, f32[2,128,128]{2,1,0:T(8,128)S(1)}, u32[]{:S(2)}, u32[]{:S(2)}) collective-permute-start(f32[2,128,128]{2,1,0:T(8,128)S(1)} %collective-permute-done.5.refs_9_), channel_id=1, source_target_pairs={{0,8},{8,0},{16,24},{24,16},{1,9},{9,1},{17,25},{25,17},{2,10},{10... | collective-permute-start | bytes 393224 | tf_op jit(solution)/shard_map/ppermute | solution.py:152
  41.7 36.9 %copy-start.6 = (f32[8,128]{1,0:T(8,128)S(1)}, f32[8,128]{1,0:T(8,128)}, u32[]{:S(2)}) copy-start(f32[8,128]{1,0:T(8,128)} %refs_23_.1) | copy-start | bytes 12292
  44.2 9.3 %collective-permute-start.10 = (f32[2,128,256]{2,1,0:T(8,128)S(1)}, f32[2,128,256]{2,1,0:T(8,128)S(1)}, u32[]{:S(2)}, u32[]{:S(2)}) collective-permute-start(f32[2,128,256]{2,1,0:T(8,128)S(1)} %get-tuple-element.41.refs_2_), channel_id=1, source_target_pairs={{0,1},{1,0},{2,3},{3,2},{4,5},{5,4},{6,7},{7,6},{8,9},{9,8},{10,11... | collective-permute-start | bytes 786440 | tf_op jit(solution)/shard_map/ppermute | solution.py:137
  44.3 14.8 %collective-permute-start.11 = (f32[2,128,256]{2,1,0:T(8,128)S(1)}, f32[2,128,256]{2,1,0:T(8,128)S(1)}, u32[]{:S(2)}, u32[]{:S(2)}) collective-permute-start(f32[2,128,256]{2,1,0:T(8,128)S(1)} %get-tuple-element.42.refs_3_), channel_id=1, source_target_pairs={{0,1},{1,0},{2,3},{3,2},{4,5},{5,4},{6,7},{7,6},{8,9},{9,8},{10,11... | collective-permute-start | bytes 786440 | tf_op jit(solution)/shard_map/ppermute | solution.py:137
  46.3 18.5 %collective-permute-start.12 = (f32[2,128,256]{2,1,0:T(8,128)S(1)}, f32[2,128,256]{2,1,0:T(8,128)S(1)}, u32[]{:S(2)}, u32[]{:S(2)}) collective-permute-start(f32[2,128,256]{2,1,0:T(8,128)S(1)} %get-tuple-element.43.refs_4_), channel_id=1, source_target_pairs={{0,1},{1,0},{2,3},{3,2},{4,5},{5,4},{6,7},{7,6},{8,9},{9,8},{10,11... | collective-permute-start | bytes 786440 | tf_op jit(solution)/shard_map/ppermute | solution.py:137
  46.4 22.8 %collective-permute-start.13 = (f32[2,128,256]{2,1,0:T(8,128)S(1)}, f32[2,128,256]{2,1,0:T(8,128)S(1)}, u32[]{:S(2)}, u32[]{:S(2)}) collective-permute-start(f32[2,128,256]{2,1,0:T(8,128)S(1)} %get-tuple-element.44.refs_5_), channel_id=1, source_target_pairs={{0,1},{1,0},{2,3},{3,2},{4,5},{5,4},{6,7},{7,6},{8,9},{9,8},{10,11... | collective-permute-start | bytes 786440 | tf_op jit(solution)/shard_map/ppermute | solution.py:137
  53.5 19.5 %collective-permute-start.14 = (f32[2,128,256]{2,1,0:T(8,128)S(1)}, f32[2,128,256]{2,1,0:T(8,128)S(1)}, u32[]{:S(2)}, u32[]{:S(2)}) collective-permute-start(f32[2,128,256]{2,1,0:T(8,128)S(1)} %collective-permute-done.10.refs_6_), channel_id=1, source_target_pairs={{0,2},{2,4},{4,6},{3,1},{5,3},{7,5},{8,10},{10,12},{12,14},{11,9},... | collective-permute-start | bytes 786440 | tf_op jit(solution)/shard_map/ppermute | solution.py:143
  59.1 13.9 %collective-permute-start.15 = (f32[2,128,256]{2,1,0:T(8,128)S(1)}, f32[2,128,256]{2,1,0:T(8,128)S(1)}, u32[]{:S(2)}, u32[]{:S(2)}) collective-permute-start(f32[2,128,256]{2,1,0:T(8,128)S(1)} %collective-permute-done.11.refs_7_), channel_id=1, source_target_pairs={{0,2},{2,4},{4,6},{3,1},{5,3},{7,5},{8,10},{10,12},{12,14},{11,9},... | collective-permute-start | bytes 786440 | tf_op jit(solution)/shard_map/ppermute | solution.py:143
  64.7 9.9 %collective-permute-start.16 = (f32[2,128,256]{2,1,0:T(8,128)S(1)}, f32[2,128,256]{2,1,0:T(8,128)S(1)}, u32[]{:S(2)}, u32[]{:S(2)}) collective-permute-start(f32[2,128,256]{2,1,0:T(8,128)S(1)} %collective-permute-done.12.refs_8_), channel_id=1, source_target_pairs={{0,2},{2,4},{4,6},{3,1},{5,3},{7,5},{8,10},{10,12},{12,14},{11,9},... | collective-permute-start | bytes 786440 | tf_op jit(solution)/shard_map/ppermute | solution.py:143
  69.1 9.5 %collective-permute-start.17 = (f32[2,128,256]{2,1,0:T(8,128)S(1)}, f32[2,128,256]{2,1,0:T(8,128)S(1)}, u32[]{:S(2)}, u32[]{:S(2)}) collective-permute-start(f32[2,128,256]{2,1,0:T(8,128)S(1)} %collective-permute-done.13.refs_9_), channel_id=1, source_target_pairs={{0,2},{2,4},{4,6},{3,1},{5,3},{7,5},{8,10},{10,12},{12,14},{11,9},... | collective-permute-start | bytes 786440 | tf_op jit(solution)/shard_map/ppermute | solution.py:143
  88.3 10.4 %collective-permute-start.21 = (f32[256,128]{1,0:T(8,128)S(1)}, f32[256,128]{1,0:T(8,128)S(1)}, u32[]{:S(2)}, u32[]{:S(2)}) collective-permute-start(f32[256,128]{1,0:T(8,128)S(1)} %get-tuple-element.49.own_f), channel_id=1, source_target_pairs={{0,1},{1,0},{2,3},{3,2},{4,5},{5,4},{6,7},{7,6},{8,9},{9,8},{10,11... | collective-permute-start | bytes 393224 | tf_op jit(solution)/shard_map/ppermute | solution.py:137
  97.0 6.2 %collective-permute-start.18 = (f32[128,128]{1,0:T(8,128)S(1)}, f32[128,128]{1,0:T(8,128)S(1)}, u32[]{:S(2)}, u32[]{:S(2)}) collective-permute-start(f32[128,128]{1,0:T(8,128)S(1)} %get-tuple-element.50), channel_id=1, source_target_pairs={{0,1},{1,0},{2,3},{3,2},{4,5},{5,4},{6,7},{7,6},{8,9},{9,8},{10,11... | collective-permute-start | bytes 196616 | tf_op jit(solution)/shard_map/ppermute | solution.py:162
  98.7 9.2 %collective-permute-start.22 = (f32[256,128]{1,0:T(8,128)S(1)}, f32[256,128]{1,0:T(8,128)S(1)}, u32[]{:S(2)}, u32[]{:S(2)}) collective-permute-start(f32[256,128]{1,0:T(8,128)S(1)} %collective-permute-done.21.first_f), channel_id=1, source_target_pairs={{0,2},{2,4},{4,6},{3,1},{5,3},{7,5},{8,10},{10,12},{12,14},{11,9},... | collective-permute-start | bytes 393224 | tf_op jit(solution)/shard_map/ppermute | solution.py:143
  103.3 4.3 %collective-permute-start.19 = (f32[128,128]{1,0:T(8,128)S(1)}, f32[128,128]{1,0:T(8,128)S(1)}, u32[]{:S(2)}, u32[]{:S(2)}) collective-permute-start(f32[128,128]{1,0:T(8,128)S(1)} %add.44), channel_id=1, source_target_pairs={{0,2},{1,3},{2,0},{3,1},{4,6},{5,7},{6,4},{7,5},{8,10},{9,11},{10,... | collective-permute-start | bytes 196616 | tf_op jit(solution)/shard_map/ppermute | solution.py:162
  107.6 10.3 %collective-permute-start.20 = (f32[128,128]{1,0:T(8,128)S(1)}, f32[128,128]{1,0:T(8,128)S(1)}, u32[]{:S(2)}, u32[]{:S(2)}) collective-permute-start(f32[128,128]{1,0:T(8,128)S(1)} %add.45), channel_id=1, source_target_pairs={{0,4},{1,5},{2,6},{3,7},{4,0},{5,1},{6,2},{7,3},{8,12},{9,13},{10,... | collective-permute-start | bytes 196616 | tf_op jit(solution)/shard_map/ppermute | solution.py:162
  115.7 3.9 %collective-permute-start.23 = (f32[32,128]{1,0:T(8,128)S(1)}, f32[32,128]{1,0:T(8,128)S(1)}, u32[]{:S(2)}, u32[]{:S(2)}) collective-permute-start(f32[32,128]{1,0:T(8,128)S(1)} %get-tuple-element.55), channel_id=1, source_target_pairs={{0,1},{1,0},{2,3},{3,2},{4,5},{5,4},{6,7},{7,6},{8,9},{9,8},{10,11... | collective-permute-start | bytes 49160 | tf_op jit(solution)/shard_map/ppermute | solution.py:162
  119.6 14.4 %collective-permute-start.24 = (f32[32,128]{1,0:T(8,128)S(1)}, f32[32,128]{1,0:T(8,128)S(1)}, u32[]{:S(2)}, u32[]{:S(2)}) collective-permute-start(f32[32,128]{1,0:T(8,128)S(1)} %add.47), channel_id=1, source_target_pairs={{0,2},{1,3},{2,0},{3,1},{4,6},{5,7},{6,4},{7,5},{8,10},{9,11},{10,... | collective-permute-start | bytes 49160 | tf_op jit(solution)/shard_map/ppermute | solution.py:162
  134.0 9.4 %collective-permute-start.25 = (f32[32,128]{1,0:T(8,128)S(1)}, f32[32,128]{1,0:T(8,128)S(1)}, u32[]{:S(2)}, u32[]{:S(2)}) collective-permute-start(f32[32,128]{1,0:T(8,128)S(1)} %add.48), channel_id=1, source_target_pairs={{0,4},{1,5},{2,6},{3,7},{4,0},{5,1},{6,2},{7,3},{8,12},{9,13},{10,... | collective-permute-start | bytes 49160 | tf_op jit(solution)/shard_map/ppermute | solution.py:162
  (2 other events, 1.4 us)

commit v2 on v0

v2 whole, which is shorter than its diff:
```python
import functools

import jax
import jax.numpy as jnp
import numpy as np
from jax import lax
from jax.experimental import pallas as pl
from jax.experimental.pallas import tpu as pltpu
from jax.sharding import PartitionSpec as P

RADIUS = 1.0
DAMPING = 0.8
CHUNKS = 4
KEEP = 1.0 - DAMPING
VMEM_LIMIT = 24 * 1024 * 1024
FLOPS_PER_MICRO = 1.1e9
GRAM_MICROS = 6.0
F32 = jnp.float32
BF16 = jnp.bfloat16


def split(value):
    high = value.astype(BF16)
    low = (value - high.astype(F32)).astype(BF16)
    return high, low


def dot(left, right):
    return jnp.dot(left, right, preferred_element_type=F32)


def dot_three(stacked, high, low):
    half = stacked.shape[0] // 2
    both = dot(stacked, high)
    return both[:half] + both[half:] + dot(stacked[:half], low)


def apply_three(stacked, value):
    return dot_three(stacked, *split(value))


def exact(left, right, contract):
    return lax.dot_general(
        left, right, (contract, ((), ())), precision=lax.Precision.HIGHEST,
        preferred_element_type=F32,
    )


def lane_group(shape, width):
    return lax.broadcasted_iota(jnp.int32, shape, len(shape) - 1) // width


def spread(value, group, width):
    kept = jnp.where(lane_group(value.shape, width) == group, value, 0.0)
    return fold(kept, width)


def fold(value, width):
    lanes = value.shape[-1]
    groups = lanes // width
    if groups & (groups - 1) == 0:
        step = lanes // 2
        while step >= width:
            value = value + pltpu.roll(value, step, value.ndim - 1)
            step //= 2
        return value
    total = value
    for k in range(1, groups):
        total = total + pltpu.roll(value, k * width, value.ndim - 1)
    return total


def column_of(row):
    n = row.shape[1]
    shape = (n, n)
    diagonal = lax.broadcasted_iota(jnp.int32, shape, 0) == lax.broadcasted_iota(jnp.int32, shape, 1)
    return jnp.sum(jnp.where(diagonal, jnp.broadcast_to(row, shape), 0.0), axis=1, keepdims=True)


def lane_table(values, shape, width):
    groups = lane_group(shape, width)
    out = jnp.full(shape, float(values[0]), F32)
    for j in range(1, len(values)):
        out = jnp.where(groups == j, float(values[j]), out)
    return out


def call(kernel, out_shape, in_specs, scratch=(), micros=1.0):
    single = not isinstance(out_shape, (tuple, list))
    return pl.pallas_call(
        kernel,
        out_shape=out_shape,
        in_specs=in_specs,
        out_specs=VMEM() if single else [VMEM()] * len(out_shape),
        scratch_shapes=list(scratch),
        compiler_params=pltpu.CompilerParams(vmem_limit_bytes=VMEM_LIMIT),
        cost_estimate=pl.CostEstimate(flops=int(micros * FLOPS_PER_MICRO), bytes_accessed=0, transcendentals=0),
    )


VMEM = functools.partial(pl.BlockSpec, memory_space=pltpu.VMEM)
SMEM = functools.partial(pl.BlockSpec, memory_space=pltpu.SMEM)
HBM = functools.partial(pl.BlockSpec, memory_space=pltpu.HBM)


def per_device(neighbours, couplings, eigvectors, eigvalues, start_block):
    blk_dev, blk = eigvalues.shape
    nnb = neighbours.shape[1]
    ncol = start_block.shape[1]
    rows_here = blk_dev * blk
    count = lax.axis_size("shift")
    nrows = lax.axis_size("rows")
    total = rows_here * nrows
    width = ncol // count
    packs = blk_dev // count
    wide = 2 * ncol
    here = lax.axis_index("shift")
    me = lax.axis_index("rows")
    paired = nrows % 2 == 0
    halves = 2 if count % 2 == 0 else 1
    per_half = blk_dev // halves
    half_id = here % halves

    angle = np.pi * (np.arange(count, dtype=np.float64) + 0.5) / count
    real_parts = RADIUS * np.cos(angle)
    imag_parts = RADIUS * np.sin(angle)

    def inverse_scale(energy):
        offset = lane_table(real_parts, (1, ncol), width) - energy
        imag = lane_table(imag_parts, (1, ncol), width)
        inverse = 1.0 / (offset * offset + imag * imag)
        return offset * inverse, -(imag * inverse)

    def own_group():
        return lax.axis_index("shift")

    def block_rows(i):
        return slice((i // count) * blk, (i // count + 1) * blk)

    def store_packed(ref, i, value):
        kept = jnp.where(lane_group(value.shape, width) == i % count, value, 0.0)
        if i % count == 0:
            ref[block_rows(i), :] = kept
        else:
            ref[block_rows(i), :] += kept

    def swap(value):
        if paired:
            return lax.ppermute(value, "rows", [(i, i ^ 1) for i in range(nrows)])
        return lax.ppermute(value, "rows", [(i + 1, i) for i in range(nrows - 1)])

    def pass_on(value, arrived):
        if paired:
            pairs = [(i, i + 2) for i in range(0, nrows - 2, 2)] + [(i, i - 2) for i in range(3, nrows, 2)]
            return lax.ppermute(arrived, "rows", pairs)
        return lax.ppermute(value, "rows", [(i, i + 1) for i in range(nrows - 1)])

    def after(value, *others):
        return lax.optimization_barrier((value,) + others)[0]

    def halo(values):
        first = [swap(v) for v in values]
        second = [pass_on(v, a) for v, a in zip(values, first)]
        return first, second

    def mate(value):
        return lax.ppermute(value, "shift", [(i, i ^ 1) for i in range(count)])

    def gather_pairs(value):
        if count & (count - 1):
            return gather_shift(value)
        rows_each = value.shape[0]
        step = 1
        while step < count:
            value = jnp.concatenate(
                [value, lax.ppermute(value, "shift", [(i, i ^ step) for i in range(count)])], axis=0
            )
            step *= 2
        return [value[k * rows_each:(k + 1) * rows_each] for k in range(count)]

    def gather_shift(value):
        return [value] + [
            lax.ppermute(value, "shift", [(source(i, k), i) for i in range(count)]) for k in range(1, count)
        ]

    def source(i, k):
        return i ^ k if count & (count - 1) == 0 else (i + count - k) % count

    def sum_rows(value):
        if nrows & (nrows - 1):
            return lax.psum(value, "rows")
        step = 1
        while step < nrows:
            value = value + lax.ppermute(value, "rows", [(i, i ^ step) for i in range(nrows)])
            step *= 2
        return value

    place = neighbours - (me * blk_dev - blk_dev)
    group = place // blk_dev
    partner_group = jnp.where(me % 2 == 0, 2, 0) if paired else 2
    slot = place % blk_dev + blk_dev * jnp.where(group == 1, 0, jnp.where(group == partner_group, 1, 2))
    slot = slot.astype(jnp.int32)

    mine = lax.dynamic_slice_in_dim(eigvectors, half_id * per_half, per_half, axis=0)
    cuts = 1
    per_cut = per_half // cuts
    sends = [v.reshape(per_cut * blk, blk) for v in jnp.split(mine, cuts, axis=0)]
    sends[0] = jnp.concatenate([sends[0], eigvalues], axis=0)
    vec_first = [swap(v) for v in sends]
    def prepare(start_hbm, vec_hbm, spun, packed, vec_st, vec_ts, start, vec, sems):
        copies = []
        for i in range(blk_dev):
            rows = pl.ds(i * blk, blk)
            copies.append(pltpu.make_async_copy(vec_hbm.at[i], vec.at[i], sems.at[i]))
            copies.append(pltpu.make_async_copy(start_hbm.at[rows], start.at[rows], sems.at[blk_dev + i]))
        for copy in copies:
            copy.start()
        for copy in copies:
            copy.wait()
        mine_now = own_group()
        lefts, rights = [], []
        for i in range(blk_dev):
            v = vec[i]
            vh, vl = split(v)
            vec_st[i, :blk, :] = vh
            vec_st[i, blk:, :] = vl
            th, tl = split(v.T)
            vec_ts[i, :blk, :] = th
            vec_ts[i, blk:, :] = tl
            lefts.append(jnp.concatenate([th, tl], axis=0))
            rights.append(split(spread(start[i * blk:(i + 1) * blk, :], mine_now, width)))
        turned = [dot_three(left, *right) for left, right in zip(lefts, rights)]
        for i in range(blk_dev):
            spun[i] = turned[i]
            store_packed(packed, i, turned[i])

    sds = jax.ShapeDtypeStruct
    spun, packed, vec_st, vec_ts = call(
        prepare,
        (
            sds((blk_dev, blk, ncol), F32),
            sds((packs * blk, ncol), F32),
            sds((blk_dev, 2 * blk, blk), BF16),
            sds((blk_dev, 2 * blk, blk), BF16),
        ),
        in_specs=[HBM()] * 2,
        scratch=[
            pltpu.VMEM((rows_here, ncol), F32), pltpu.VMEM((blk_dev, blk, blk), F32),
            pltpu.SemaphoreType.DMA((2 * blk_dev,)),
        ],
        micros=2.5,
    )(start_block, eigvectors)

    vec_first = [after(v, packed) for v in vec_first]
    vec_second = [pass_on(v, a) for v, a in zip(sends, vec_first)]
    mate_first = [mate(v[:per_cut * blk]) for v in vec_first] if halves == 2 else []
    pack_first = swap(packed)
    pack_second = pass_on(packed, after(pack_first, *mate_first))
    begun = (pack_first, *mate_first)

    def couple(coup_hbm, spun_ref, val, vec, cst, xh, xl, scale_ref, coup, sems):
        copies = [pltpu.make_async_copy(coup_hbm.at[i], coup.at[i], sems.at[i]) for i in range(blk_dev)]
        for copy in copies:
            copy.start()
        fields = []
        for i in range(blk_dev):
            b = DAMPING * spun_ref[i]
            re, im = inverse_scale(column_of(val[i:i + 1, :]))
            scale_ref[i, :, :ncol] = re
            scale_ref[i, :, ncol:] = im
            fields.append(apply_three(vec[i], jnp.concatenate([re * b, im * b], axis=1)))
        for i in range(blk_dev):
            put(xh, xl, i, fields[i])
        for i in range(blk_dev):
            copies[i].wait()
            for k in range(nnb):
                ch, cl = split(coup[i, k])
                cst[i, :blk, k * blk:(k + 1) * blk] = ch
                cst[i, blk:, k * blk:(k + 1) * blk] = cl

    def put(xh, xl, block, value):
        rows = pl.ds(pl.multiple_of(block * blk, blk), blk)
        h, l = split(value)
        xh[rows, :] = h
        xl[rows, :] = l

    field_shape = (sds((rows_here, wide), BF16), sds((rows_here, wide), BF16))
    cst, own_h, own_l, scale = call(
        couple,
        (sds((blk_dev, 2 * blk, nnb * blk), BF16),) + field_shape + (sds((blk_dev, blk, wide), F32),),
        in_specs=[HBM()] + [VMEM()] * 3,
        scratch=[pltpu.VMEM((blk_dev, nnb, blk, blk), F32), pltpu.SemaphoreType.DMA((blk_dev,))],
        micros=2.5,
    )(after(couplings, *begun), spun, eigvalues, vec_st)

    vec_second = [after(v, cst) for v in vec_second]
    mate_second = [mate(v[:per_cut * blk]) for v in vec_second] if halves == 2 else []

    def fill_first(inputs, xh, xl, offset):
        pack = inputs[0]
        vecs = inputs[1:]
        names, lefts, rights = [], [], []
        for h in range(halves):
            base = ((lax.axis_index("shift") + h) % halves) * per_half if halves > 1 else 0
            for c in range(cuts):
                for j in range(per_cut):
                    b = base + c * per_cut + j
                    row0 = pl.multiple_of((b // count) * blk, blk)
                    turned = spread(pack[pl.ds(row0, blk), :], b % count, width) * DAMPING
                    re, im = inverse_scale(column_of(vecs[0][pl.ds(per_cut * blk + b, 1), :]))
                    names.append(b)
                    lefts.append(jnp.concatenate(split(vecs[h * cuts + c][j * blk:(j + 1) * blk, :]), axis=0))
                    rights.append(jnp.concatenate([re * turned, im * turned], axis=1))
        fields = [apply_three(left, right) for left, right in zip(lefts, rights)]
        for b, field in zip(names, fields):
            put(xh, xl, b + offset, field)

    def first_partner(*refs):
        fill_first(refs[:-2], refs[-2], refs[-1], 0)

    partners = [pack_first] + vec_first + mate_first
    partner_h, partner_l = call(
        first_partner,
        field_shape,
        in_specs=[VMEM()] * len(partners),
        micros=1.5,
    )(*partners)

    def near_of(ref, slots, i):
        return jnp.concatenate(
            [ref[pl.ds(pl.multiple_of(slots[i, k] * blk, blk), blk), :] for k in range(nnb)], axis=0
        )

    def coupled(slots, c, xh, xl, i):
        return dot_three(c[i], near_of(xh, slots, i), near_of(xl, slots, i))

    def times(s, g):
        re, im = g[:, :ncol], g[:, ncol:]
        sre, sim = s[:, :ncol], s[:, ncol:]
        return jnp.concatenate([sre * re - sim * im, sre * im + sim * re], axis=1)

    def plus_real(g, b):
        return jnp.concatenate([g[:, :ncol] + b, g[:, ncol:]], axis=1)

    sizes = [blk_dev // CHUNKS] * CHUNKS if blk_dev % CHUNKS == 0 else [blk_dev]
    chunks = len(sizes)
    spots = [(c, j) for c in range(chunks) for j in range(sizes[c])]

    others = [pack_second] + vec_second + mate_second

    def second_iterate(*refs):
        slots, oh, ol, ph, pl_, c, vec, vec_t, spun_ref, scale_ref = refs[:10]
        inputs = refs[10:10 + len(others)]
        outs = refs[10 + len(others):10 + len(others) + chunks]
        hats, xh, xl = refs[10 + len(others) + chunks:]
        fill_first(inputs, xh, xl, 2 * blk_dev)
        xh[:rows_here, :] = oh[...]
        xl[:rows_here, :] = ol[...]
        xh[rows_here:2 * rows_here, :] = ph[...]
        xl[rows_here:2 * rows_here, :] = pl_[...]
        blocks = range(blk_dev)
        sums = [coupled(slots, c, xh, xl, i) for i in blocks]
        turned = [apply_three(vec_t[i], sums[i]) for i in blocks]
        for i in blocks:
            hats[i] = times(scale_ref[i], DAMPING * plus_real(turned[i], (1.0 + KEEP) * spun_ref[i]))
        result = [apply_three(vec[i], hats[i]) for i in blocks]
        for i in blocks:
            q, j = spots[i]
            outs[q][j] = result[i]

    field_scratch = [pltpu.VMEM((3 * rows_here, wide), BF16)] * 2
    *own, hats = call(
        second_iterate,
        [sds((size, blk, wide), F32) for size in sizes] + [sds((blk_dev, blk, wide), F32)],
        in_specs=[SMEM()] + [VMEM()] * (9 + len(others)),
        scratch=field_scratch,
        micros=6.0,
    )(slot, own_h, own_l, partner_h, partner_l, cst, vec_st, vec_ts, spun, scale, *others)

    two_first, two_second = halo(own)

    def third_iterate(*refs):
        slots = refs[0]
        fields = refs[1:1 + 3 * chunks]
        hats_ref, c, vec, vec_t, spun_ref, scale_ref, val = refs[1 + 3 * chunks:8 + 3 * chunks]
        packed_out, diag_out, xh, xl = refs[8 + 3 * chunks:]
        for side in range(3):
            for i, (q, j) in enumerate(spots):
                put(xh, xl, side * blk_dev + i, fields[side * chunks + q][j])
        weight_re = lane_table(real_parts / count, (1, ncol), width)
        weight_im = lane_table(imag_parts / count, (1, ncol), width)
        blocks = range(blk_dev)
        sums = [coupled(slots, c, xh, xl, i) for i in blocks]
        turned = [apply_three(vec_t[i], sums[i]) for i in blocks]
        ends = []
        for i in blocks:
            hat = KEEP * hats_ref[i] + times(scale_ref[i], DAMPING * plus_real(turned[i], spun_ref[i]))
            term = fold(weight_re * hat[:, :ncol] - weight_im * hat[:, ncol:], width)
            energy = column_of(val[i:i + 1, :])
            ends.append(jnp.concatenate([term, energy * term], axis=1))
        result = [apply_three(vec[i], ends[i]) for i in blocks]
        for i in blocks:
            diag_out[i] = result[i][:, ncol:]
            store_packed(packed_out, i, result[i][:, :ncol])

    filtered, diagonal = call(
        third_iterate,
        (sds((packs * blk, ncol), F32), sds((blk_dev, blk, ncol), F32)),
        in_specs=[SMEM()] + [VMEM()] * (7 + 3 * chunks),
        scratch=field_scratch,
        micros=6.0,
    )(slot, *own, *two_first, *two_second, hats, cst, vec_st, vec_ts, spun, scale, eigvalues)

    (filt_first,), (filt_second,) = halo([filtered])
    filt_all = gather_shift(filtered)

    def unpacked(refs, rows, g):
        lanes = lane_group((rows.stop - rows.start, ncol), width)
        out = jnp.zeros(lanes.shape, F32)
        mine_now = own_group()
        for k, ref in enumerate(refs):
            s = source(mine_now, k) if k else mine_now
            moved = pltpu.roll(ref[rows, :], ((s - g + count) % count) * width, 1)
            out = jnp.where(lanes == s, moved, out)
        return out

    def gram_of(*refs):
        pieces, full, gram = refs[:count], refs[count], refs[1 + count]
        for i in range(blk_dev):
            full[i * blk:(i + 1) * blk, :] = unpacked(pieces, block_rows(i), i % count)
        gram[...] = exact(full[...], full[...], ((0,), (0,)))

    full, gram = call(
        gram_of,
        (sds((rows_here, ncol), F32), sds((ncol, ncol), F32)),
        in_specs=[VMEM()] * count,
        micros=GRAM_MICROS,
    )(*filt_all)

    span = ncol // count

    def image_of(slots, own_f, first_f, second_f, full_ref, gram_ref, c, diag, packed_out, sums, xh, xl, image_ref):
        for f, field in enumerate((own_f, first_f, second_f)):
            for b in range(blk_dev):
                put(xh, xl, f * blk_dev + b, spread(field[block_rows(b), :], b % count, width))
        for i in range(blk_dev):
            image = diag[i] + coupled(slots, c, xh, xl, i)
            image_ref[i * blk:(i + 1) * blk, :] = image
            store_packed(packed_out, i, image)
        part = exact(full_ref[...], image_ref[...], ((0,), (0,)))
        piece = jnp.zeros((span, ncol), F32)
        for s in range(count):
            piece = piece + jnp.where(
                lane_group((span, ncol), width) == s, part[s * span:(s + 1) * span, :], 0.0
            )
        sums[:ncol, :] = gram_ref[...]
        sums[ncol:, :] = piece

    image, sums = call(
        image_of,
        (sds((packs * blk, ncol), F32), sds((ncol + span, ncol), F32)),
        in_specs=[SMEM()] + [VMEM()] * 7,
        scratch=[pltpu.VMEM((3 * rows_here, ncol), BF16)] * 2 + [pltpu.VMEM((rows_here, ncol), F32)],
        micros=3.8,
    )(slot, filtered, filt_first, filt_second, full, gram, cst, diagonal)

    image_all = gather_pairs(image)
    sums = sum_rows(sums)
    moment_all = gather_pairs(sums[ncol:])

    def factor_of(sums_ref, inverse):
        tiles = ncol // 8
        a = [sums_ref[t * 8:(t + 1) * 8, :] * (1.0 / total) for t in range(tiles)]
        lanes = lax.broadcasted_iota(jnp.int32, (8, ncol), 1)
        subs = lax.broadcasted_iota(jnp.int32, (8, ncol), 0)
        e = [jnp.where(lanes == subs + t * 8, 1.0, 0.0).astype(F32) for t in range(tiles)]
        for t in range(tiles):
            below = range(t, tiles)
            cols = [
                {u: jnp.broadcast_to(a[u][:, t * 8 + j:t * 8 + j + 1], (8, ncol)) for u in below} for j in range(8)
            ]
            rows = [a[t][j:j + 1, :] for j in range(8)]
            erows = [e[t][j:j + 1, :] for j in range(8)]
            factors = []
            for j in range(8):
                inv = 1.0 / cols[j][t][j:j + 1, :]
                m = {u: cols[j][u] * inv for u in below}
                m[t] = jnp.where(subs > j, m[t], 0.0)
                for q in range(j + 1, 8):
                    above = cols[q][t][j:j + 1, :]
                    for u in below:
                        cols[q][u] = cols[q][u] - m[u] * above
                    left = m[t][q:q + 1, :]
                    rows[q] = rows[q] - left * rows[j]
                    erows[q] = erows[q] - left * erows[j]
                factors.append(m)
            for u in below:
                for j in range(8):
                    a[u] = a[u] - factors[j][u] * rows[j]
                    e[u] = e[u] - factors[j][u] * erows[j]
        for t in range(tiles):
            pivot = jnp.sum(jnp.where(lanes == subs + t * 8, a[t], 0.0), axis=1, keepdims=True)
            inverse[t * 8:(t + 1) * 8, :] = e[t] * (1.0 / jnp.sqrt(pivot))

    inverse = call(
        factor_of, sds((ncol, ncol), F32), in_specs=[VMEM()], micros=5.5,
    )(sums)

    def finish(*refs):
        full_ref, pieces, moments, inv_ref = refs[0], refs[1:1 + count], refs[1 + count:1 + 2 * count], refs[1 + 2 * count]
        basis_ref, image_ref, projected_ref, raw = refs[2 + 2 * count:]
        inv = inv_ref[...]
        strips = [unpacked(moments, slice(0, span), g) for g in range(count)]
        m = jnp.concatenate(strips, axis=0) * (1.0 / total)
        for i in range(blk_dev):
            raw[i * blk:(i + 1) * blk, :] = unpacked(pieces, block_rows(i), i % count)
        half = exact(inv, m, ((1,), (0,)))
        basis_ref[...] = exact(full_ref[...], inv, ((1,), (1,)))
        image_ref[...] = exact(raw[...], inv, ((1,), (1,)))
        projected_ref[...] = exact(half, inv, ((1,), (1,)))

    return call(
        finish,
        (sds((rows_here, ncol), F32), sds((rows_here, ncol), F32), sds((ncol, ncol), F32)),
        in_specs=[VMEM()] * (2 + 2 * count),
        scratch=[pltpu.VMEM((rows_here, ncol), F32)],
        micros=3.0,
    )(full, *image_all, *moment_all, inverse)


def solution(mesh):
    in_specs = (
        P("rows", None),
        P("rows", None, None, None),
        P("rows", None, None),
        P("rows", None),
        P("rows", None),
    )
    out_specs = (P("rows", None), P("rows", None), P())
    return jax.shard_map(
        per_device, mesh=mesh, in_specs=in_specs, out_specs=out_specs, check_vma=False
    )
```

time: 362 us -> 119 us (0.33); the launches traced: 357 us -> 119 us
  waiting for transfers between devices: 201 us -> 33 us
  matrix products: 64.1 us -> 0 us
  other arithmetic: 35.8 us -> 0.78 us
  starting transfers between devices: 18.8 us -> 52.6 us
  Pallas kernels: 0 us -> 26 us
  local copies, waits for them, and re-layouts: 22.9 us -> 5.31 us
  between operations: 14.7 us -> 0.92 us
    psum x2 -> x0, waiting for transfers between devices: 108 us -> none  [the longest x1 71 us: per_device(): lax.psum((product(field.T, field), product(field.T, image)), 'rows')]
    dot_general x17 -> x0, matrix products: 61.4 us -> none  [the longest x3 43 us: coupled(): jnp.einsum('iknm,ikmc->inc', couplings, near_blocks, precision=lax.Precis...]
    ppermute x6 -> x26, waiting for transfers between devices: 92.6 us -> 33 us  [the longest x7 11.9 us: swap(): return lax.ppermute(value, 'rows', [(i, i ^ 1) for i in range(nrows)])]
    ppermute x6 -> x26, starting transfers between devices: 18.8 us -> 52.6 us  [the longest x7 29.9 us: pass_on(): return lax.ppermute(arrived, 'rows', pairs)]
    pallas_call x0 -> x9, Pallas kernels: none -> 26 us  [the longest x1 4.73 us: per_device(): call(second_iterate, [sds((size, blk, wide), F32) for size in sizes] + [s...]
    another operation x5 -> x0, other arithmetic: 23 us -> none  [the longest x3 12.6 us: per_device(): factor = jnp.linalg.cholesky(gram)]
    gather x3 -> x0, local copies, waits for them, and re-layouts: 15.1 us -> none  [operate_on(): near = blocks_all[local_index]]
    concatenate x3, other arithmetic: 7.64 us -> 0.73 us  [the longest x1 0.71 us: per_device(): sends[0] = jnp.concatenate([sends[0], eigvalues], axis=0)]
  transfers between devices with their start and end apart: 8 -> 26, of which waited for: 5 -> 16; matrix products, arithmetic and copies ran while one was open for 4% -> 0% of each run, Pallas kernels for 0% -> 9%
where the time goes in v2:
time: 119 us
  starting transfers between devices  52.6 us (44%)
  waiting for transfers between devices  33 us (28%)
  Pallas kernels  26 us (22%)
  local copies, waits for them, and re-layouts  5.31 us (4%)
    ppermute x7, starting transfers between devices, pass_on(): return lax.ppermute(arrived, 'rows', pairs)  29.9 us
    ppermute x7, waiting for transfers between devices, swap(): return lax.ppermute(value, 'rows', [(i, i ^ 1) for i in range(nrows)])  11.9 us
    ppermute x7, starting transfers between devices, swap(): return lax.ppermute(value, 'rows', [(i, i ^ 1) for i in range(nrows)])  10.3 us
    ppermute x7, waiting for transfers between devices, pass_on(): return lax.ppermute(arrived, 'rows', pairs)  8.97 us
    ppermute x3, waiting for transfers between devices, sum_rows(): lax.ppermute(value, 'rows', [(i, i ^ step) for i in range(nrows)])  8.93 us
    ppermute x3, starting transfers between devices, sum_rows(): lax.ppermute(value, 'rows', [(i, i ^ step) for i in range(nrows)])  7.69 us
    pallas_call x1, Pallas kernels, per_device(): call(second_iterate, [sds((size, blk, wide), F32) for size in sizes] + [s...  4.73 us
    unnamed x10, local copies, waits for them, and re-layouts  4.28 us
  transfers between devices with their start and end apart: 26, of which 16 were waited for; matrix products, arithmetic and copies ran while one was open for 0% of the time, Pallas kernels for 9%

profile of v2, /device:TPU:0, one launch (start us, length us, event | category | flops | bytes accessed | tf_op | source)
XLA Modules:
  0.0 118.6 jit_solution(7851589786822003232)
XLA Ops:
  2.3 3.0 %collective-permute-start.1 = (f32[520,128]{1,0:T(8,128)S(1)}, f32[520,128]{1,0:T(8,128)S(1)}, u32[]{:S(2)}, u32[]{:S(2)}) collective-permute-start(f32[520,128]{1,0:T(8,128)S(1)} %pad_maximum_fusion), channel_id=1, source_target_pairs={{0,1},{1,0},{2,3},{3,2},{4,5},{5,4},{6,7},{7,6},{8,9},{9,8},{10,11... | collective-permute-start | bytes 798728 | tf_op jit(solution)/shard_map/ppermute | solution.py:149
  7.5 2.4 %shard_map.76 = (f32[8,128,128]{2,1,0:T(8,128)S(1)}, f32[256,128]{1,0:T(8,128)S(1)}, bf16[8,256,128]{2,1,0:T(8,128)(2,1)S(1)}, bf16[8,256,128]{2,1,0:T(8,128)(2,1)S(1)}) custom-call(f32[1024,128]{1,0:T(8,128)S(1)} %copy-done.3, f32[8,128,128]{2,1,0:T(8,128)S(1)} %copy-done), custom_call_target="tpu_custom_call" | custom-call | flops 2750000128 | tf_op jit(solution)/shard_map/pallas_call | solution.py:238
  9.9 1.9 %collective-permute-done.1.refs_1_ = f32[520,128]{1,0:T(8,128)S(1)} collective-permute-done((f32[520,128]{1,0:T(8,128)S(1)}, f32[520,128]{1,0:T(8,128)S(1)}, u32[]{:S(2)}, u32[]{:S(2)}) %collective-permute-start.1) | collective-permute-done | bytes 266272 | tf_op jit(solution)/shard_map/ppermute | solution.py:149
  11.9 1.8 %collective-permute-start = (f32[256,128]{1,0:T(8,128)S(1)}, f32[256,128]{1,0:T(8,128)S(1)}, u32[]{:S(2)}, u32[]{:S(2)}) collective-permute-start(f32[256,128]{1,0:T(8,128)S(1)} %get-tuple-element.28), channel_id=1, source_target_pairs={{0,1},{1,0},{2,3},{3,2},{4,5},{5,4},{6,7},{7,6},{8,9},{9,8},{10,11... | collective-permute-start | bytes 393224 | tf_op jit(solution)/shard_map/ppermute | solution.py:149
  13.7 3.5 %collective-permute-start.4 = (f32[520,128]{1,0:T(8,128)S(1)}, f32[520,128]{1,0:T(8,128)S(1)}, u32[]{:S(2)}, u32[]{:S(2)}) collective-permute-start(f32[520,128]{1,0:T(8,128)S(1)} %collective-permute-done.1.refs_1_), channel_id=1, source_target_pairs={{0,2},{2,4},{4,6},{3,1},{5,3},{7,5},{8,10},{10,12},{12,14},{11,9},... | collective-permute-start | bytes 798728 | tf_op jit(solution)/shard_map/ppermute | solution.py:155
  17.8 2.2 %copy-done.2 = f32[8,8,128,128]{3,2,1,0:T(8,128)S(1)} copy-done((f32[8,8,128,128]{3,2,1,0:T(8,128)S(1)}, f32[8,8,128,128]{3,2,1,0:T(8,128)}, u32[]{:S(2)}) %copy-start.2) | copy-done | bytes 4194328
  20.0 2.1 %shard_map.77 = (bf16[8,256,1024]{2,1,0:T(8,128)(2,1)S(1)}, bf16[1024,256]{1,0:T(8,128)(2,1)S(1)}, bf16[1024,256]{1,0:T(8,128)(2,1)S(1)}, f32[8,128,256]{2,1,0:T(8,128)S(1)}) custom-call(f32[8,8,128,128]{3,2,1,0:T(8,128)S(1)} %copy-done.2, f32[8,128,128]{2,1,0:T(8,128)S(1)} %get-tuple-element.31.spun_ref.refs_8_.refs_17_, f32[8,128]{1,0:T(8,128)S(1)} %copy-done.1, ...), custom_call_target="tpu_custom_call" | custom-call | flops 2750000128 | tf_op jit(solution)/shard_map/pallas_call | solution.py:288
  23.2 4.4 %collective-permute-start.3 = (f32[256,128]{1,0:T(8,128)S(1)}, f32[256,128]{1,0:T(8,128)S(1)}, u32[]{:S(2)}, u32[]{:S(2)}) collective-permute-start(f32[256,128]{1,0:T(8,128)S(1)} %collective-permute-done.refs_0_), channel_id=1, source_target_pairs={{0,2},{2,4},{4,6},{3,1},{5,3},{7,5},{8,10},{10,12},{12,14},{11,9},... | collective-permute-start | bytes 393224 | tf_op jit(solution)/shard_map/ppermute | solution.py:155
  27.6 1.3 %shard_map.78 = (bf16[1024,256]{1,0:T(8,128)(2,1)S(1)}, bf16[1024,256]{1,0:T(8,128)(2,1)S(1)}) custom-call(f32[256,128]{1,0:T(8,128)S(1)} %collective-permute-done.refs_0_, f32[520,128]{1,0:T(8,128)S(1)} %collective-permute-done.1.refs_1_, f32[512,128]{1,0:T(8,128)S(1)} %collective-permute-done.2.refs_2_), custom_call_target="tpu_custom_call" | custom-call | flops 1650000000 | tf_op jit(solution)/shard_map/pallas_call | solution.py:322
  29.0 2.0 %collective-permute-done.3.refs_10_ = f32[256,128]{1,0:T(8,128)S(1)} collective-permute-done((f32[256,128]{1,0:T(8,128)S(1)}, f32[256,128]{1,0:T(8,128)S(1)}, u32[]{:S(2)}, u32[]{:S(2)}) %collective-permute-start.3) | collective-permute-done | bytes 131104 | tf_op jit(solution)/shard_map/ppermute | solution.py:155
  31.0 4.7 %shard_map.79 = (f32[2,128,256]{2,1,0:T(8,128)S(1)}, f32[2,128,256]{2,1,0:T(8,128)S(1)}, f32[2,128,256]{2,1,0:T(8,128)S(1)}, f32[2,128,256]{2,1,0:T(8,128)S(1)}, f32[8,128,256]{2,1,0:T(8,128)S(1)}) custom-call(s32[8,8]{1,0:T(8,128)S(1)} %fusion.refs_0_.slots, bf16[1024,256]{1,0:T(8,128)(2,1)S(1)} %get-tuple-element.33.refs_1_, ...), custom_call_target="tpu_custom_call" | custom-call | flops 6600000000 | tf_op jit(solution)/shard_map/pallas_call | solution.py:372
  35.8 1.3 %collective-permute-start.6 = (f32[2,128,256]{2,1,0:T(8,128)S(1)}, f32[2,128,256]{2,1,0:T(8,128)S(1)}, u32[]{:S(2)}, u32[]{:S(2)}) collective-permute-start(f32[2,128,256]{2,1,0:T(8,128)S(1)} %get-tuple-element.42.refs_1_), channel_id=1, source_target_pairs={{0,1},{1,0},{2,3},{3,2},{4,5},{5,4},{6,7},{7,6},{8,9},{9,8},{10,11... | collective-permute-start | bytes 786440 | tf_op jit(solution)/shard_map/ppermute | solution.py:149
  39.9 5.2 %collective-permute-done.6.refs_5_ = f32[2,128,256]{2,1,0:T(8,128)S(1)} collective-permute-done((f32[2,128,256]{2,1,0:T(8,128)S(1)}, f32[2,128,256]{2,1,0:T(8,128)S(1)}, u32[]{:S(2)}, u32[]{:S(2)}) %collective-permute-start.6) | collective-permute-done | bytes 262176 | tf_op jit(solution)/shard_map/ppermute | solution.py:149
  45.0 4.4 %collective-permute-start.10 = (f32[2,128,256]{2,1,0:T(8,128)S(1)}, f32[2,128,256]{2,1,0:T(8,128)S(1)}, u32[]{:S(2)}, u32[]{:S(2)}) collective-permute-start(f32[2,128,256]{2,1,0:T(8,128)S(1)} %collective-permute-done.6.refs_5_), channel_id=1, source_target_pairs={{0,2},{2,4},{4,6},{3,1},{5,3},{7,5},{8,10},{10,12},{12,14},{11,9},... | collective-permute-start | bytes 786440 | tf_op jit(solution)/shard_map/ppermute | solution.py:155
  50.7 4.4 %collective-permute-start.11 = (f32[2,128,256]{2,1,0:T(8,128)S(1)}, f32[2,128,256]{2,1,0:T(8,128)S(1)}, u32[]{:S(2)}, u32[]{:S(2)}) collective-permute-start(f32[2,128,256]{2,1,0:T(8,128)S(1)} %collective-permute-done.7.refs_6_), channel_id=1, source_target_pairs={{0,2},{2,4},{4,6},{3,1},{5,3},{7,5},{8,10},{10,12},{12,14},{11,9},... | collective-permute-start | bytes 786440 | tf_op jit(solution)/shard_map/ppermute | solution.py:155
  56.3 4.4 %collective-permute-start.12 = (f32[2,128,256]{2,1,0:T(8,128)S(1)}, f32[2,128,256]{2,1,0:T(8,128)S(1)}, u32[]{:S(2)}, u32[]{:S(2)}) collective-permute-start(f32[2,128,256]{2,1,0:T(8,128)S(1)} %collective-permute-done.8.refs_7_), channel_id=1, source_target_pairs={{0,2},{2,4},{4,6},{3,1},{5,3},{7,5},{8,10},{10,12},{12,14},{11,9},... | collective-permute-start | bytes 786440 | tf_op jit(solution)/shard_map/ppermute | solution.py:155
  60.7 4.3 %collective-permute-start.13 = (f32[2,128,256]{2,1,0:T(8,128)S(1)}, f32[2,128,256]{2,1,0:T(8,128)S(1)}, u32[]{:S(2)}, u32[]{:S(2)}) collective-permute-start(f32[2,128,256]{2,1,0:T(8,128)S(1)} %collective-permute-done.9.refs_8_), channel_id=1, source_target_pairs={{0,2},{2,4},{4,6},{3,1},{5,3},{7,5},{8,10},{10,12},{12,14},{11,9},... | collective-permute-start | bytes 786440 | tf_op jit(solution)/shard_map/ppermute | solution.py:155
  65.1 5.0 %collective-permute-done.13.refs_12_ = f32[2,128,256]{2,1,0:T(8,128)S(1)} collective-permute-done((f32[2,128,256]{2,1,0:T(8,128)S(1)}, f32[2,128,256]{2,1,0:T(8,128)S(1)}, u32[]{:S(2)}, u32[]{:S(2)}) %collective-permute-start.13) | collective-permute-done | bytes 262176 | tf_op jit(solution)/shard_map/ppermute | solution.py:155
  70.2 4.1 %shard_map.80 = (f32[256,128]{1,0:T(8,128)S(1)}, f32[8,128,128]{2,1,0:T(8,128)S(1)}) custom-call(s32[8,8]{1,0:T(8,128)S(1)} %fusion.refs_0_.slots, f32[2,128,256]{2,1,0:T(8,128)S(1)} %get-tuple-element.42.refs_1_, f32[2,128,256]{2,1,0:T(8,128)S(1)} %get-tuple-element.43.refs_2_, f32[2,128,256]{2,1,0:T(8,128)S(1)} %get-tuple-element.44.refs_3_, ...), custom_call_target="tpu_custom_call" | custom-call | flops 6600000000 | tf_op jit(solution)/shard_map/pallas_call | solution.py:406
  75.6 1.7 %collective-permute-start.15 = (f32[256,128]{1,0:T(8,128)S(1)}, f32[256,128]{1,0:T(8,128)S(1)}, u32[]{:S(2)}, u32[]{:S(2)}) collective-permute-start(f32[256,128]{1,0:T(8,128)S(1)} %get-tuple-element.47.refs_0_.own_f), channel_id=1, source_target_pairs={{16,0},{24,8},{0,16},{8,24},{17,1},{25,9},{1,17},{9,25},{18,2},{26... | collective-permute-start | bytes 393224 | tf_op jit(solution)/shard_map/ppermute | solution.py:183
  77.4 1.8 %collective-permute-done.17.first_f = f32[256,128]{1,0:T(8,128)S(1)} collective-permute-done((f32[256,128]{1,0:T(8,128)S(1)}, f32[256,128]{1,0:T(8,128)S(1)}, u32[]{:S(2)}, u32[]{:S(2)}) %collective-permute-start.17) | collective-permute-done | bytes 131104 | tf_op jit(solution)/shard_map/ppermute | solution.py:149
  79.3 4.6 %collective-permute-start.18 = (f32[256,128]{1,0:T(8,128)S(1)}, f32[256,128]{1,0:T(8,128)S(1)}, u32[]{:S(2)}, u32[]{:S(2)}) collective-permute-start(f32[256,128]{1,0:T(8,128)S(1)} %collective-permute-done.17.first_f), channel_id=1, source_target_pairs={{0,2},{2,4},{4,6},{3,1},{5,3},{7,5},{8,10},{10,12},{12,14},{11,9},... | collective-permute-start | bytes 393224 | tf_op jit(solution)/shard_map/ppermute | solution.py:155
  86.2 3.7 %shard_map.82 = (f32[256,128]{1,0:T(8,128)S(1)}, f32[160,128]{1,0:T(8,128)S(1)}) custom-call(s32[8,8]{1,0:T(8,128)S(1)} %fusion.refs_0_.slots, f32[256,128]{1,0:T(8,128)S(1)} %get-tuple-element.47.refs_0_.own_f, f32[256,128]{1,0:T(8,128)S(1)} %collective-permute-done.17.first_f, f32[256,128]{1,0:T(8,128)S(1)} %collective-permute-done.18.second_f, ...), custom_call_target="tpu_custom_call" | custom-call | flops 4180000000 | tf_op jit(solution)/shard_map/pallas_call | solution.py:459
  91.2 3.2 %collective-permute-done.21 = f32[160,128]{1,0:T(8,128)S(1)} collective-permute-done((f32[160,128]{1,0:T(8,128)S(1)}, f32[160,128]{1,0:T(8,128)S(1)}, u32[]{:S(2)}, u32[]{:S(2)}) %collective-permute-start.21) | collective-permute-done | bytes 81952 | tf_op jit(solution)/shard_map/ppermute | solution.py:194
  94.4 2.5 %collective-permute-start.22 = (f32[160,128]{1,0:T(8,128)S(1)}, f32[160,128]{1,0:T(8,128)S(1)}, u32[]{:S(2)}, u32[]{:S(2)}) collective-permute-start(f32[160,128]{1,0:T(8,128)S(1)} %add.35), channel_id=1, source_target_pairs={{0,2},{1,3},{2,0},{3,1},{4,6},{5,7},{6,4},{7,5},{8,10},{9,11},{10,... | collective-permute-start | bytes 245768 | tf_op jit(solution)/shard_map/ppermute | solution.py:194
  97.0 2.4 %collective-permute-done.22 = f32[160,128]{1,0:T(8,128)S(1)} collective-permute-done((f32[160,128]{1,0:T(8,128)S(1)}, f32[160,128]{1,0:T(8,128)S(1)}, u32[]{:S(2)}, u32[]{:S(2)}) %collective-permute-start.22) | collective-permute-done | bytes 81952 | tf_op jit(solution)/shard_map/ppermute | solution.py:194
  99.4 3.9 %collective-permute-start.23 = (f32[160,128]{1,0:T(8,128)S(1)}, f32[160,128]{1,0:T(8,128)S(1)}, u32[]{:S(2)}, u32[]{:S(2)}) collective-permute-start(f32[160,128]{1,0:T(8,128)S(1)} %add.36), channel_id=1, source_target_pairs={{0,4},{1,5},{2,6},{3,7},{4,0},{5,1},{6,2},{7,3},{8,12},{9,13},{10,... | collective-permute-start | bytes 245768 | tf_op jit(solution)/shard_map/ppermute | solution.py:194
  103.3 3.3 %collective-permute-done.23 = f32[160,128]{1,0:T(8,128)S(1)} collective-permute-done((f32[160,128]{1,0:T(8,128)S(1)}, f32[160,128]{1,0:T(8,128)S(1)}, u32[]{:S(2)}, u32[]{:S(2)}) %collective-permute-start.23) | collective-permute-done | bytes 81952 | tf_op jit(solution)/shard_map/ppermute | solution.py:194
  106.7 1.6 %collective-permute-start.20 = (f32[512,128]{1,0:T(8,128)S(1)}, f32[512,128]{1,0:T(8,128)S(1)}, u32[]{:S(2)}, u32[]{:S(2)}) collective-permute-start(f32[512,128]{1,0:T(8,128)S(1)} %pad_maximum_fusion.1), channel_id=1, source_target_pairs={{0,16},{8,24},{16,0},{24,8},{1,17},{9,25},{17,1},{25,9},{2,18},{10... | collective-permute-start | bytes 786440 | tf_op jit(solution)/shard_map/ppermute | solution.py:176
  109.3 4.0 %shard_map.83.refs_9_ = f32[128,128]{1,0:T(8,128)S(1)} custom-call(f32[160,128]{1,0:T(8,128)S(1)} %add.37.sums_ref), custom_call_target="tpu_custom_call" | custom-call | flops 6049999872 | tf_op jit(solution)/shard_map/pallas_call | solution.py:505
  113.4 2.8 %collective-permute-done.25 = f32[64,128]{1,0:T(8,128)S(1)} collective-permute-done((f32[64,128]{1,0:T(8,128)S(1)}, f32[64,128]{1,0:T(8,128)S(1)}, u32[]{:S(2)}, u32[]{:S(2)}) %collective-permute-start.25) | collective-permute-done | bytes 32800 | tf_op jit(solution)/shard_map/ppermute | solution.py:176
  116.2 2.4 %shard_map.84 = (f32[1024,128]{1,0:T(8,128)}, f32[1024,128]{1,0:T(8,128)}, f32[128,128]{1,0:T(8,128)}) custom-call(f32[1024,128]{1,0:T(8,128)S(1)} %get-tuple-element.48.full_ref.refs_0_, f32[256,128]{1,0:T(8,128)S(1)} %get-tuple-element.51.refs_1_, f32[256,128]{1,0:T(8,128)S(1)} %collective-permute-done.19.refs_2_, ...), custom_call_target="tpu_custom_call" | custom-call | flops 3300000000 | tf_op jit(solution)/shard_map/pallas_call | solution.py:522
  (52 shorter events, 17.2 us)
Async XLA Ops:
  2.3 9.4 %collective-permute-start.1 = (f32[520,128]{1,0:T(8,128)S(1)}, f32[520,128]{1,0:T(8,128)S(1)}, u32[]{:S(2)}, u32[]{:S(2)}) collective-permute-start(f32[520,128]{1,0:T(8,128)S(1)} %pad_maximum_fusion), channel_id=1, source_target_pairs={{0,1},{1,0},{2,3},{3,2},{4,5},{5,4},{6,7},{7,6},{8,9},{9,8},{10,11... | collective-permute-start | bytes 798728 | tf_op jit(solution)/shard_map/ppermute | solution.py:149
  5.4 1.0 copy-start
  6.4 1.0 copy-start.3
  7.4 10.3 %copy-start.1 = (f32[8,128]{1,0:T(8,128)S(1)}, f32[8,128]{1,0:T(8,128)}, u32[]{:S(2)}) copy-start(f32[8,128]{1,0:T(8,128)} %refs_19_.1) | copy-start | bytes 12292
  11.8 6.0 %collective-permute-start.2 = (f32[512,128]{1,0:T(8,128)S(1)}, f32[512,128]{1,0:T(8,128)S(1)}, u32[]{:S(2)}, u32[]{:S(2)}) collective-permute-start(f32[512,128]{1,0:T(8,128)S(1)} %slice.21), channel_id=1, source_target_pairs={{0,8},{8,0},{16,24},{24,16},{1,9},{9,1},{17,25},{25,17},{2,10},{10... | collective-permute-start | bytes 786440 | tf_op jit(solution)/shard_map/ppermute | solution.py:167
  11.9 5.9 %collective-permute-start = (f32[256,128]{1,0:T(8,128)S(1)}, f32[256,128]{1,0:T(8,128)S(1)}, u32[]{:S(2)}, u32[]{:S(2)}) collective-permute-start(f32[256,128]{1,0:T(8,128)S(1)} %get-tuple-element.28), channel_id=1, source_target_pairs={{0,1},{1,0},{2,3},{3,2},{4,5},{5,4},{6,7},{7,6},{8,9},{9,8},{10,11... | collective-permute-start | bytes 393224 | tf_op jit(solution)/shard_map/ppermute | solution.py:149
  13.7 9.4 %collective-permute-start.4 = (f32[520,128]{1,0:T(8,128)S(1)}, f32[520,128]{1,0:T(8,128)S(1)}, u32[]{:S(2)}, u32[]{:S(2)}) collective-permute-start(f32[520,128]{1,0:T(8,128)S(1)} %collective-permute-done.1.refs_1_), channel_id=1, source_target_pairs={{0,2},{2,4},{4,6},{3,1},{5,3},{7,5},{8,10},{10,12},{12,14},{11,9},... | collective-permute-start | bytes 798728 | tf_op jit(solution)/shard_map/ppermute | solution.py:155
  17.8 2.2 %copy-start.2 = (f32[8,8,128,128]{3,2,1,0:T(8,128)S(1)}, f32[8,8,128,128]{3,2,1,0:T(8,128)}, u32[]{:S(2)}) copy-start(f32[8,8,128,128]{3,2,1,0:T(8,128)} %coup_hbm) | copy-start | bytes 12582916
  20.0 3.2 %copy-start.4 = (s32[8,8]{1,0:T(8,128)S(1)}, s32[8,8]{1,0:T(8,128)}, u32[]{:S(2)}) copy-start(s32[8,8]{1,0:T(8,128)} %param.5) | copy-start | bytes 772
  23.1 7.9 %collective-permute-start.5 = (f32[512,128]{1,0:T(8,128)S(1)}, f32[512,128]{1,0:T(8,128)S(1)}, u32[]{:S(2)}, u32[]{:S(2)}) collective-permute-start(f32[512,128]{1,0:T(8,128)S(1)} %slice.22), channel_id=1, source_target_pairs={{0,8},{8,0},{16,24},{24,16},{1,9},{9,1},{17,25},{25,17},{2,10},{10... | collective-permute-start | bytes 786440 | tf_op jit(solution)/shard_map/ppermute | solution.py:167
  23.2 7.8 %collective-permute-start.3 = (f32[256,128]{1,0:T(8,128)S(1)}, f32[256,128]{1,0:T(8,128)S(1)}, u32[]{:S(2)}, u32[]{:S(2)}) collective-permute-start(f32[256,128]{1,0:T(8,128)S(1)} %collective-permute-done.refs_0_), channel_id=1, source_target_pairs={{0,2},{2,4},{4,6},{3,1},{5,3},{7,5},{8,10},{10,12},{12,14},{11,9},... | collective-permute-start | bytes 393224 | tf_op jit(solution)/shard_map/ppermute | solution.py:155
  35.8 9.3 %collective-permute-start.6 = (f32[2,128,256]{2,1,0:T(8,128)S(1)}, f32[2,128,256]{2,1,0:T(8,128)S(1)}, u32[]{:S(2)}, u32[]{:S(2)}) collective-permute-start(f32[2,128,256]{2,1,0:T(8,128)S(1)} %get-tuple-element.42.refs_1_), channel_id=1, source_target_pairs={{0,1},{1,0},{2,3},{3,2},{4,5},{5,4},{6,7},{7,6},{8,9},{9,8},{10,11... | collective-permute-start | bytes 786440 | tf_op jit(solution)/shard_map/ppermute | solution.py:149
  37.1 13.6 %collective-permute-start.7 = (f32[2,128,256]{2,1,0:T(8,128)S(1)}, f32[2,128,256]{2,1,0:T(8,128)S(1)}, u32[]{:S(2)}, u32[]{:S(2)}) collective-permute-start(f32[2,128,256]{2,1,0:T(8,128)S(1)} %get-tuple-element.43.refs_2_), channel_id=1, source_target_pairs={{0,1},{1,0},{2,3},{3,2},{4,5},{5,4},{6,7},{7,6},{8,9},{9,8},{10,11... | collective-permute-start | bytes 786440 | tf_op jit(solution)/shard_map/ppermute | solution.py:149
  37.9 18.4 %collective-permute-start.8 = (f32[2,128,256]{2,1,0:T(8,128)S(1)}, f32[2,128,256]{2,1,0:T(8,128)S(1)}, u32[]{:S(2)}, u32[]{:S(2)}) collective-permute-start(f32[2,128,256]{2,1,0:T(8,128)S(1)} %get-tuple-element.44.refs_3_), channel_id=1, source_target_pairs={{0,1},{1,0},{2,3},{3,2},{4,5},{5,4},{6,7},{7,6},{8,9},{9,8},{10,11... | collective-permute-start | bytes 786440 | tf_op jit(solution)/shard_map/ppermute | solution.py:149
  39.1 21.6 %collective-permute-start.9 = (f32[2,128,256]{2,1,0:T(8,128)S(1)}, f32[2,128,256]{2,1,0:T(8,128)S(1)}, u32[]{:S(2)}, u32[]{:S(2)}) collective-permute-start(f32[2,128,256]{2,1,0:T(8,128)S(1)} %get-tuple-element.45.refs_4_), channel_id=1, source_target_pairs={{0,1},{1,0},{2,3},{3,2},{4,5},{5,4},{6,7},{7,6},{8,9},{9,8},{10,11... | collective-permute-start | bytes 786440 | tf_op jit(solution)/shard_map/ppermute | solution.py:149
  45.0 20.0 %collective-permute-start.10 = (f32[2,128,256]{2,1,0:T(8,128)S(1)}, f32[2,128,256]{2,1,0:T(8,128)S(1)}, u32[]{:S(2)}, u32[]{:S(2)}) collective-permute-start(f32[2,128,256]{2,1,0:T(8,128)S(1)} %collective-permute-done.6.refs_5_), channel_id=1, source_target_pairs={{0,2},{2,4},{4,6},{3,1},{5,3},{7,5},{8,10},{10,12},{12,14},{11,9},... | collective-permute-start | bytes 786440 | tf_op jit(solution)/shard_map/ppermute | solution.py:155
  50.7 14.3 %collective-permute-start.11 = (f32[2,128,256]{2,1,0:T(8,128)S(1)}, f32[2,128,256]{2,1,0:T(8,128)S(1)}, u32[]{:S(2)}, u32[]{:S(2)}) collective-permute-start(f32[2,128,256]{2,1,0:T(8,128)S(1)} %collective-permute-done.7.refs_6_), channel_id=1, source_target_pairs={{0,2},{2,4},{4,6},{3,1},{5,3},{7,5},{8,10},{10,12},{12,14},{11,9},... | collective-permute-start | bytes 786440 | tf_op jit(solution)/shard_map/ppermute | solution.py:155
  56.3 8.9 %collective-permute-start.12 = (f32[2,128,256]{2,1,0:T(8,128)S(1)}, f32[2,128,256]{2,1,0:T(8,128)S(1)}, u32[]{:S(2)}, u32[]{:S(2)}) collective-permute-start(f32[2,128,256]{2,1,0:T(8,128)S(1)} %collective-permute-done.8.refs_7_), channel_id=1, source_target_pairs={{0,2},{2,4},{4,6},{3,1},{5,3},{7,5},{8,10},{10,12},{12,14},{11,9},... | collective-permute-start | bytes 786440 | tf_op jit(solution)/shard_map/ppermute | solution.py:155
  60.7 9.5 %collective-permute-start.13 = (f32[2,128,256]{2,1,0:T(8,128)S(1)}, f32[2,128,256]{2,1,0:T(8,128)S(1)}, u32[]{:S(2)}, u32[]{:S(2)}) collective-permute-start(f32[2,128,256]{2,1,0:T(8,128)S(1)} %collective-permute-done.9.refs_8_), channel_id=1, source_target_pairs={{0,2},{2,4},{4,6},{3,1},{5,3},{7,5},{8,10},{10,12},{12,14},{11,9},... | collective-permute-start | bytes 786440 | tf_op jit(solution)/shard_map/ppermute | solution.py:155
  74.2 5.0 %collective-permute-start.17 = (f32[256,128]{1,0:T(8,128)S(1)}, f32[256,128]{1,0:T(8,128)S(1)}, u32[]{:S(2)}, u32[]{:S(2)}) collective-permute-start(f32[256,128]{1,0:T(8,128)S(1)} %get-tuple-element.47.refs_0_.own_f), channel_id=1, source_target_pairs={{0,1},{1,0},{2,3},{3,2},{4,5},{5,4},{6,7},{7,6},{8,9},{9,8},{10,11... | collective-permute-start | bytes 393224 | tf_op jit(solution)/shard_map/ppermute | solution.py:149
  75.6 8.3 %collective-permute-start.16 = (f32[256,128]{1,0:T(8,128)S(1)}, f32[256,128]{1,0:T(8,128)S(1)}, u32[]{:S(2)}, u32[]{:S(2)}) collective-permute-start(f32[256,128]{1,0:T(8,128)S(1)} %get-tuple-element.47.refs_0_.own_f), channel_id=1, source_target_pairs={{24,0},{16,8},{8,16},{0,24},{25,1},{17,9},{9,17},{1,25},{26,2},{18... | collective-permute-start | bytes 393224 | tf_op jit(solution)/shard_map/ppermute | solution.py:183
  75.6 8.6 %collective-permute-start.15 = (f32[256,128]{1,0:T(8,128)S(1)}, f32[256,128]{1,0:T(8,128)S(1)}, u32[]{:S(2)}, u32[]{:S(2)}) collective-permute-start(f32[256,128]{1,0:T(8,128)S(1)} %get-tuple-element.47.refs_0_.own_f), channel_id=1, source_target_pairs={{16,0},{24,8},{0,16},{8,24},{17,1},{25,9},{1,17},{9,25},{18,2},{26... | collective-permute-start | bytes 393224 | tf_op jit(solution)/shard_map/ppermute | solution.py:183
  77.2 6.9 %collective-permute-start.14 = (f32[256,128]{1,0:T(8,128)S(1)}, f32[256,128]{1,0:T(8,128)S(1)}, u32[]{:S(2)}, u32[]{:S(2)}) collective-permute-start(f32[256,128]{1,0:T(8,128)S(1)} %get-tuple-element.47.refs_0_.own_f), channel_id=1, source_target_pairs={{8,0},{0,8},{24,16},{16,24},{9,1},{1,9},{25,17},{17,25},{10,2},{2,... | collective-permute-start | bytes 393224 | tf_op jit(solution)/shard_map/ppermute | solution.py:183
  79.3 6.9 %collective-permute-start.18 = (f32[256,128]{1,0:T(8,128)S(1)}, f32[256,128]{1,0:T(8,128)S(1)}, u32[]{:S(2)}, u32[]{:S(2)}) collective-permute-start(f32[256,128]{1,0:T(8,128)S(1)} %collective-permute-done.17.first_f), channel_id=1, source_target_pairs={{0,2},{2,4},{4,6},{3,1},{5,3},{7,5},{8,10},{10,12},{12,14},{11,9},... | collective-permute-start | bytes 393224 | tf_op jit(solution)/shard_map/ppermute | solution.py:155
  89.9 4.5 %collective-permute-start.21 = (f32[160,128]{1,0:T(8,128)S(1)}, f32[160,128]{1,0:T(8,128)S(1)}, u32[]{:S(2)}, u32[]{:S(2)}) collective-permute-start(f32[160,128]{1,0:T(8,128)S(1)} %get-tuple-element.52), channel_id=1, source_target_pairs={{0,1},{1,0},{2,3},{3,2},{4,5},{5,4},{6,7},{7,6},{8,9},{9,8},{10,11... | collective-permute-start | bytes 245768 | tf_op jit(solution)/shard_map/ppermute | solution.py:194
  94.4 4.9 %collective-permute-start.22 = (f32[160,128]{1,0:T(8,128)S(1)}, f32[160,128]{1,0:T(8,128)S(1)}, u32[]{:S(2)}, u32[]{:S(2)}) collective-permute-start(f32[160,128]{1,0:T(8,128)S(1)} %add.35), channel_id=1, source_target_pairs={{0,2},{1,3},{2,0},{3,1},{4,6},{5,7},{6,4},{7,5},{8,10},{9,11},{10,... | collective-permute-start | bytes 245768 | tf_op jit(solution)/shard_map/ppermute | solution.py:194
  97.0 9.7 %collective-permute-start.19 = (f32[256,128]{1,0:T(8,128)S(1)}, f32[256,128]{1,0:T(8,128)S(1)}, u32[]{:S(2)}, u32[]{:S(2)}) collective-permute-start(f32[256,128]{1,0:T(8,128)S(1)} %get-tuple-element.51.refs_1_), channel_id=1, source_target_pairs={{0,8},{8,0},{16,24},{24,16},{1,9},{9,1},{17,25},{25,17},{2,10},{10... | collective-permute-start | bytes 393224 | tf_op jit(solution)/shard_map/ppermute | solution.py:176
  99.4 7.2 %collective-permute-start.23 = (f32[160,128]{1,0:T(8,128)S(1)}, f32[160,128]{1,0:T(8,128)S(1)}, u32[]{:S(2)}, u32[]{:S(2)}) collective-permute-start(f32[160,128]{1,0:T(8,128)S(1)} %add.36), channel_id=1, source_target_pairs={{0,4},{1,5},{2,6},{3,7},{4,0},{5,1},{6,2},{7,3},{8,12},{9,13},{10,... | collective-permute-start | bytes 245768 | tf_op jit(solution)/shard_map/ppermute | solution.py:194
  106.6 1.7 %collective-permute-start.24 = (f32[32,128]{1,0:T(8,128)S(1)}, f32[32,128]{1,0:T(8,128)S(1)}, u32[]{:S(2)}, u32[]{:S(2)}) collective-permute-start(f32[32,128]{1,0:T(8,128)S(1)} %slice.30.refs_5_), channel_id=1, source_target_pairs={{0,8},{8,0},{16,24},{24,16},{1,9},{9,1},{17,25},{25,17},{2,10},{10... | collective-permute-start | bytes 49160 | tf_op jit(solution)/shard_map/ppermute | solution.py:176
  106.7 9.5 %collective-permute-start.20 = (f32[512,128]{1,0:T(8,128)S(1)}, f32[512,128]{1,0:T(8,128)S(1)}, u32[]{:S(2)}, u32[]{:S(2)}) collective-permute-start(f32[512,128]{1,0:T(8,128)S(1)} %pad_maximum_fusion.1), channel_id=1, source_target_pairs={{0,16},{8,24},{16,0},{24,8},{1,17},{9,25},{17,1},{25,9},{2,18},{10... | collective-permute-start | bytes 786440 | tf_op jit(solution)/shard_map/ppermute | solution.py:176
  108.3 7.9 %collective-permute-start.25 = (f32[64,128]{1,0:T(8,128)S(1)}, f32[64,128]{1,0:T(8,128)S(1)}, u32[]{:S(2)}, u32[]{:S(2)}) collective-permute-start(f32[64,128]{1,0:T(8,128)S(1)} %pad_maximum_fusion.2), channel_id=1, source_target_pairs={{0,16},{8,24},{16,0},{24,8},{1,17},{9,25},{17,1},{25,9},{2,18},{10... | collective-permute-start | bytes 98312 | tf_op jit(solution)/shard_map/ppermute | solution.py:176

commit v3 on v2

--- a/solution.py
+++ b/solution.py
@@ -13,6 +13,7 @@
 CHUNKS = 4
 KEEP = 1.0 - DAMPING
 VMEM_LIMIT = 24 * 1024 * 1024
+FIRST_LIMIT = 52 * 1024 * 1024
 FLOPS_PER_MICRO = 1.1e9
 GRAM_MICROS = 6.0
 F32 = jnp.float32
@@ -85,7 +86,7 @@
     return out
 
 
-def call(kernel, out_shape, in_specs, scratch=(), micros=1.0):
+def call(kernel, out_shape, in_specs, scratch=(), micros=1.0, limit=VMEM_LIMIT):
     single = not isinstance(out_shape, (tuple, list))
     return pl.pallas_call(
         kernel,
@@ -93,7 +94,7 @@
         in_specs=in_specs,
         out_specs=VMEM() if single else [VMEM()] * len(out_shape),
         scratch_shapes=list(scratch),
-        compiler_params=pltpu.CompilerParams(vmem_limit_bytes=VMEM_LIMIT),
+        compiler_params=pltpu.CompilerParams(vmem_limit_bytes=limit),
         cost_estimate=pl.CostEstimate(flops=int(micros * FLOPS_PER_MICRO), bytes_accessed=0, transcendentals=0),
     )
 
@@ -166,16 +167,16 @@
     def mate(value):
         return lax.ppermute(value, "shift", [(i, i ^ 1) for i in range(count)])
 
-    def gather_pairs(value):
-        if count & (count - 1):
-            return gather_shift(value)
-        rows_each = value.shape[0]
-        step = 1
-        while step < count:
-            value = jnp.concatenate(
-                [value, lax.ppermute(value, "shift", [(i, i ^ step) for i in range(count)])], axis=0
-            )
-            step *= 2
+    def mate_rows(value, step):
+        return jnp.concatenate(
+            [value, lax.ppermute(value, "shift", [(i, i ^ step) for i in range(count)])], axis=0
+        )
+
+    def rest_of_pairs(value, parts):
+        while parts < count:
+            value = mate_rows(value, parts)
+            parts *= 2
+        rows_each = value.shape[0] // count
         return [value[k * rows_each:(k + 1) * rows_each] for k in range(count)]
 
     def gather_shift(value):
@@ -201,82 +202,7 @@
     slot = place % blk_dev + blk_dev * jnp.where(group == 1, 0, jnp.where(group == partner_group, 1, 2))
     slot = slot.astype(jnp.int32)
 
-    mine = lax.dynamic_slice_in_dim(eigvectors, half_id * per_half, per_half, axis=0)
-    cuts = 1
-    per_cut = per_half // cuts
-    sends = [v.reshape(per_cut * blk, blk) for v in jnp.split(mine, cuts, axis=0)]
-    sends[0] = jnp.concatenate([sends[0], eigvalues], axis=0)
-    vec_first = [swap(v) for v in sends]
-    def prepare(start_hbm, vec_hbm, spun, packed, vec_st, vec_ts, start, vec, sems):
-        copies = []
-        for i in range(blk_dev):
-            rows = pl.ds(i * blk, blk)
-            copies.append(pltpu.make_async_copy(vec_hbm.at[i], vec.at[i], sems.at[i]))
-            copies.append(pltpu.make_async_copy(start_hbm.at[rows], start.at[rows], sems.at[blk_dev + i]))
-        for copy in copies:
-            copy.start()
-        for copy in copies:
-            copy.wait()
-        mine_now = own_group()
-        lefts, rights = [], []
-        for i in range(blk_dev):
-            v = vec[i]
-            vh, vl = split(v)
-            vec_st[i, :blk, :] = vh
-            vec_st[i, blk:, :] = vl
-            th, tl = split(v.T)
-            vec_ts[i, :blk, :] = th
-            vec_ts[i, blk:, :] = tl
-            lefts.append(jnp.concatenate([th, tl], axis=0))
-            rights.append(split(spread(start[i * blk:(i + 1) * blk, :], mine_now, width)))
-        turned = [dot_three(left, *right) for left, right in zip(lefts, rights)]
-        for i in range(blk_dev):
-            spun[i] = turned[i]
-            store_packed(packed, i, turned[i])
-
-    sds = jax.ShapeDtypeStruct
-    spun, packed, vec_st, vec_ts = call(
-        prepare,
-        (
-            sds((blk_dev, blk, ncol), F32),
-            sds((packs * blk, ncol), F32),
-            sds((blk_dev, 2 * blk, blk), BF16),
-            sds((blk_dev, 2 * blk, blk), BF16),
-        ),
-        in_specs=[HBM()] * 2,
-        scratch=[
-            pltpu.VMEM((rows_here, ncol), F32), pltpu.VMEM((blk_dev, blk, blk), F32),
-            pltpu.SemaphoreType.DMA((2 * blk_dev,)),
-        ],
-        micros=2.5,
-    )(start_block, eigvectors)
-
-    vec_first = [after(v, packed) for v in vec_first]
-    vec_second = [pass_on(v, a) for v, a in zip(sends, vec_first)]
-    mate_first = [mate(v[:per_cut * blk]) for v in vec_first] if halves == 2 else []
-    pack_first = swap(packed)
-    pack_second = pass_on(packed, after(pack_first, *mate_first))
-    begun = (pack_first, *mate_first)
-
-    def couple(coup_hbm, spun_ref, val, vec, cst, xh, xl, scale_ref, coup, sems):
-        copies = [pltpu.make_async_copy(coup_hbm.at[i], coup.at[i], sems.at[i]) for i in range(blk_dev)]
-        for copy in copies:
-            copy.start()
-        fields = []
-        for i in range(blk_dev):
-            b = DAMPING * spun_ref[i]
-            re, im = inverse_scale(column_of(val[i:i + 1, :]))
-            scale_ref[i, :, :ncol] = re
-            scale_ref[i, :, ncol:] = im
-            fields.append(apply_three(vec[i], jnp.concatenate([re * b, im * b], axis=1)))
-        for i in range(blk_dev):
-            put(xh, xl, i, fields[i])
-        for i in range(blk_dev):
-            copies[i].wait()
-            for k in range(nnb):
-                ch, cl = split(coup[i, k])
-                cst[i, :blk, k * blk:(k + 1) * blk] = ch
-                cst[i, blk:, k * blk:(k + 1) * blk] = cl
+    lead = lax.dynamic_slice_in_dim(eigvectors, half_id * per_half, per_half, axis=0).reshape(per_half * blk, blk)
 
     def put(xh, xl, block, value):
         rows = pl.ds(pl.multiple_of(block * blk, blk), blk)
@@ -284,47 +210,108 @@
         xh[rows, :] = h
         xl[rows, :] = l
 
-    field_shape = (sds((rows_here, wide), BF16), sds((rows_here, wide), BF16))
-    cst, own_h, own_l, scale = call(
-        couple,
-        (sds((blk_dev, 2 * blk, nnb * blk), BF16),) + field_shape + (sds((blk_dev, blk, wide), F32),),
-        in_specs=[HBM()] + [VMEM()] * 3,
-        scratch=[pltpu.VMEM((blk_dev, nnb, blk, blk), F32), pltpu.SemaphoreType.DMA((blk_dev,))],
-        micros=2.5,
-    )(after(couplings, *begun), spun, eigvalues, vec_st)
-
-    vec_second = [after(v, cst) for v in vec_second]
-    mate_second = [mate(v[:per_cut * blk]) for v in vec_second] if halves == 2 else []
+    def prepare(
+        start_hbm, vec_hbm, coup_hbm, val, spun, packed, vec_st, vec_ts, scale, cst, start, vec, coup, sems
+    ):
+        blocks = range(blk_dev)
+        copies, late = [], []
+        for i in blocks:
+            rows = pl.ds(i * blk, blk)
+            copies.append(pltpu.make_async_copy(vec_hbm.at[i], vec.at[i], sems.at[i]))
+            copies.append(pltpu.make_async_copy(start_hbm.at[rows], start.at[rows], sems.at[blk_dev + i]))
+            late.append(pltpu.make_async_copy(coup_hbm.at[i], coup.at[i], sems.at[2 * blk_dev + i]))
+        for copy in copies + late:
+            copy.start()
+        scales = [inverse_scale(column_of(val[i:i + 1, :])) for i in blocks]
+        for i in blocks:
+            scale[i, :, :ncol] = scales[i][0]
+            scale[i, :, ncol:] = scales[i][1]
+        for copy in copies:
+            copy.wait()
+        mine_now = own_group()
+        packed[packs * blk:, :] = val[...]
+        backward, rights = [], []
+        for i in blocks:
+            v = vec[i]
+            backward.append(jnp.concatenate(split(v.T), axis=0))
+            vec_st[i] = jnp.concatenate(split(v), axis=0)
+            vec_ts[i] = backward[i]
+            rights.append(split(spread(start[i * blk:(i + 1) * blk, :], mine_now, width)))
+        turned = [dot_three(backward[i], *rights[i]) for i in blocks]
+        for i in blocks:
+            spun[i] = turned[i]
+            store_packed(packed, i, turned[i])
+        for i in blocks:
+            late[i].wait()
+            for k in range(nnb):
+                ch, cl = split(coup[i, k])
+                cst[i, :blk, k * blk:(k + 1) * blk] = ch
+                cst[i, blk:, k * blk:(k + 1) * blk] = cl
+
+    sds = jax.ShapeDtypeStruct
+    spun, packed, vec_st, vec_ts, scale, cst = call(
+        prepare,
+        (
+            sds((blk_dev, blk, ncol), F32),
+            sds((packs * blk + blk_dev, ncol), F32),
+            sds((blk_dev, 2 * blk, blk), BF16),
+            sds((blk_dev, 2 * blk, blk), BF16),
+            sds((blk_dev, blk, wide), F32),
+            sds((blk_dev, 2 * blk, nnb * blk), BF16),
+        ),
+        in_specs=[HBM()] * 3 + [VMEM()],
+        scratch=[
+            pltpu.VMEM((rows_here, ncol), F32), pltpu.VMEM((blk_dev, blk, blk), F32),
+            pltpu.VMEM((blk_dev, nnb, blk, blk), F32), pltpu.SemaphoreType.DMA((3 * blk_dev,)),
+        ],
+        micros=20.0, limit=FIRST_LIMIT,
+    )(start_block, eigvectors, couplings, eigvalues)
+
+    lead_first = after(swap(lead), packed)
+    pack_first = swap(after(packed, lead_first))
+    lead_second = pass_on(lead, lead_first)
+    pack_second = pass_on(packed, pack_first)
+
+    mate_first = [mate(after(lead_first, pack_first))] if halves == 2 else []
 
     def fill_first(inputs, xh, xl, offset):
         pack = inputs[0]
-        vecs = inputs[1:]
         names, lefts, rights = [], [], []
         for h in range(halves):
             base = ((lax.axis_index("shift") + h) % halves) * per_half if halves > 1 else 0
-            for c in range(cuts):
-                for j in range(per_cut):
-                    b = base + c * per_cut + j
-                    row0 = pl.multiple_of((b // count) * blk, blk)
-                    turned = spread(pack[pl.ds(row0, blk), :], b % count, width) * DAMPING
-                    re, im = inverse_scale(column_of(vecs[0][pl.ds(per_cut * blk + b, 1), :]))
-                    names.append(b)
-                    lefts.append(jnp.concatenate(split(vecs[h * cuts + c][j * blk:(j + 1) * blk, :]), axis=0))
-                    rights.append(jnp.concatenate([re * turned, im * turned], axis=1))
+            for j in range(per_half):
+                b = base + j
+                row0 = pl.multiple_of((b // count) * blk, blk)
+                turned = spread(pack[pl.ds(row0, blk), :], b % count, width) * DAMPING
+                re, im = inverse_scale(column_of(pack[pl.ds(packs * blk + b, 1), :]))
+                vector = inputs[1 + h][j * blk:(j + 1) * blk, :]
+                names.append(b)
+                lefts.append(jnp.concatenate(split(vector), axis=0))
+                rights.append(jnp.concatenate([re * turned, im * turned], axis=1))
         fields = [apply_three(left, right) for left, right in zip(lefts, rights)]
         for b, field in zip(names, fields):
             put(xh, xl, b + offset, field)
 
-    def first_partner(*refs):
-        fill_first(refs[:-2], refs[-2], refs[-1], 0)
-
-    partners = [pack_first] + vec_first + mate_first
-    partner_h, partner_l = call(
-        first_partner,
-        field_shape,
-        in_specs=[VMEM()] * len(partners),
-        micros=1.5,
-    )(*partners)
+    partners = [pack_first, lead_first] + mate_first
+
+    def first_two(*refs):
+        spun_ref, scale_ref, vec = refs[:3]
+        inputs = refs[3:3 + len(partners)]
+        xh, xl = refs[3 + len(partners):]
+        firsts = []
+        for i in range(blk_dev):
+            turned = DAMPING * spun_ref[i]
+            s = scale_ref[i]
+            firsts.append(jnp.concatenate([s[:, :ncol] * turned, s[:, ncol:] * turned], axis=1))
+        fields = [apply_three(vec[i], firsts[i]) for i in range(blk_dev)]
+        for i in range(blk_dev):
+            put(xh, xl, i, fields[i])
+        fill_first(inputs, xh, xl, blk_dev)
+
+    two_shape = (sds((2 * rows_here, wide), BF16), sds((2 * rows_here, wide), BF16))
+    two_h, two_l = call(
+        first_two, two_shape, in_specs=[VMEM()] * (3 + len(partners)), micros=2.0,
+    )(spun, scale, vec_st, *partners)
 
     def near_of(ref, slots, i):
         return jnp.concatenate(
@@ -346,18 +333,17 @@
     chunks = len(sizes)
     spots = [(c, j) for c in range(chunks) for j in range(sizes[c])]
 
-    others = [pack_second] + vec_second + mate_second
+    mate_second = [mate(after(lead_second, pack_second))] if halves == 2 else []
+    others = [pack_second, lead_second] + mate_second
 
     def second_iterate(*refs):
-        slots, oh, ol, ph, pl_, c, vec, vec_t, spun_ref, scale_ref = refs[:10]
-        inputs = refs[10:10 + len(others)]
-        outs = refs[10 + len(others):10 + len(others) + chunks]
-        hats, xh, xl = refs[10 + len(others) + chunks:]
+        slots, th, tl, c, vec, vec_t, spun_ref, scale_ref = refs[:8]
+        inputs = refs[8:8 + len(others)]
+        outs = refs[8 + len(others):8 + len(others) + chunks]
+        hats, xh, xl = refs[8 + len(others) + chunks:]
         fill_first(inputs, xh, xl, 2 * blk_dev)
-        xh[:rows_here, :] = oh[...]
-        xl[:rows_here, :] = ol[...]
-        xh[rows_here:2 * rows_here, :] = ph[...]
-        xl[rows_here:2 * rows_here, :] = pl_[...]
+        xh[:2 * rows_here, :] = th[...]
+        xl[:2 * rows_here, :] = tl[...]
         blocks = range(blk_dev)
         sums = [coupled(slots, c, xh, xl, i) for i in blocks]
         turned = [apply_three(vec_t[i], sums[i]) for i in blocks]
@@ -372,10 +358,10 @@
     *own, hats = call(
         second_iterate,
         [sds((size, blk, wide), F32) for size in sizes] + [sds((blk_dev, blk, wide), F32)],
-        in_specs=[SMEM()] + [VMEM()] * (9 + len(others)),
+        in_specs=[SMEM()] + [VMEM()] * (7 + len(others)),
         scratch=field_scratch,
         micros=6.0,
-    )(slot, own_h, own_l, partner_h, partner_l, cst, vec_st, vec_ts, spun, scale, *others)
+    )(slot, two_h, two_l, cst, vec_st, vec_ts, spun, scale, *others)
 
     two_first, two_second = halo(own)
 
@@ -439,36 +425,43 @@
 
     span = ncol // count
 
-    def image_of(slots, own_f, first_f, second_f, full_ref, gram_ref, c, diag, packed_out, sums, xh, xl, image_ref):
+    def image_of(slots, own_f, first_f, second_f, full_ref, c, diag, joined, xh, xl, image_ref):
         for f, field in enumerate((own_f, first_f, second_f)):
             for b in range(blk_dev):
                 put(xh, xl, f * blk_dev + b, spread(field[block_rows(b), :], b % count, width))
         for i in range(blk_dev):
             image = diag[i] + coupled(slots, c, xh, xl, i)
             image_ref[i * blk:(i + 1) * blk, :] = image
-            store_packed(packed_out, i, image)
+            store_packed(joined, i, image)
         part = exact(full_ref[...], image_ref[...], ((0,), (0,)))
         piece = jnp.zeros((span, ncol), F32)
         for s in range(count):
             piece = piece + jnp.where(
                 lane_group((span, ncol), width) == s, part[s * span:(s + 1) * span, :], 0.0
             )
-        sums[:ncol, :] = gram_ref[...]
-        sums[ncol:, :] = piece
-
-    image, sums = call(
+        joined[packs * blk:, :] = piece
+
+    joined = call(
         image_of,
-        (sds((packs * blk, ncol), F32), sds((ncol + span, ncol), F32)),
-        in_specs=[SMEM()] + [VMEM()] * 7,
+        sds((packs * blk + span, ncol), F32),
+        in_specs=[SMEM()] + [VMEM()] * 6,
         scratch=[pltpu.VMEM((3 * rows_here, ncol), BF16)] * 2 + [pltpu.VMEM((rows_here, ncol), F32)],
         micros=3.8,
-    )(slot, filtered, filt_first, filt_second, full, gram, cst, diagonal)
-
-    image_all = gather_pairs(image)
-    sums = sum_rows(sums)
-    moment_all = gather_pairs(sums[ncol:])
-
-    def factor_of(sums_ref, inverse):
+    )(slot, filtered, filt_first, filt_second, full, cst, diagonal)
+
+    if count & (count - 1):
+        pieces, parts = gather_shift(joined), count
+    else:
+        parts = min(2, count)
+        both = mate_rows(joined, 1) if parts == 2 else joined
+        pieces = [both[k * (packs * blk + span):(k + 1) * (packs * blk + span)] for k in range(parts)]
+    sums = sum_rows(jnp.concatenate([gram] + [piece[packs * blk:] for piece in pieces], axis=0))
+    image_all = rest_of_pairs(jnp.concatenate([piece[:packs * blk] for piece in pieces], axis=0), parts)
+    moment_all = rest_of_pairs(sums[ncol:], parts)
+
+    def factor_of(*refs):
+        sums_ref, full_ref, pieces = refs[0], refs[1], refs[2:2 + count]
+        inverse, basis_ref, image_ref, raw = refs[2 + count:]
         tiles = ncol // 8
         a = [sums_ref[t * 8:(t + 1) * 8, :] * (1.0 / total) for t in range(tiles)]
         lanes = lax.broadcasted_iota(jnp.int32, (8, ncol), 1)
@@ -502,30 +495,31 @@
             pivot = jnp.sum(jnp.where(lanes == subs + t * 8, a[t], 0.0), axis=1, keepdims=True)
             inverse[t * 8:(t + 1) * 8, :] = e[t] * (1.0 / jnp.sqrt(pivot))
 
-    inverse = call(
-        factor_of, sds((ncol, ncol), F32), in_specs=[VMEM()], micros=5.5,
-    )(sums)
-
-    def finish(*refs):
-        full_ref, pieces, moments, inv_ref = refs[0], refs[1:1 + count], refs[1 + count:1 + 2 * count], refs[1 + 2 * count]
-        basis_ref, image_ref, projected_ref, raw = refs[2 + 2 * count:]
+        inv = inverse[...]
+        for i in range(blk_dev):
+            raw[i * blk:(i + 1) * blk, :] = unpacked(pieces, block_rows(i), i % count)
+        basis_ref[...] = exact(full_ref[...], inv, ((1,), (1,)))
+        image_ref[...] = exact(raw[...], inv, ((1,), (1,)))
+
+    inverse, basis, basis_image = call(
+        factor_of,
+        (sds((ncol, ncol), F32), sds((rows_here, ncol), F32), sds((rows_here, ncol), F32)),
+        in_specs=[VMEM()] * (2 + count),
+        scratch=[pltpu.VMEM((rows_here, ncol), F32)],
+        micros=7.0,
+    )(sums, full, *image_all)
+
+    def project(*refs):
+        moments, inv_ref, projected_ref = refs[:count], refs[count], refs[count + 1]
         inv = inv_ref[...]
         strips = [unpacked(moments, slice(0, span), g) for g in range(count)]
         m = jnp.concatenate(strips, axis=0) * (1.0 / total)
-        for i in range(blk_dev):
-            raw[i * blk:(i + 1) * blk, :] = unpacked(pieces, block_rows(i), i % count)
-        half = exact(inv, m, ((1,), (0,)))
-        basis_ref[...] = exact(full_ref[...], inv, ((1,), (1,)))
-        image_ref[...] = exact(raw[...], inv, ((1,), (1,)))
-        projected_ref[...] = exact(half, inv, ((1,), (1,)))
-
-    return call(
-        finish,
-        (sds((rows_here, ncol), F32), sds((rows_here, ncol), F32), sds((ncol, ncol), F32)),
-        in_specs=[VMEM()] * (2 + 2 * count),
-        scratch=[pltpu.VMEM((rows_here, ncol), F32)],
-        micros=3.0,
-    )(full, *image_all, *moment_all, inverse)
+        projected_ref[...] = exact(exact(inv, m, ((1,), (0,))), inv, ((1,), (1,)))
+
+    projected = call(
+        project, sds((ncol, ncol), F32), in_specs=[VMEM()] * (count + 1), micros=1.0,
+    )(*moment_all, inverse)
+    return (basis, basis_image, projected)
 
 
 def solution(mesh):

time: 119 us -> 113 us (0.950)
  waiting for transfers between devices: 33 us -> 28.1 us
  local copies, waits for them, and re-layouts: 5.31 us -> 2.95 us
  Pallas kernels: 26 us -> 28.2 us
    unnamed x10 -> x12, local copies, waits for them, and re-layouts: 4.28 us -> 1.92 us
    ppermute x3, waiting for transfers between devices: 8.93 us -> 6.65 us  [sum_rows(): lax.ppermute(value, 'rows', [(i, i ^ step) for i in range(nrows)])]
    pallas_call x6 -> x5, Pallas kernels: 16 us -> 18.3 us  [the longest x1 6.21 us: per_device(): call(factor_of, (sds((ncol, ncol), F32), sds((rows_here, ncol), F32), sds...]
    ppermute x7, waiting for transfers between devices: 11.9 us -> 9.96 us  [swap(): return lax.ppermute(value, 'rows', [(i, i ^ 1) for i in range(nrows)])]
    ppermute x4 -> x3, waiting for transfers between devices: 2.84 us -> 1.33 us  [mate_rows(): lax.ppermute(value, 'shift', [(i, i ^ step) for i in range(count)])]
    ppermute x7, starting transfers between devices: 29.9 us -> 28.7 us  [pass_on(): return lax.ppermute(arrived, 'rows', pairs)]
    ppermute x4 -> x3, starting transfers between devices: 2.69 us -> 3.24 us  [mate_rows(): lax.ppermute(value, 'shift', [(i, i ^ step) for i in range(count)])]
  transfers between devices with their start and end apart: 26 -> 25, of which waited for: 16 -> 14; matrix products, arithmetic and copies ran while one was open for 0% -> 0% of each run, Pallas kernels for 9% -> 13%
where the time goes in v3:
time: 113 us; the launch traced here: 112 us
  starting transfers between devices  52 us (46%)
  Pallas kernels  28.2 us (25%)
  waiting for transfers between devices  28.1 us (25%)
  local copies, waits for them, and re-layouts  2.95 us (3%)
    ppermute x7, starting transfers between devices, pass_on(): return lax.ppermute(arrived, 'rows', pairs)  28.7 us
    ppermute x7, starting transfers between devices, swap(): return lax.ppermute(value, 'rows', [(i, i ^ 1) for i in range(nrows)])  10.8 us
    ppermute x7, waiting for transfers between devices, swap(): return lax.ppermute(value, 'rows', [(i, i ^ 1) for i in range(nrows)])  9.96 us
    ppermute x7, waiting for transfers between devices, pass_on(): return lax.ppermute(arrived, 'rows', pairs)  9.26 us
    ppermute x3, starting transfers between devices, sum_rows(): lax.ppermute(value, 'rows', [(i, i ^ step) for i in range(nrows)])  7.41 us
    ppermute x3, waiting for transfers between devices, sum_rows(): lax.ppermute(value, 'rows', [(i, i ^ step) for i in range(nrows)])  6.65 us
    pallas_call x1, Pallas kernels, per_device(): call(factor_of, (sds((ncol, ncol), F32), sds((rows_here, ncol), F32), sds...  6.21 us
    pallas_call x1, Pallas kernels, per_device(): call(prepare, (sds((blk_dev, blk, ncol), F32), sds((packs * blk + blk_dev...  5.64 us
  transfers between devices with their start and end apart: 25, of which 14 were waited for; matrix products, arithmetic and copies ran while one was open for 0% of the time, Pallas kernels for 13%

profile of v3, /device:TPU:0, one launch (start us, length us, event | category | flops | bytes accessed | tf_op | source)
XLA Modules:
  0.0 112.4 jit_solution(2962898836147208730)
XLA Ops:
  1.6 3.0 %collective-permute-start = (f32[512,128]{1,0:T(8,128)S(1)}, f32[512,128]{1,0:T(8,128)S(1)}, u32[]{:S(2)}, u32[]{:S(2)}) collective-permute-start(f32[512,128]{1,0:T(8,128)S(1)} %bitcast.1), channel_id=1, source_target_pairs={{0,1},{1,0},{2,3},{3,2},{4,5},{5,4},{6,7},{7,6},{8,9},{9,8},{10,11... | collective-permute-start | bytes 786440 | tf_op jit(solution)/shard_map/ppermute | solution.py:150
  5.3 5.6 %shard_map.76 = (f32[8,128,128]{2,1,0:T(8,128)S(1)}, f32[264,128]{1,0:T(8,128)S(1)}, bf16[8,256,128]{2,1,0:T(8,128)(2,1)S(1)}, bf16[8,256,128]{2,1,0:T(8,128)(2,...) custom-call(f32[1024,128]{1,0:T(8,128)} %start_hbm.1, f32[8,128,128]{2,1,0:T(8,128)} %vec_hbm.1, ...), custom_call_target="tpu_custom_call" | custom-call | flops 22000001024 | tf_op jit(solution)/shard_map/pallas_call | solution.py:252
  11.0 1.7 %collective-permute-start.1 = (f32[264,128]{1,0:T(8,128)S(1)}, f32[264,128]{1,0:T(8,128)S(1)}, u32[]{:S(2)}, u32[]{:S(2)}) collective-permute-start(f32[264,128]{1,0:T(8,128)S(1)} %get-tuple-element.32), channel_id=1, source_target_pairs={{0,1},{1,0},{2,3},{3,2},{4,5},{5,4},{6,7},{7,6},{8,9},{9,8},{10,11... | collective-permute-start | bytes 405512 | tf_op jit(solution)/shard_map/ppermute | solution.py:150
  12.7 3.5 %collective-permute-start.4 = (f32[512,128]{1,0:T(8,128)S(1)}, f32[512,128]{1,0:T(8,128)S(1)}, u32[]{:S(2)}, u32[]{:S(2)}) collective-permute-start(f32[512,128]{1,0:T(8,128)S(1)} %collective-permute-done.refs_4_), channel_id=1, source_target_pairs={{0,2},{2,4},{4,6},{3,1},{5,3},{7,5},{8,10},{10,12},{12,14},{11,9},... | collective-permute-start | bytes 786440 | tf_op jit(solution)/shard_map/ppermute | solution.py:156
  16.2 3.5 %collective-permute-start.3 = (f32[264,128]{1,0:T(8,128)S(1)}, f32[264,128]{1,0:T(8,128)S(1)}, u32[]{:S(2)}, u32[]{:S(2)}) collective-permute-start(f32[264,128]{1,0:T(8,128)S(1)} %collective-permute-done.1.refs_3_), channel_id=1, source_target_pairs={{0,2},{2,4},{4,6},{3,1},{5,3},{7,5},{8,10},{10,12},{12,14},{11,9},... | collective-permute-start | bytes 405512 | tf_op jit(solution)/shard_map/ppermute | solution.py:156
  19.8 2.2 %collective-permute-done.4.refs_9_ = f32[512,128]{1,0:T(8,128)S(1)} collective-permute-done((f32[512,128]{1,0:T(8,128)S(1)}, f32[512,128]{1,0:T(8,128)S(1)}, u32[]{:S(2)}, u32[]{:S(2)}) %collective-permute-start.4) | collective-permute-done | bytes 262176 | tf_op jit(solution)/shard_map/ppermute | solution.py:156
  22.0 1.4 %collective-permute-done.3.refs_8_ = f32[264,128]{1,0:T(8,128)S(1)} collective-permute-done((f32[264,128]{1,0:T(8,128)S(1)}, f32[264,128]{1,0:T(8,128)S(1)}, u32[]{:S(2)}, u32[]{:S(2)}) %collective-permute-start.3) | collective-permute-done | bytes 135200 | tf_op jit(solution)/shard_map/ppermute | solution.py:156
  24.7 1.4 %shard_map.77 = (bf16[2048,256]{1,0:T(8,128)(2,1)S(1)}, bf16[2048,256]{1,0:T(8,128)(2,1)S(1)}) custom-call(f32[8,128,128]{2,1,0:T(8,128)S(1)} %get-tuple-element.27.refs_0_.refs_6_.refs_17_, f32[8,128,256]{2,1,0:T(8,128)S(1)} %copy-done.3, bf16[8,256,128]{2,1,0:T(8,128)(2,1)S(1)} %get-tuple-element.29.refs_2_.refs_4_.refs_15_, ...), custom_call_target="tpu_custom_call" | custom-call | flops 2200000000 | tf_op jit(solution)/shard_map/pallas_call | solution.py:312
  26.2 4.7 %shard_map.78 = (f32[2,128,256]{2,1,0:T(8,128)S(1)}, f32[2,128,256]{2,1,0:T(8,128)S(1)}, f32[2,128,256]{2,1,0:T(8,128)S(1)}, f32[2,128,256]{2,1,0:T(8,128)S(1)}, f32[8,128,256]{2,1,0:T(8,128)S(1)}) custom-call(s32[8,8]{1,0:T(8,128)S(1)} %fusion.refs_0_.slots, bf16[2048,256]{1,0:T(8,128)(2,1)S(1)} %get-tuple-element.34.refs_1_, ...), custom_call_target="tpu_custom_call" | custom-call | flops 6600000000 | tf_op jit(solution)/shard_map/pallas_call | solution.py:358
  30.9 2.0 %collective-permute-start.6 = (f32[2,128,256]{2,1,0:T(8,128)S(1)}, f32[2,128,256]{2,1,0:T(8,128)S(1)}, u32[]{:S(2)}, u32[]{:S(2)}) collective-permute-start(f32[2,128,256]{2,1,0:T(8,128)S(1)} %get-tuple-element.39.refs_1_), channel_id=1, source_target_pairs={{0,1},{1,0},{2,3},{3,2},{4,5},{5,4},{6,7},{7,6},{8,9},{9,8},{10,11... | collective-permute-start | bytes 786440 | tf_op jit(solution)/shard_map/ppermute | solution.py:150
  33.0 1.9 %collective-permute-start.8 = (f32[2,128,256]{2,1,0:T(8,128)S(1)}, f32[2,128,256]{2,1,0:T(8,128)S(1)}, u32[]{:S(2)}, u32[]{:S(2)}) collective-permute-start(f32[2,128,256]{2,1,0:T(8,128)S(1)} %get-tuple-element.41.refs_3_), channel_id=1, source_target_pairs={{0,1},{1,0},{2,3},{3,2},{4,5},{5,4},{6,7},{7,6},{8,9},{9,8},{10,11... | collective-permute-start | bytes 786440 | tf_op jit(solution)/shard_map/ppermute | solution.py:150
  35.0 5.1 %collective-permute-done.6.refs_5_ = f32[2,128,256]{2,1,0:T(8,128)S(1)} collective-permute-done((f32[2,128,256]{2,1,0:T(8,128)S(1)}, f32[2,128,256]{2,1,0:T(8,128)S(1)}, u32[]{:S(2)}, u32[]{:S(2)}) %collective-permute-start.6) | collective-permute-done | bytes 262176 | tf_op jit(solution)/shard_map/ppermute | solution.py:150
  40.1 4.3 %collective-permute-start.10 = (f32[2,128,256]{2,1,0:T(8,128)S(1)}, f32[2,128,256]{2,1,0:T(8,128)S(1)}, u32[]{:S(2)}, u32[]{:S(2)}) collective-permute-start(f32[2,128,256]{2,1,0:T(8,128)S(1)} %collective-permute-done.6.refs_5_), channel_id=1, source_target_pairs={{0,2},{2,4},{4,6},{3,1},{5,3},{7,5},{8,10},{10,12},{12,14},{11,9},... | collective-permute-start | bytes 786440 | tf_op jit(solution)/shard_map/ppermute | solution.py:156
  45.8 4.3 %collective-permute-start.11 = (f32[2,128,256]{2,1,0:T(8,128)S(1)}, f32[2,128,256]{2,1,0:T(8,128)S(1)}, u32[]{:S(2)}, u32[]{:S(2)}) collective-permute-start(f32[2,128,256]{2,1,0:T(8,128)S(1)} %collective-permute-done.7.refs_6_), channel_id=1, source_target_pairs={{0,2},{2,4},{4,6},{3,1},{5,3},{7,5},{8,10},{10,12},{12,14},{11,9},... | collective-permute-start | bytes 786440 | tf_op jit(solution)/shard_map/ppermute | solution.py:156
  51.4 4.3 %collective-permute-start.12 = (f32[2,128,256]{2,1,0:T(8,128)S(1)}, f32[2,128,256]{2,1,0:T(8,128)S(1)}, u32[]{:S(2)}, u32[]{:S(2)}) collective-permute-start(f32[2,128,256]{2,1,0:T(8,128)S(1)} %collective-permute-done.8.refs_7_), channel_id=1, source_target_pairs={{0,2},{2,4},{4,6},{3,1},{5,3},{7,5},{8,10},{10,12},{12,14},{11,9},... | collective-permute-start | bytes 786440 | tf_op jit(solution)/shard_map/ppermute | solution.py:156
  56.7 4.2 %collective-permute-start.13 = (f32[2,128,256]{2,1,0:T(8,128)S(1)}, f32[2,128,256]{2,1,0:T(8,128)S(1)}, u32[]{:S(2)}, u32[]{:S(2)}) collective-permute-start(f32[2,128,256]{2,1,0:T(8,128)S(1)} %collective-permute-done.9.refs_8_), channel_id=1, source_target_pairs={{0,2},{2,4},{4,6},{3,1},{5,3},{7,5},{8,10},{10,12},{12,14},{11,9},... | collective-permute-start | bytes 786440 | tf_op jit(solution)/shard_map/ppermute | solution.py:156
  61.0 5.4 %collective-permute-done.13.refs_12_ = f32[2,128,256]{2,1,0:T(8,128)S(1)} collective-permute-done((f32[2,128,256]{2,1,0:T(8,128)S(1)}, f32[2,128,256]{2,1,0:T(8,128)S(1)}, u32[]{:S(2)}, u32[]{:S(2)}) %collective-permute-start.13) | collective-permute-done | bytes 262176 | tf_op jit(solution)/shard_map/ppermute | solution.py:156
  66.3 4.1 %shard_map.79 = (f32[256,128]{1,0:T(8,128)S(1)}, f32[8,128,128]{2,1,0:T(8,128)S(1)}) custom-call(s32[8,8]{1,0:T(8,128)S(1)} %fusion.refs_0_.slots, f32[2,128,256]{2,1,0:T(8,128)S(1)} %get-tuple-element.39.refs_1_, f32[2,128,256]{2,1,0:T(8,128)S(1)} %get-tuple-element.40.refs_2_, f32[2,128,256]{2,1,0:T(8,128)S(1)} %get-tuple-element.41.refs_3_, ...), custom_call_target="tpu_custom_call" | custom-call | flops 6600000000 | tf_op jit(solution)/shard_map/pallas_call | solution.py:392
  70.4 1.9 %collective-permute-start.17 = (f32[256,128]{1,0:T(8,128)S(1)}, f32[256,128]{1,0:T(8,128)S(1)}, u32[]{:S(2)}, u32[]{:S(2)}) collective-permute-start(f32[256,128]{1,0:T(8,128)S(1)} %get-tuple-element.44.refs_0_.own_f), channel_id=1, source_target_pairs={{0,1},{1,0},{2,3},{3,2},{4,5},{5,4},{6,7},{7,6},{8,9},{9,8},{10,11... | collective-permute-start | bytes 393224 | tf_op jit(solution)/shard_map/ppermute | solution.py:150
  72.4 1.5 %collective-permute-start.15 = (f32[256,128]{1,0:T(8,128)S(1)}, f32[256,128]{1,0:T(8,128)S(1)}, u32[]{:S(2)}, u32[]{:S(2)}) collective-permute-start(f32[256,128]{1,0:T(8,128)S(1)} %get-tuple-element.44.refs_0_.own_f), channel_id=1, source_target_pairs={{16,0},{24,8},{0,16},{8,24},{17,1},{25,9},{1,17},{9,25},{18,2},{26... | collective-permute-start | bytes 393224 | tf_op jit(solution)/shard_map/ppermute | solution.py:184
  75.5 4.6 %collective-permute-start.18 = (f32[256,128]{1,0:T(8,128)S(1)}, f32[256,128]{1,0:T(8,128)S(1)}, u32[]{:S(2)}, u32[]{:S(2)}) collective-permute-start(f32[256,128]{1,0:T(8,128)S(1)} %collective-permute-done.17.first_f), channel_id=1, source_target_pairs={{0,2},{2,4},{4,6},{3,1},{5,3},{7,5},{8,10},{10,12},{12,14},{11,9},... | collective-permute-start | bytes 393224 | tf_op jit(solution)/shard_map/ppermute | solution.py:156
  82.4 3.7 %shard_map.81 = f32[288,128]{1,0:T(8,128)S(1)} custom-call(s32[8,8]{1,0:T(8,128)S(1)} %fusion.refs_0_.slots, f32[256,128]{1,0:T(8,128)S(1)} %get-tuple-element.44.refs_0_.own_f, f32[256,128]{1,0:T(8,128)S(1)} %collective-permute-done.17.first_f, f32[256,128]{1,0:T(8,128)S(1)} %collective-permute-done.18.second_f, ...), custom_call_target="tpu_custom_call" | custom-call | flops 4180000000 | tf_op jit(solution)/shard_map/pallas_call | solution.py:444
  86.2 1.3 %collective-permute-done.19 = f32[288,128]{1,0:T(8,128)S(1)} collective-permute-done((f32[288,128]{1,0:T(8,128)S(1)}, f32[288,128]{1,0:T(8,128)S(1)}, u32[]{:S(2)}, u32[]{:S(2)}) %collective-permute-start.19) | collective-permute-done | bytes 147488 | tf_op jit(solution)/shard_map/ppermute | solution.py:172
  87.6 1.9 %collective-permute-start.20 = (f32[192,128]{1,0:T(8,128)S(1)}, f32[192,128]{1,0:T(8,128)S(1)}, u32[]{:S(2)}, u32[]{:S(2)}) collective-permute-start(f32[192,128]{1,0:T(8,128)S(1)} %pad_maximum_fusion.1), channel_id=1, source_target_pairs={{0,1},{1,0},{2,3},{3,2},{4,5},{5,4},{6,7},{7,6},{8,9},{9,8},{10,11... | collective-permute-start | bytes 294920 | tf_op jit(solution)/shard_map/ppermute | solution.py:195
  89.5 1.6 %collective-permute-start.23 = (f32[512,128]{1,0:T(8,128)S(1)}, f32[512,128]{1,0:T(8,128)S(1)}, u32[]{:S(2)}, u32[]{:S(2)}) collective-permute-start(f32[512,128]{1,0:T(8,128)S(1)} %pad_maximum_fusion), channel_id=1, source_target_pairs={{0,16},{8,24},{16,0},{24,8},{1,17},{9,25},{17,1},{25,9},{2,18},{10... | collective-permute-start | bytes 786440 | tf_op jit(solution)/shard_map/ppermute | solution.py:172
  91.1 1.5 %collective-permute-done.20 = f32[192,128]{1,0:T(8,128)S(1)} collective-permute-done((f32[192,128]{1,0:T(8,128)S(1)}, f32[192,128]{1,0:T(8,128)S(1)}, u32[]{:S(2)}, u32[]{:S(2)}) %collective-permute-start.20) | collective-permute-done | bytes 98336 | tf_op jit(solution)/shard_map/ppermute | solution.py:195
  92.6 2.4 %collective-permute-start.21 = (f32[192,128]{1,0:T(8,128)S(1)}, f32[192,128]{1,0:T(8,128)S(1)}, u32[]{:S(2)}, u32[]{:S(2)}) collective-permute-start(f32[192,128]{1,0:T(8,128)S(1)} %fusion.3), channel_id=1, source_target_pairs={{0,2},{1,3},{2,0},{3,1},{4,6},{5,7},{6,4},{7,5},{8,10},{9,11},{10,... | collective-permute-start | bytes 294920 | tf_op jit(solution)/shard_map/ppermute | solution.py:195
  95.0 2.6 %collective-permute-done.21 = f32[192,128]{1,0:T(8,128)S(1)} collective-permute-done((f32[192,128]{1,0:T(8,128)S(1)}, f32[192,128]{1,0:T(8,128)S(1)}, u32[]{:S(2)}, u32[]{:S(2)}) %collective-permute-start.21) | collective-permute-done | bytes 98336 | tf_op jit(solution)/shard_map/ppermute | solution.py:195
  97.6 3.1 %collective-permute-start.22 = (f32[192,128]{1,0:T(8,128)S(1)}, f32[192,128]{1,0:T(8,128)S(1)}, u32[]{:S(2)}, u32[]{:S(2)}) collective-permute-start(f32[192,128]{1,0:T(8,128)S(1)} %add.36), channel_id=1, source_target_pairs={{0,4},{1,5},{2,6},{3,7},{4,0},{5,1},{6,2},{7,3},{8,12},{9,13},{10,... | collective-permute-start | bytes 294920 | tf_op jit(solution)/shard_map/ppermute | solution.py:195
  100.7 2.6 %collective-permute-done.22 = f32[192,128]{1,0:T(8,128)S(1)} collective-permute-done((f32[192,128]{1,0:T(8,128)S(1)}, f32[192,128]{1,0:T(8,128)S(1)}, u32[]{:S(2)}, u32[]{:S(2)}) %collective-permute-start.22) | collective-permute-done | bytes 98336 | tf_op jit(solution)/shard_map/ppermute | solution.py:195
  103.3 1.6 %collective-permute-start.24 = (f32[64,128]{1,0:T(8,128)S(1)}, f32[64,128]{1,0:T(8,128)S(1)}, u32[]{:S(2)}, u32[]{:S(2)}) collective-permute-start(f32[64,128]{1,0:T(8,128)S(1)} %slice.54), channel_id=1, source_target_pairs={{0,16},{8,24},{16,0},{24,8},{1,17},{9,25},{17,1},{25,9},{2,18},{10... | collective-permute-start | bytes 98312 | tf_op jit(solution)/shard_map/ppermute | solution.py:172
  104.9 6.2 %shard_map.82 = (f32[128,128]{1,0:T(8,128)S(1)}, f32[1024,128]{1,0:T(8,128)}, f32[1024,128]{1,0:T(8,128)}) custom-call(f32[192,128]{1,0:T(8,128)S(1)} %add.37.refs_0_, f32[1024,128]{1,0:T(8,128)S(1)} %get-tuple-element.46.full_ref.refs_1_, f32[256,128]{1,0:T(8,128)S(1)} %slice.48.refs_2_, f32[256,128]{1,0:T(8,128)S(1)} %slice.49.refs_3_, ...), custom_call_target="tpu_custom_call" | custom-call | flops 7699999744 | tf_op jit(solution)/shard_map/pallas_call | solution.py:504
  (53 shorter events, 12.2 us)
Async XLA Ops:
  1.6 9.4 %collective-permute-start = (f32[512,128]{1,0:T(8,128)S(1)}, f32[512,128]{1,0:T(8,128)S(1)}, u32[]{:S(2)}, u32[]{:S(2)}) collective-permute-start(f32[512,128]{1,0:T(8,128)S(1)} %bitcast.1), channel_id=1, source_target_pairs={{0,1},{1,0},{2,3},{3,2},{4,5},{5,4},{6,7},{7,6},{8,9},{9,8},{10,11... | collective-permute-start | bytes 786440 | tf_op jit(solution)/shard_map/ppermute | solution.py:150
  4.7 0.7 copy-start
  5.3 18.1 %copy-start.5 = (s32[8,8]{1,0:T(8,128)S(1)}, s32[8,8]{1,0:T(8,128)}, u32[]{:S(2)}) copy-start(s32[8,8]{1,0:T(8,128)} %param.5) | copy-start | bytes 772
  11.0 5.2 %collective-permute-start.1 = (f32[264,128]{1,0:T(8,128)S(1)}, f32[264,128]{1,0:T(8,128)S(1)}, u32[]{:S(2)}, u32[]{:S(2)}) collective-permute-start(f32[264,128]{1,0:T(8,128)S(1)} %get-tuple-element.32), channel_id=1, source_target_pairs={{0,1},{1,0},{2,3},{3,2},{4,5},{5,4},{6,7},{7,6},{8,9},{9,8},{10,11... | collective-permute-start | bytes 405512 | tf_op jit(solution)/shard_map/ppermute | solution.py:150
  12.7 9.3 %collective-permute-start.4 = (f32[512,128]{1,0:T(8,128)S(1)}, f32[512,128]{1,0:T(8,128)S(1)}, u32[]{:S(2)}, u32[]{:S(2)}) collective-permute-start(f32[512,128]{1,0:T(8,128)S(1)} %collective-permute-done.refs_4_), channel_id=1, source_target_pairs={{0,2},{2,4},{4,6},{3,1},{5,3},{7,5},{8,10},{10,12},{12,14},{11,9},... | collective-permute-start | bytes 786440 | tf_op jit(solution)/shard_map/ppermute | solution.py:156
  16.2 7.3 %collective-permute-start.3 = (f32[264,128]{1,0:T(8,128)S(1)}, f32[264,128]{1,0:T(8,128)S(1)}, u32[]{:S(2)}, u32[]{:S(2)}) collective-permute-start(f32[264,128]{1,0:T(8,128)S(1)} %collective-permute-done.1.refs_3_), channel_id=1, source_target_pairs={{0,2},{2,4},{4,6},{3,1},{5,3},{7,5},{8,10},{10,12},{12,14},{11,9},... | collective-permute-start | bytes 405512 | tf_op jit(solution)/shard_map/ppermute | solution.py:156
  19.7 3.8 %collective-permute-start.2 = (f32[512,128]{1,0:T(8,128)S(1)}, f32[512,128]{1,0:T(8,128)S(1)}, u32[]{:S(2)}, u32[]{:S(2)}) collective-permute-start(f32[512,128]{1,0:T(8,128)S(1)} %collective-permute-done.refs_4_), channel_id=1, source_target_pairs={{0,8},{8,0},{16,24},{24,16},{1,9},{9,1},{17,25},{25,17},{2,10},{10... | collective-permute-start | bytes 786440 | tf_op jit(solution)/shard_map/ppermute | solution.py:168
  19.8 6.4 %copy-start.2 = (bf16[8,256,1024]{2,1,0:T(8,128)(2,1)S(1)}, bf16[8,256,1024]{2,1,0:T(8,128)(2,1)}, u32[]{:S(2)}) copy-start(bf16[8,256,1024]{2,1,0:T(8,128)(2,1)} %get-tuple-element.36.refs_3_.refs_14_.c) | copy-start | bytes 12582916
  23.5 2.7 %collective-permute-start.5 = (f32[512,128]{1,0:T(8,128)S(1)}, f32[512,128]{1,0:T(8,128)S(1)}, u32[]{:S(2)}, u32[]{:S(2)}) collective-permute-start(f32[512,128]{1,0:T(8,128)S(1)} %collective-permute-done.4.refs_9_), channel_id=1, source_target_pairs={{0,8},{8,0},{16,24},{24,16},{1,9},{9,1},{17,25},{25,17},{2,10},{10... | collective-permute-start | bytes 786440 | tf_op jit(solution)/shard_map/ppermute | solution.py:168
  23.5 1.2 %copy-start.3 = (f32[8,128,256]{2,1,0:T(8,128)S(1)}, f32[8,128,256]{2,1,0:T(8,128)}, u32[]{:S(2)}) copy-start(f32[8,128,256]{2,1,0:T(8,128)} %get-tuple-element.28.refs_1_.refs_7_.refs_18_) | copy-start | bytes 3145732
  24.7 1.4 %copy-start.4 = (f32[8,128,256]{2,1,0:T(8,128)S(1)}, f32[8,128,256]{2,1,0:T(8,128)}, u32[]{:S(2)}) copy-start(f32[8,128,256]{2,1,0:T(8,128)} %get-tuple-element.28.refs_1_.refs_7_.refs_18_) | copy-start | bytes 3145732
  26.2 40.2 %copy-start.1 = (f32[8,128]{1,0:T(8,128)S(1)}, f32[8,128]{1,0:T(8,128)}, u32[]{:S(2)}) copy-start(f32[8,128]{1,0:T(8,128)} %refs_19_.1) | copy-start | bytes 12292
  30.9 9.2 %collective-permute-start.6 = (f32[2,128,256]{2,1,0:T(8,128)S(1)}, f32[2,128,256]{2,1,0:T(8,128)S(1)}, u32[]{:S(2)}, u32[]{:S(2)}) collective-permute-start(f32[2,128,256]{2,1,0:T(8,128)S(1)} %get-tuple-element.39.refs_1_), channel_id=1, source_target_pairs={{0,1},{1,0},{2,3},{3,2},{4,5},{5,4},{6,7},{7,6},{8,9},{9,8},{10,11... | collective-permute-start | bytes 786440 | tf_op jit(solution)/shard_map/ppermute | solution.py:150
  32.9 12.9 %collective-permute-start.7 = (f32[2,128,256]{2,1,0:T(8,128)S(1)}, f32[2,128,256]{2,1,0:T(8,128)S(1)}, u32[]{:S(2)}, u32[]{:S(2)}) collective-permute-start(f32[2,128,256]{2,1,0:T(8,128)S(1)} %get-tuple-element.40.refs_2_), channel_id=1, source_target_pairs={{0,1},{1,0},{2,3},{3,2},{4,5},{5,4},{6,7},{7,6},{8,9},{9,8},{10,11... | collective-permute-start | bytes 786440 | tf_op jit(solution)/shard_map/ppermute | solution.py:150
  33.0 18.4 %collective-permute-start.8 = (f32[2,128,256]{2,1,0:T(8,128)S(1)}, f32[2,128,256]{2,1,0:T(8,128)S(1)}, u32[]{:S(2)}, u32[]{:S(2)}) collective-permute-start(f32[2,128,256]{2,1,0:T(8,128)S(1)} %get-tuple-element.41.refs_3_), channel_id=1, source_target_pairs={{0,1},{1,0},{2,3},{3,2},{4,5},{5,4},{6,7},{7,6},{8,9},{9,8},{10,11... | collective-permute-start | bytes 786440 | tf_op jit(solution)/shard_map/ppermute | solution.py:150
  34.9 21.8 %collective-permute-start.9 = (f32[2,128,256]{2,1,0:T(8,128)S(1)}, f32[2,128,256]{2,1,0:T(8,128)S(1)}, u32[]{:S(2)}, u32[]{:S(2)}) collective-permute-start(f32[2,128,256]{2,1,0:T(8,128)S(1)} %get-tuple-element.42.refs_4_), channel_id=1, source_target_pairs={{0,1},{1,0},{2,3},{3,2},{4,5},{5,4},{6,7},{7,6},{8,9},{9,8},{10,11... | collective-permute-start | bytes 786440 | tf_op jit(solution)/shard_map/ppermute | solution.py:150
  40.1 20.8 %collective-permute-start.10 = (f32[2,128,256]{2,1,0:T(8,128)S(1)}, f32[2,128,256]{2,1,0:T(8,128)S(1)}, u32[]{:S(2)}, u32[]{:S(2)}) collective-permute-start(f32[2,128,256]{2,1,0:T(8,128)S(1)} %collective-permute-done.6.refs_5_), channel_id=1, source_target_pairs={{0,2},{2,4},{4,6},{3,1},{5,3},{7,5},{8,10},{10,12},{12,14},{11,9},... | collective-permute-start | bytes 786440 | tf_op jit(solution)/shard_map/ppermute | solution.py:156
  45.8 15.2 %collective-permute-start.11 = (f32[2,128,256]{2,1,0:T(8,128)S(1)}, f32[2,128,256]{2,1,0:T(8,128)S(1)}, u32[]{:S(2)}, u32[]{:S(2)}) collective-permute-start(f32[2,128,256]{2,1,0:T(8,128)S(1)} %collective-permute-done.7.refs_6_), channel_id=1, source_target_pairs={{0,2},{2,4},{4,6},{3,1},{5,3},{7,5},{8,10},{10,12},{12,14},{11,9},... | collective-permute-start | bytes 786440 | tf_op jit(solution)/shard_map/ppermute | solution.py:156
  51.4 9.6 %collective-permute-start.12 = (f32[2,128,256]{2,1,0:T(8,128)S(1)}, f32[2,128,256]{2,1,0:T(8,128)S(1)}, u32[]{:S(2)}, u32[]{:S(2)}) collective-permute-start(f32[2,128,256]{2,1,0:T(8,128)S(1)} %collective-permute-done.8.refs_7_), channel_id=1, source_target_pairs={{0,2},{2,4},{4,6},{3,1},{5,3},{7,5},{8,10},{10,12},{12,14},{11,9},... | collective-permute-start | bytes 786440 | tf_op jit(solution)/shard_map/ppermute | solution.py:156
  56.7 9.7 %collective-permute-start.13 = (f32[2,128,256]{2,1,0:T(8,128)S(1)}, f32[2,128,256]{2,1,0:T(8,128)S(1)}, u32[]{:S(2)}, u32[]{:S(2)}) collective-permute-start(f32[2,128,256]{2,1,0:T(8,128)S(1)} %collective-permute-done.9.refs_8_), channel_id=1, source_target_pairs={{0,2},{2,4},{4,6},{3,1},{5,3},{7,5},{8,10},{10,12},{12,14},{11,9},... | collective-permute-start | bytes 786440 | tf_op jit(solution)/shard_map/ppermute | solution.py:156
  70.4 5.0 %collective-permute-start.17 = (f32[256,128]{1,0:T(8,128)S(1)}, f32[256,128]{1,0:T(8,128)S(1)}, u32[]{:S(2)}, u32[]{:S(2)}) collective-permute-start(f32[256,128]{1,0:T(8,128)S(1)} %get-tuple-element.44.refs_0_.own_f), channel_id=1, source_target_pairs={{0,1},{1,0},{2,3},{3,2},{4,5},{5,4},{6,7},{7,6},{8,9},{9,8},{10,11... | collective-permute-start | bytes 393224 | tf_op jit(solution)/shard_map/ppermute | solution.py:150
  72.4 7.7 %collective-permute-start.16 = (f32[256,128]{1,0:T(8,128)S(1)}, f32[256,128]{1,0:T(8,128)S(1)}, u32[]{:S(2)}, u32[]{:S(2)}) collective-permute-start(f32[256,128]{1,0:T(8,128)S(1)} %get-tuple-element.44.refs_0_.own_f), channel_id=1, source_target_pairs={{24,0},{16,8},{8,16},{0,24},{25,1},{17,9},{9,17},{1,25},{26,2},{18... | collective-permute-start | bytes 393224 | tf_op jit(solution)/shard_map/ppermute | solution.py:184
  72.4 8.6 %collective-permute-start.15 = (f32[256,128]{1,0:T(8,128)S(1)}, f32[256,128]{1,0:T(8,128)S(1)}, u32[]{:S(2)}, u32[]{:S(2)}) collective-permute-start(f32[256,128]{1,0:T(8,128)S(1)} %get-tuple-element.44.refs_0_.own_f), channel_id=1, source_target_pairs={{16,0},{24,8},{0,16},{8,24},{17,1},{25,9},{1,17},{9,25},{18,2},{26... | collective-permute-start | bytes 393224 | tf_op jit(solution)/shard_map/ppermute | solution.py:184
  73.9 7.1 %collective-permute-start.14 = (f32[256,128]{1,0:T(8,128)S(1)}, f32[256,128]{1,0:T(8,128)S(1)}, u32[]{:S(2)}, u32[]{:S(2)}) collective-permute-start(f32[256,128]{1,0:T(8,128)S(1)} %get-tuple-element.44.refs_0_.own_f), channel_id=1, source_target_pairs={{8,0},{0,8},{24,16},{16,24},{9,1},{1,9},{25,17},{17,25},{10,2},{2,... | collective-permute-start | bytes 393224 | tf_op jit(solution)/shard_map/ppermute | solution.py:184
  75.5 6.9 %collective-permute-start.18 = (f32[256,128]{1,0:T(8,128)S(1)}, f32[256,128]{1,0:T(8,128)S(1)}, u32[]{:S(2)}, u32[]{:S(2)}) collective-permute-start(f32[256,128]{1,0:T(8,128)S(1)} %collective-permute-done.17.first_f), channel_id=1, source_target_pairs={{0,2},{2,4},{4,6},{3,1},{5,3},{7,5},{8,10},{10,12},{12,14},{11,9},... | collective-permute-start | bytes 393224 | tf_op jit(solution)/shard_map/ppermute | solution.py:156
  86.1 1.4 %collective-permute-start.19 = (f32[288,128]{1,0:T(8,128)S(1)}, f32[288,128]{1,0:T(8,128)S(1)}, u32[]{:S(2)}, u32[]{:S(2)}) collective-permute-start(f32[288,128]{1,0:T(8,128)S(1)} %shard_map.81), channel_id=1, source_target_pairs={{0,8},{8,0},{16,24},{24,16},{1,9},{9,1},{17,25},{25,17},{2,10},{10... | collective-permute-start | bytes 442376 | tf_op jit(solution)/shard_map/ppermute | solution.py:172
  87.6 5.0 %collective-permute-start.20 = (f32[192,128]{1,0:T(8,128)S(1)}, f32[192,128]{1,0:T(8,128)S(1)}, u32[]{:S(2)}, u32[]{:S(2)}) collective-permute-start(f32[192,128]{1,0:T(8,128)S(1)} %pad_maximum_fusion.1), channel_id=1, source_target_pairs={{0,1},{1,0},{2,3},{3,2},{4,5},{5,4},{6,7},{7,6},{8,9},{9,8},{10,11... | collective-permute-start | bytes 294920 | tf_op jit(solution)/shard_map/ppermute | solution.py:195
  89.5 11.2 %collective-permute-start.23 = (f32[512,128]{1,0:T(8,128)S(1)}, f32[512,128]{1,0:T(8,128)S(1)}, u32[]{:S(2)}, u32[]{:S(2)}) collective-permute-start(f32[512,128]{1,0:T(8,128)S(1)} %pad_maximum_fusion), channel_id=1, source_target_pairs={{0,16},{8,24},{16,0},{24,8},{1,17},{9,25},{17,1},{25,9},{2,18},{10... | collective-permute-start | bytes 786440 | tf_op jit(solution)/shard_map/ppermute | solution.py:172
  92.6 5.0 %collective-permute-start.21 = (f32[192,128]{1,0:T(8,128)S(1)}, f32[192,128]{1,0:T(8,128)S(1)}, u32[]{:S(2)}, u32[]{:S(2)}) collective-permute-start(f32[192,128]{1,0:T(8,128)S(1)} %fusion.3), channel_id=1, source_target_pairs={{0,2},{1,3},{2,0},{3,1},{4,6},{5,7},{6,4},{7,5},{8,10},{9,11},{10,... | collective-permute-start | bytes 294920 | tf_op jit(solution)/shard_map/ppermute | solution.py:195
  97.6 5.7 %collective-permute-start.22 = (f32[192,128]{1,0:T(8,128)S(1)}, f32[192,128]{1,0:T(8,128)S(1)}, u32[]{:S(2)}, u32[]{:S(2)}) collective-permute-start(f32[192,128]{1,0:T(8,128)S(1)} %add.36), channel_id=1, source_target_pairs={{0,4},{1,5},{2,6},{3,7},{4,0},{5,1},{6,2},{7,3},{8,12},{9,13},{10,... | collective-permute-start | bytes 294920 | tf_op jit(solution)/shard_map/ppermute | solution.py:195
  103.3 7.8 %collective-permute-start.24 = (f32[64,128]{1,0:T(8,128)S(1)}, f32[64,128]{1,0:T(8,128)S(1)}, u32[]{:S(2)}, u32[]{:S(2)}) collective-permute-start(f32[64,128]{1,0:T(8,128)S(1)} %slice.54), channel_id=1, source_target_pairs={{0,16},{8,24},{16,0},{24,8},{1,17},{9,25},{17,1},{25,9},{2,18},{10... | collective-permute-start | bytes 98312 | tf_op jit(solution)/shard_map/ppermute | solution.py:172

commit v4 on v3

--- a/solution.py
+++ b/solution.py
@@ -211,7 +211,7 @@
         xl[rows, :] = l
 
     def prepare(
-        start_hbm, vec_hbm, coup_hbm, val, spun, packed, vec_st, vec_ts, scale, cst, start, vec, coup, sems
+        start_hbm, vec_hbm, coup_hbm, val, spun, packed, vec_st, vec_ts, cst, start, vec, coup, sems
     ):
         blocks = range(blk_dev)
         copies, late = [], []
@@ -222,10 +222,6 @@
             late.append(pltpu.make_async_copy(coup_hbm.at[i], coup.at[i], sems.at[2 * blk_dev + i]))
         for copy in copies + late:
             copy.start()
-        scales = [inverse_scale(column_of(val[i:i + 1, :])) for i in blocks]
-        for i in blocks:
-            scale[i, :, :ncol] = scales[i][0]
-            scale[i, :, ncol:] = scales[i][1]
         for copy in copies:
             copy.wait()
         mine_now = own_group()
@@ -249,14 +245,13 @@
                 cst[i, blk:, k * blk:(k + 1) * blk] = cl
 
     sds = jax.ShapeDtypeStruct
-    spun, packed, vec_st, vec_ts, scale, cst = call(
+    spun, packed, vec_st, vec_ts, cst = call(
         prepare,
         (
             sds((blk_dev, blk, ncol), F32),
             sds((packs * blk + blk_dev, ncol), F32),
             sds((blk_dev, 2 * blk, blk), BF16),
             sds((blk_dev, 2 * blk, blk), BF16),
-            sds((blk_dev, blk, wide), F32),
             sds((blk_dev, 2 * blk, nnb * blk), BF16),
         ),
         in_specs=[HBM()] * 3 + [VMEM()],
@@ -295,23 +290,25 @@
     partners = [pack_first, lead_first] + mate_first
 
     def first_two(*refs):
-        spun_ref, scale_ref, vec = refs[:3]
+        spun_ref, val, vec = refs[:3]
         inputs = refs[3:3 + len(partners)]
-        xh, xl = refs[3 + len(partners):]
+        xh, xl, scale = refs[3 + len(partners):]
         firsts = []
         for i in range(blk_dev):
             turned = DAMPING * spun_ref[i]
-            s = scale_ref[i]
-            firsts.append(jnp.concatenate([s[:, :ncol] * turned, s[:, ncol:] * turned], axis=1))
+            re, im = inverse_scale(column_of(val[i:i + 1, :]))
+            scale[i, :, :ncol] = re
+            scale[i, :, ncol:] = im
+            firsts.append(jnp.concatenate([re * turned, im * turned], axis=1))
         fields = [apply_three(vec[i], firsts[i]) for i in range(blk_dev)]
         for i in range(blk_dev):
             put(xh, xl, i, fields[i])
         fill_first(inputs, xh, xl, blk_dev)
 
-    two_shape = (sds((2 * rows_here, wide), BF16), sds((2 * rows_here, wide), BF16))
-    two_h, two_l = call(
+    two_shape = (sds((2 * rows_here, wide), BF16),) * 2 + (sds((blk_dev, blk, wide), F32),)
+    two_h, two_l, scale = call(
         first_two, two_shape, in_specs=[VMEM()] * (3 + len(partners)), micros=2.0,
-    )(spun, scale, vec_st, *partners)
+    )(spun, eigvalues, vec_st, *partners)
 
     def near_of(ref, slots, i):
         return jnp.concatenate(
@@ -410,15 +407,37 @@
             out = jnp.where(lanes == s, moved, out)
         return out
 
+    half_col = ncol // 2
+
+    def triangle(gram):
+        top, low = gram[:half_col, :], gram[half_col:, :]
+        lanes = lax.broadcasted_iota(jnp.int32, top.shape, 1)
+        rows = lax.broadcasted_iota(jnp.int32, top.shape, 0)
+        body = jnp.where(lanes - half_col >= rows, low, pltpu.roll(top, half_col, 1))
+        diagonal = jnp.sum(jnp.where(lanes == rows, top, 0.0), axis=0, keepdims=True)
+        return body, jnp.broadcast_to(diagonal, (8, ncol))
+
+    def whole_of(body, diagonal):
+        lanes = lax.broadcasted_iota(jnp.int32, body.shape, 1)
+        rows = lax.broadcasted_iota(jnp.int32, body.shape, 0)
+        moved = pltpu.roll(body, half_col, 1)
+        top = jnp.where((lanes < rows) | (lanes >= half_col), moved, jnp.where(lanes == rows, 0.5 * diagonal, 0.0))
+        past = lanes - half_col
+        low = jnp.where(past > rows, body, jnp.where(past == rows, 0.5 * body, 0.0))
+        both = jnp.concatenate([top, low], axis=0)
+        return both + both.T
+
     def gram_of(*refs):
         pieces, full, gram = refs[:count], refs[count], refs[1 + count]
         for i in range(blk_dev):
             full[i * blk:(i + 1) * blk, :] = unpacked(pieces, block_rows(i), i % count)
-        gram[...] = exact(full[...], full[...], ((0,), (0,)))
+        body, diagonal = triangle(exact(full[...], full[...], ((0,), (0,))))
+        gram[:half_col, :] = body
+        gram[half_col:, :] = diagonal
 
     full, gram = call(
         gram_of,
-        (sds((rows_here, ncol), F32), sds((ncol, ncol), F32)),
+        (sds((rows_here, ncol), F32), sds((half_col + 8, ncol), F32)),
         in_specs=[VMEM()] * count,
         micros=GRAM_MICROS,
     )(*filt_all)
@@ -457,13 +476,14 @@
         pieces = [both[k * (packs * blk + span):(k + 1) * (packs * blk + span)] for k in range(parts)]
     sums = sum_rows(jnp.concatenate([gram] + [piece[packs * blk:] for piece in pieces], axis=0))
     image_all = rest_of_pairs(jnp.concatenate([piece[:packs * blk] for piece in pieces], axis=0), parts)
-    moment_all = rest_of_pairs(sums[ncol:], parts)
+    moment_all = rest_of_pairs(after(sums[half_col + 8:], *image_all), parts)
 
     def factor_of(*refs):
         sums_ref, full_ref, pieces = refs[0], refs[1], refs[2:2 + count]
         inverse, basis_ref, image_ref, raw = refs[2 + count:]
         tiles = ncol // 8
-        a = [sums_ref[t * 8:(t + 1) * 8, :] * (1.0 / total) for t in range(tiles)]
+        gram_now = whole_of(sums_ref[:half_col, :], sums_ref[half_col:half_col + 1, :]) * (1.0 / total)
+        a = [gram_now[t * 8:(t + 1) * 8, :] for t in range(tiles)]
         lanes = lax.broadcasted_iota(jnp.int32, (8, ncol), 1)
         subs = lax.broadcasted_iota(jnp.int32, (8, ncol), 0)
         e = [jnp.where(lanes == subs + t * 8, 1.0, 0.0).astype(F32) for t in range(tiles)]
@@ -506,7 +526,7 @@
         (sds((ncol, ncol), F32), sds((rows_here, ncol), F32), sds((rows_here, ncol), F32)),
         in_specs=[VMEM()] * (2 + count),
         scratch=[pltpu.VMEM((rows_here, ncol), F32)],
-        micros=7.0,
+        micros=0.5,
     )(sums, full, *image_all)
 
     def project(*refs):

time: 113 us -> 111 us (0.982)
  local copies, waits for them, and re-layouts: 2.95 us -> 1.73 us
    unnamed x12 -> x8, local copies, waits for them, and re-layouts: 1.92 us -> 0.7 us
  transfers between devices with their start and end apart: 25 -> 25, of which waited for: 14 -> 15; matrix products, arithmetic and copies ran while one was open for 0% -> 0% of each run, Pallas kernels for 13% -> 13%
where the time goes in v4:
time: 111 us; the launch traced here: 110 us
  starting transfers between devices  52.2 us (47%)
  Pallas kernels  28.3 us (25%)
  waiting for transfers between devices  27 us (24%)
  local copies, waits for them, and re-layouts  1.73 us (2%)
    ppermute x7, starting transfers between devices, pass_on(): return lax.ppermute(arrived, 'rows', pairs)  29.1 us
    ppermute x7, starting transfers between devices, swap(): return lax.ppermute(value, 'rows', [(i, i ^ 1) for i in range(nrows)])  10.7 us
    ppermute x7, waiting for transfers between devices, swap(): return lax.ppermute(value, 'rows', [(i, i ^ 1) for i in range(nrows)])  9.88 us
    ppermute x7, waiting for transfers between devices, pass_on(): return lax.ppermute(arrived, 'rows', pairs)  9.39 us
    ppermute x3, starting transfers between devices, sum_rows(): lax.ppermute(value, 'rows', [(i, i ^ step) for i in range(nrows)])  7.37 us
    pallas_call x1, Pallas kernels, per_device(): call(factor_of, (sds((ncol, ncol), F32), sds((rows_here, ncol), F32), sds...  6.22 us
    ppermute x3, waiting for transfers between devices, sum_rows(): lax.ppermute(value, 'rows', [(i, i ^ step) for i in range(nrows)])  5.63 us
    pallas_call x1, Pallas kernels, per_device(): call(prepare, (sds((blk_dev, blk, ncol), F32), sds((packs * blk + blk_dev...  5.45 us
  transfers between devices with their start and end apart: 25, of which 15 were waited for; matrix products, arithmetic and copies ran while one was open for 0% of the time, Pallas kernels for 13%

profile of v4, /device:TPU:0, one launch (start us, length us, event | category | flops | bytes accessed | tf_op | source)
XLA Modules:
  0.0 110.2 jit_solution(6576764423901154876)
XLA Ops:
  1.6 3.0 %collective-permute-start = (f32[512,128]{1,0:T(8,128)S(1)}, f32[512,128]{1,0:T(8,128)S(1)}, u32[]{:S(2)}, u32[]{:S(2)}) collective-permute-start(f32[512,128]{1,0:T(8,128)S(1)} %bitcast.1), channel_id=1, source_target_pairs={{0,1},{1,0},{2,3},{3,2},{4,5},{5,4},{6,7},{7,6},{8,9},{9,8},{10,11... | collective-permute-start | bytes 786440 | tf_op jit(solution)/shard_map/ppermute | solution.py:150
  5.3 5.5 %shard_map.76 = (f32[8,128,128]{2,1,0:T(8,128)S(1)}, f32[264,128]{1,0:T(8,128)S(1)}, bf16[8,256,128]{2,1,0:T(8,128)(2,1)S(1)}, bf16[8,256,128]{2,1,0:T(8,128)(2,1)S(1)}, bf16[8,256,1024]{2,1,0:T(8,128)(2,1)}) custom-call(f32[1024,128]{1,0:T(8,128)} %start_hbm.1, f32[8,128,128]{2,1,0:T(8,128)} %vec_hbm.1, f32[8,8,128,128]{3,2,1,0:T(8,128)} %coup_hbm.1, ...), custom_call_target="tpu_custom_call" | custom-call | flops 22000001024 | tf_op jit(solution)/shard_map/pallas_call | solution.py:248
  11.0 1.7 %collective-permute-start.1 = (f32[264,128]{1,0:T(8,128)S(1)}, f32[264,128]{1,0:T(8,128)S(1)}, u32[]{:S(2)}, u32[]{:S(2)}) collective-permute-start(f32[264,128]{1,0:T(8,128)S(1)} %get-tuple-element.32), channel_id=1, source_target_pairs={{0,1},{1,0},{2,3},{3,2},{4,5},{5,4},{6,7},{7,6},{8,9},{9,8},{10,11... | collective-permute-start | bytes 405512 | tf_op jit(solution)/shard_map/ppermute | solution.py:150
  12.7 3.5 %collective-permute-start.4 = (f32[512,128]{1,0:T(8,128)S(1)}, f32[512,128]{1,0:T(8,128)S(1)}, u32[]{:S(2)}, u32[]{:S(2)}) collective-permute-start(f32[512,128]{1,0:T(8,128)S(1)} %collective-permute-done.refs_4_), channel_id=1, source_target_pairs={{0,2},{2,4},{4,6},{3,1},{5,3},{7,5},{8,10},{10,12},{12,14},{11,9},... | collective-permute-start | bytes 786440 | tf_op jit(solution)/shard_map/ppermute | solution.py:156
  16.2 3.5 %collective-permute-start.3 = (f32[264,128]{1,0:T(8,128)S(1)}, f32[264,128]{1,0:T(8,128)S(1)}, u32[]{:S(2)}, u32[]{:S(2)}) collective-permute-start(f32[264,128]{1,0:T(8,128)S(1)} %collective-permute-done.1.refs_3_), channel_id=1, source_target_pairs={{0,2},{2,4},{4,6},{3,1},{5,3},{7,5},{8,10},{10,12},{12,14},{11,9},... | collective-permute-start | bytes 405512 | tf_op jit(solution)/shard_map/ppermute | solution.py:156
  19.8 2.2 %collective-permute-done.4.refs_9_ = f32[512,128]{1,0:T(8,128)S(1)} collective-permute-done((f32[512,128]{1,0:T(8,128)S(1)}, f32[512,128]{1,0:T(8,128)S(1)}, u32[]{:S(2)}, u32[]{:S(2)}) %collective-permute-start.4) | collective-permute-done | bytes 262176 | tf_op jit(solution)/shard_map/ppermute | solution.py:156
  22.0 1.4 %collective-permute-done.3.refs_8_ = f32[264,128]{1,0:T(8,128)S(1)} collective-permute-done((f32[264,128]{1,0:T(8,128)S(1)}, f32[264,128]{1,0:T(8,128)S(1)}, u32[]{:S(2)}, u32[]{:S(2)}) %collective-permute-start.3) | collective-permute-done | bytes 135200 | tf_op jit(solution)/shard_map/ppermute | solution.py:156
  23.5 1.6 %shard_map.77 = (bf16[2048,256]{1,0:T(8,128)(2,1)S(1)}, bf16[2048,256]{1,0:T(8,128)(2,1)S(1)}, f32[8,128,256]{2,1,0:T(8,128)S(1)}) custom-call(f32[8,128,128]{2,1,0:T(8,128)S(1)} %get-tuple-element.28.refs_0_.refs_6_.refs_17_, f32[8,128]{1,0:T(8,128)S(1)} %copy-done.1, bf16[8,256,128]{2,1,0:T(8,128)(2,1)S(1)} %get-tuple-element.29.refs_2_.refs_4_.refs_15_, ...), custom_call_target="tpu_custom_call" | custom-call | flops 2200000000 | tf_op jit(solution)/shard_map/pallas_call | solution.py:309
  25.1 4.7 %shard_map.78 = (f32[2,128,256]{2,1,0:T(8,128)S(1)}, f32[2,128,256]{2,1,0:T(8,128)S(1)}, f32[2,128,256]{2,1,0:T(8,128)S(1)}, f32[2,128,256]{2,1,0:T(8,128)S(1)}, f32[8,128,256]{2,1,0:T(8,128)S(1)}) custom-call(s32[8,8]{1,0:T(8,128)S(1)} %fusion.refs_0_.slots, bf16[2048,256]{1,0:T(8,128)(2,1)S(1)} %get-tuple-element.34.refs_1_, ...), custom_call_target="tpu_custom_call" | custom-call | flops 6600000000 | tf_op jit(solution)/shard_map/pallas_call | solution.py:355
  29.9 1.8 %collective-permute-start.6 = (f32[2,128,256]{2,1,0:T(8,128)S(1)}, f32[2,128,256]{2,1,0:T(8,128)S(1)}, u32[]{:S(2)}, u32[]{:S(2)}) collective-permute-start(f32[2,128,256]{2,1,0:T(8,128)S(1)} %get-tuple-element.40.refs_1_), channel_id=1, source_target_pairs={{0,1},{1,0},{2,3},{3,2},{4,5},{5,4},{6,7},{7,6},{8,9},{9,8},{10,11... | collective-permute-start | bytes 786440 | tf_op jit(solution)/shard_map/ppermute | solution.py:150
  31.9 1.7 %collective-permute-start.8 = (f32[2,128,256]{2,1,0:T(8,128)S(1)}, f32[2,128,256]{2,1,0:T(8,128)S(1)}, u32[]{:S(2)}, u32[]{:S(2)}) collective-permute-start(f32[2,128,256]{2,1,0:T(8,128)S(1)} %get-tuple-element.42.refs_3_), channel_id=1, source_target_pairs={{0,1},{1,0},{2,3},{3,2},{4,5},{5,4},{6,7},{7,6},{8,9},{9,8},{10,11... | collective-permute-start | bytes 786440 | tf_op jit(solution)/shard_map/ppermute | solution.py:150
  34.0 5.0 %collective-permute-done.6.refs_5_ = f32[2,128,256]{2,1,0:T(8,128)S(1)} collective-permute-done((f32[2,128,256]{2,1,0:T(8,128)S(1)}, f32[2,128,256]{2,1,0:T(8,128)S(1)}, u32[]{:S(2)}, u32[]{:S(2)}) %collective-permute-start.6) | collective-permute-done | bytes 262176 | tf_op jit(solution)/shard_map/ppermute | solution.py:150
  39.0 4.4 %collective-permute-start.10 = (f32[2,128,256]{2,1,0:T(8,128)S(1)}, f32[2,128,256]{2,1,0:T(8,128)S(1)}, u32[]{:S(2)}, u32[]{:S(2)}) collective-permute-start(f32[2,128,256]{2,1,0:T(8,128)S(1)} %collective-permute-done.6.refs_5_), channel_id=1, source_target_pairs={{0,2},{2,4},{4,6},{3,1},{5,3},{7,5},{8,10},{10,12},{12,14},{11,9},... | collective-permute-start | bytes 786440 | tf_op jit(solution)/shard_map/ppermute | solution.py:156
  44.6 4.4 %collective-permute-start.11 = (f32[2,128,256]{2,1,0:T(8,128)S(1)}, f32[2,128,256]{2,1,0:T(8,128)S(1)}, u32[]{:S(2)}, u32[]{:S(2)}) collective-permute-start(f32[2,128,256]{2,1,0:T(8,128)S(1)} %collective-permute-done.7.refs_6_), channel_id=1, source_target_pairs={{0,2},{2,4},{4,6},{3,1},{5,3},{7,5},{8,10},{10,12},{12,14},{11,9},... | collective-permute-start | bytes 786440 | tf_op jit(solution)/shard_map/ppermute | solution.py:156
  50.3 4.4 %collective-permute-start.12 = (f32[2,128,256]{2,1,0:T(8,128)S(1)}, f32[2,128,256]{2,1,0:T(8,128)S(1)}, u32[]{:S(2)}, u32[]{:S(2)}) collective-permute-start(f32[2,128,256]{2,1,0:T(8,128)S(1)} %collective-permute-done.8.refs_7_), channel_id=1, source_target_pairs={{0,2},{2,4},{4,6},{3,1},{5,3},{7,5},{8,10},{10,12},{12,14},{11,9},... | collective-permute-start | bytes 786440 | tf_op jit(solution)/shard_map/ppermute | solution.py:156
  55.5 4.4 %collective-permute-start.13 = (f32[2,128,256]{2,1,0:T(8,128)S(1)}, f32[2,128,256]{2,1,0:T(8,128)S(1)}, u32[]{:S(2)}, u32[]{:S(2)}) collective-permute-start(f32[2,128,256]{2,1,0:T(8,128)S(1)} %collective-permute-done.9.refs_8_), channel_id=1, source_target_pairs={{0,2},{2,4},{4,6},{3,1},{5,3},{7,5},{8,10},{10,12},{12,14},{11,9},... | collective-permute-start | bytes 786440 | tf_op jit(solution)/shard_map/ppermute | solution.py:156
  59.9 5.4 %collective-permute-done.13.refs_12_ = f32[2,128,256]{2,1,0:T(8,128)S(1)} collective-permute-done((f32[2,128,256]{2,1,0:T(8,128)S(1)}, f32[2,128,256]{2,1,0:T(8,128)S(1)}, u32[]{:S(2)}, u32[]{:S(2)}) %collective-permute-start.13) | collective-permute-done | bytes 262176 | tf_op jit(solution)/shard_map/ppermute | solution.py:156
  65.3 4.1 %shard_map.79 = (f32[256,128]{1,0:T(8,128)S(1)}, f32[8,128,128]{2,1,0:T(8,128)S(1)}) custom-call(s32[8,8]{1,0:T(8,128)S(1)} %fusion.refs_0_.slots, f32[2,128,256]{2,1,0:T(8,128)S(1)} %get-tuple-element.40.refs_1_, f32[2,128,256]{2,1,0:T(8,128)S(1)} %get-tuple-element.41.refs_2_, f32[2,128,256]{2,1,0:T(8,128)S(1)} %get-tuple-element.42.refs_3_, ...), custom_call_target="tpu_custom_call" | custom-call | flops 6600000000 | tf_op jit(solution)/shard_map/pallas_call | solution.py:389
  69.4 1.8 %collective-permute-start.17 = (f32[256,128]{1,0:T(8,128)S(1)}, f32[256,128]{1,0:T(8,128)S(1)}, u32[]{:S(2)}, u32[]{:S(2)}) collective-permute-start(f32[256,128]{1,0:T(8,128)S(1)} %get-tuple-element.45.refs_0_.own_f), channel_id=1, source_target_pairs={{0,1},{1,0},{2,3},{3,2},{4,5},{5,4},{6,7},{7,6},{8,9},{9,8},{10,11... | collective-permute-start | bytes 393224 | tf_op jit(solution)/shard_map/ppermute | solution.py:150
  71.2 1.5 %collective-permute-start.15 = (f32[256,128]{1,0:T(8,128)S(1)}, f32[256,128]{1,0:T(8,128)S(1)}, u32[]{:S(2)}, u32[]{:S(2)}) collective-permute-start(f32[256,128]{1,0:T(8,128)S(1)} %get-tuple-element.45.refs_0_.own_f), channel_id=1, source_target_pairs={{16,0},{24,8},{0,16},{8,24},{17,1},{25,9},{1,17},{9,25},{18,2},{26... | collective-permute-start | bytes 393224 | tf_op jit(solution)/shard_map/ppermute | solution.py:184
  73.0 1.4 %collective-permute-done.17.first_f = f32[256,128]{1,0:T(8,128)S(1)} collective-permute-done((f32[256,128]{1,0:T(8,128)S(1)}, f32[256,128]{1,0:T(8,128)S(1)}, u32[]{:S(2)}, u32[]{:S(2)}) %collective-permute-start.17) | collective-permute-done | bytes 131104 | tf_op jit(solution)/shard_map/ppermute | solution.py:150
  74.4 4.6 %collective-permute-start.18 = (f32[256,128]{1,0:T(8,128)S(1)}, f32[256,128]{1,0:T(8,128)S(1)}, u32[]{:S(2)}, u32[]{:S(2)}) collective-permute-start(f32[256,128]{1,0:T(8,128)S(1)} %collective-permute-done.17.first_f), channel_id=1, source_target_pairs={{0,2},{2,4},{4,6},{3,1},{5,3},{7,5},{8,10},{10,12},{12,14},{11,9},... | collective-permute-start | bytes 393224 | tf_op jit(solution)/shard_map/ppermute | solution.py:156
  81.3 3.7 %shard_map.81 = f32[288,128]{1,0:T(8,128)S(1)} custom-call(s32[8,8]{1,0:T(8,128)S(1)} %fusion.refs_0_.slots, f32[256,128]{1,0:T(8,128)S(1)} %get-tuple-element.45.refs_0_.own_f, f32[256,128]{1,0:T(8,128)S(1)} %collective-permute-done.17.first_f, f32[256,128]{1,0:T(8,128)S(1)} %collective-permute-done.18.second_f, ...), custom_call_target="tpu_custom_call" | custom-call | flops 4180000000 | tf_op jit(solution)/shard_map/pallas_call | solution.py:463
  85.2 1.3 %collective-permute-done.19 = f32[288,128]{1,0:T(8,128)S(1)} collective-permute-done((f32[288,128]{1,0:T(8,128)S(1)}, f32[288,128]{1,0:T(8,128)S(1)}, u32[]{:S(2)}, u32[]{:S(2)}) %collective-permute-start.19) | collective-permute-done | bytes 147488 | tf_op jit(solution)/shard_map/ppermute | solution.py:172
  86.5 1.7 %collective-permute-start.20 = (f32[136,128]{1,0:T(8,128)S(1)}, f32[136,128]{1,0:T(8,128)S(1)}, u32[]{:S(2)}, u32[]{:S(2)}) collective-permute-start(f32[136,128]{1,0:T(8,128)S(1)} %pad_maximum_fusion.1), channel_id=1, source_target_pairs={{0,1},{1,0},{2,3},{3,2},{4,5},{5,4},{6,7},{7,6},{8,9},{9,8},{10,11... | collective-permute-start | bytes 208904 | tf_op jit(solution)/shard_map/ppermute | solution.py:195
  88.3 1.5 %collective-permute-start.23 = (f32[512,128]{1,0:T(8,128)S(1)}, f32[512,128]{1,0:T(8,128)S(1)}, u32[]{:S(2)}, u32[]{:S(2)}) collective-permute-start(f32[512,128]{1,0:T(8,128)S(1)} %pad_maximum_fusion), channel_id=1, source_target_pairs={{0,16},{8,24},{16,0},{24,8},{1,17},{9,25},{17,1},{25,9},{2,18},{10... | collective-permute-start | bytes 786440 | tf_op jit(solution)/shard_map/ppermute | solution.py:172
  90.9 2.5 %collective-permute-start.21 = (f32[136,128]{1,0:T(8,128)S(1)}, f32[136,128]{1,0:T(8,128)S(1)}, u32[]{:S(2)}, u32[]{:S(2)}) collective-permute-start(f32[136,128]{1,0:T(8,128)S(1)} %fusion.3), channel_id=1, source_target_pairs={{0,2},{1,3},{2,0},{3,1},{4,6},{5,7},{6,4},{7,5},{8,10},{9,11},{10,... | collective-permute-start | bytes 208904 | tf_op jit(solution)/shard_map/ppermute | solution.py:195
  93.4 2.3 %collective-permute-done.21 = f32[136,128]{1,0:T(8,128)S(1)} collective-permute-done((f32[136,128]{1,0:T(8,128)S(1)}, f32[136,128]{1,0:T(8,128)S(1)}, u32[]{:S(2)}, u32[]{:S(2)}) %collective-permute-start.21) | collective-permute-done | bytes 69664 | tf_op jit(solution)/shard_map/ppermute | solution.py:195
  95.7 3.1 %collective-permute-start.22 = (f32[136,128]{1,0:T(8,128)S(1)}, f32[136,128]{1,0:T(8,128)S(1)}, u32[]{:S(2)}, u32[]{:S(2)}) collective-permute-start(f32[136,128]{1,0:T(8,128)S(1)} %add.36), channel_id=1, source_target_pairs={{0,4},{1,5},{2,6},{3,7},{4,0},{5,1},{6,2},{7,3},{8,12},{9,13},{10,... | collective-permute-start | bytes 208904 | tf_op jit(solution)/shard_map/ppermute | solution.py:195
  98.9 2.3 %collective-permute-done.22 = f32[136,128]{1,0:T(8,128)S(1)} collective-permute-done((f32[136,128]{1,0:T(8,128)S(1)}, f32[136,128]{1,0:T(8,128)S(1)}, u32[]{:S(2)}, u32[]{:S(2)}) %collective-permute-start.22) | collective-permute-done | bytes 69664 | tf_op jit(solution)/shard_map/ppermute | solution.py:195
  101.2 1.5 %collective-permute-start.24 = (f32[64,128]{1,0:T(8,128)S(1)}, f32[64,128]{1,0:T(8,128)S(1)}, u32[]{:S(2)}, u32[]{:S(2)}) collective-permute-start(f32[64,128]{1,0:T(8,128)S(1)} %slice.50), channel_id=1, source_target_pairs={{0,16},{8,24},{16,0},{24,8},{1,17},{9,25},{17,1},{25,9},{2,18},{10... | collective-permute-start | bytes 98312 | tf_op jit(solution)/shard_map/ppermute | solution.py:172
  102.8 6.2 %shard_map.82 = (f32[128,128]{1,0:T(8,128)S(1)}, f32[1024,128]{1,0:T(8,128)}, f32[1024,128]{1,0:T(8,128)}) custom-call(f32[136,128]{1,0:T(8,128)S(1)} %add.37.refs_0_, f32[1024,128]{1,0:T(8,128)S(1)} %get-tuple-element.47.full_ref.refs_1_, f32[256,128]{1,0:T(8,128)S(1)} %slice.46.refs_2_, f32[256,128]{1,0:T(8,128)S(1)} %slice.47.refs_3_, ...), custom_call_target="tpu_custom_call" | custom-call | flops 550000000 | tf_op jit(solution)/shard_map/pallas_call | solution.py:524
  (49 shorter events, 11.0 us)
Async XLA Ops:
  1.6 9.3 %collective-permute-start = (f32[512,128]{1,0:T(8,128)S(1)}, f32[512,128]{1,0:T(8,128)S(1)}, u32[]{:S(2)}, u32[]{:S(2)}) collective-permute-start(f32[512,128]{1,0:T(8,128)S(1)} %bitcast.1), channel_id=1, source_target_pairs={{0,1},{1,0},{2,3},{3,2},{4,5},{5,4},{6,7},{7,6},{8,9},{9,8},{10,11... | collective-permute-start | bytes 786440 | tf_op jit(solution)/shard_map/ppermute | solution.py:150
  4.7 0.7 copy-start
  5.3 18.1 %copy-start.3 = (s32[8,8]{1,0:T(8,128)S(1)}, s32[8,8]{1,0:T(8,128)}, u32[]{:S(2)}) copy-start(s32[8,8]{1,0:T(8,128)} %param.5) | copy-start | bytes 772
  5.3 18.2 %copy-start.1 = (f32[8,128]{1,0:T(8,128)S(1)}, f32[8,128]{1,0:T(8,128)}, u32[]{:S(2)}) copy-start(f32[8,128]{1,0:T(8,128)} %refs_19_.1) | copy-start | bytes 12292
  11.0 5.2 %collective-permute-start.1 = (f32[264,128]{1,0:T(8,128)S(1)}, f32[264,128]{1,0:T(8,128)S(1)}, u32[]{:S(2)}, u32[]{:S(2)}) collective-permute-start(f32[264,128]{1,0:T(8,128)S(1)} %get-tuple-element.32), channel_id=1, source_target_pairs={{0,1},{1,0},{2,3},{3,2},{4,5},{5,4},{6,7},{7,6},{8,9},{9,8},{10,11... | collective-permute-start | bytes 405512 | tf_op jit(solution)/shard_map/ppermute | solution.py:150
  12.7 9.3 %collective-permute-start.4 = (f32[512,128]{1,0:T(8,128)S(1)}, f32[512,128]{1,0:T(8,128)S(1)}, u32[]{:S(2)}, u32[]{:S(2)}) collective-permute-start(f32[512,128]{1,0:T(8,128)S(1)} %collective-permute-done.refs_4_), channel_id=1, source_target_pairs={{0,2},{2,4},{4,6},{3,1},{5,3},{7,5},{8,10},{10,12},{12,14},{11,9},... | collective-permute-start | bytes 786440 | tf_op jit(solution)/shard_map/ppermute | solution.py:156
  16.2 7.3 %collective-permute-start.3 = (f32[264,128]{1,0:T(8,128)S(1)}, f32[264,128]{1,0:T(8,128)S(1)}, u32[]{:S(2)}, u32[]{:S(2)}) collective-permute-start(f32[264,128]{1,0:T(8,128)S(1)} %collective-permute-done.1.refs_3_), channel_id=1, source_target_pairs={{0,2},{2,4},{4,6},{3,1},{5,3},{7,5},{8,10},{10,12},{12,14},{11,9},... | collective-permute-start | bytes 405512 | tf_op jit(solution)/shard_map/ppermute | solution.py:156
  19.7 3.8 %collective-permute-start.2 = (f32[512,128]{1,0:T(8,128)S(1)}, f32[512,128]{1,0:T(8,128)S(1)}, u32[]{:S(2)}, u32[]{:S(2)}) collective-permute-start(f32[512,128]{1,0:T(8,128)S(1)} %collective-permute-done.refs_4_), channel_id=1, source_target_pairs={{0,8},{8,0},{16,24},{24,16},{1,9},{9,1},{17,25},{25,17},{2,10},{10... | collective-permute-start | bytes 786440 | tf_op jit(solution)/shard_map/ppermute | solution.py:168
  19.8 5.3 %copy-start.2 = (bf16[8,256,1024]{2,1,0:T(8,128)(2,1)S(1)}, bf16[8,256,1024]{2,1,0:T(8,128)(2,1)}, u32[]{:S(2)}) copy-start(bf16[8,256,1024]{2,1,0:T(8,128)(2,1)} %get-tuple-element.36.refs_3_.refs_14_.c) | copy-start | bytes 12582916
  23.5 1.6 %collective-permute-start.5 = (f32[512,128]{1,0:T(8,128)S(1)}, f32[512,128]{1,0:T(8,128)S(1)}, u32[]{:S(2)}, u32[]{:S(2)}) collective-permute-start(f32[512,128]{1,0:T(8,128)S(1)} %collective-permute-done.4.refs_9_), channel_id=1, source_target_pairs={{0,8},{8,0},{16,24},{24,16},{1,9},{9,1},{17,25},{25,17},{2,10},{10... | collective-permute-start | bytes 786440 | tf_op jit(solution)/shard_map/ppermute | solution.py:168
  29.9 9.2 %collective-permute-start.6 = (f32[2,128,256]{2,1,0:T(8,128)S(1)}, f32[2,128,256]{2,1,0:T(8,128)S(1)}, u32[]{:S(2)}, u32[]{:S(2)}) collective-permute-start(f32[2,128,256]{2,1,0:T(8,128)S(1)} %get-tuple-element.40.refs_1_), channel_id=1, source_target_pairs={{0,1},{1,0},{2,3},{3,2},{4,5},{5,4},{6,7},{7,6},{8,9},{9,8},{10,11... | collective-permute-start | bytes 786440 | tf_op jit(solution)/shard_map/ppermute | solution.py:150
  31.6 13.0 %collective-permute-start.7 = (f32[2,128,256]{2,1,0:T(8,128)S(1)}, f32[2,128,256]{2,1,0:T(8,128)S(1)}, u32[]{:S(2)}, u32[]{:S(2)}) collective-permute-start(f32[2,128,256]{2,1,0:T(8,128)S(1)} %get-tuple-element.41.refs_2_), channel_id=1, source_target_pairs={{0,1},{1,0},{2,3},{3,2},{4,5},{5,4},{6,7},{7,6},{8,9},{9,8},{10,11... | collective-permute-start | bytes 786440 | tf_op jit(solution)/shard_map/ppermute | solution.py:150
  31.9 18.3 %collective-permute-start.8 = (f32[2,128,256]{2,1,0:T(8,128)S(1)}, f32[2,128,256]{2,1,0:T(8,128)S(1)}, u32[]{:S(2)}, u32[]{:S(2)}) collective-permute-start(f32[2,128,256]{2,1,0:T(8,128)S(1)} %get-tuple-element.42.refs_3_), channel_id=1, source_target_pairs={{0,1},{1,0},{2,3},{3,2},{4,5},{5,4},{6,7},{7,6},{8,9},{9,8},{10,11... | collective-permute-start | bytes 786440 | tf_op jit(solution)/shard_map/ppermute | solution.py:150
  33.7 21.8 %collective-permute-start.9 = (f32[2,128,256]{2,1,0:T(8,128)S(1)}, f32[2,128,256]{2,1,0:T(8,128)S(1)}, u32[]{:S(2)}, u32[]{:S(2)}) collective-permute-start(f32[2,128,256]{2,1,0:T(8,128)S(1)} %get-tuple-element.43.refs_4_), channel_id=1, source_target_pairs={{0,1},{1,0},{2,3},{3,2},{4,5},{5,4},{6,7},{7,6},{8,9},{9,8},{10,11... | collective-permute-start | bytes 786440 | tf_op jit(solution)/shard_map/ppermute | solution.py:150
  39.0 20.9 %collective-permute-start.10 = (f32[2,128,256]{2,1,0:T(8,128)S(1)}, f32[2,128,256]{2,1,0:T(8,128)S(1)}, u32[]{:S(2)}, u32[]{:S(2)}) collective-permute-start(f32[2,128,256]{2,1,0:T(8,128)S(1)} %collective-permute-done.6.refs_5_), channel_id=1, source_target_pairs={{0,2},{2,4},{4,6},{3,1},{5,3},{7,5},{8,10},{10,12},{12,14},{11,9},... | collective-permute-start | bytes 786440 | tf_op jit(solution)/shard_map/ppermute | solution.py:156
  44.6 15.3 %collective-permute-start.11 = (f32[2,128,256]{2,1,0:T(8,128)S(1)}, f32[2,128,256]{2,1,0:T(8,128)S(1)}, u32[]{:S(2)}, u32[]{:S(2)}) collective-permute-start(f32[2,128,256]{2,1,0:T(8,128)S(1)} %collective-permute-done.7.refs_6_), channel_id=1, source_target_pairs={{0,2},{2,4},{4,6},{3,1},{5,3},{7,5},{8,10},{10,12},{12,14},{11,9},... | collective-permute-start | bytes 786440 | tf_op jit(solution)/shard_map/ppermute | solution.py:156
  50.3 9.7 %collective-permute-start.12 = (f32[2,128,256]{2,1,0:T(8,128)S(1)}, f32[2,128,256]{2,1,0:T(8,128)S(1)}, u32[]{:S(2)}, u32[]{:S(2)}) collective-permute-start(f32[2,128,256]{2,1,0:T(8,128)S(1)} %collective-permute-done.8.refs_7_), channel_id=1, source_target_pairs={{0,2},{2,4},{4,6},{3,1},{5,3},{7,5},{8,10},{10,12},{12,14},{11,9},... | collective-permute-start | bytes 786440 | tf_op jit(solution)/shard_map/ppermute | solution.py:156
  55.5 9.8 %collective-permute-start.13 = (f32[2,128,256]{2,1,0:T(8,128)S(1)}, f32[2,128,256]{2,1,0:T(8,128)S(1)}, u32[]{:S(2)}, u32[]{:S(2)}) collective-permute-start(f32[2,128,256]{2,1,0:T(8,128)S(1)} %collective-permute-done.9.refs_8_), channel_id=1, source_target_pairs={{0,2},{2,4},{4,6},{3,1},{5,3},{7,5},{8,10},{10,12},{12,14},{11,9},... | collective-permute-start | bytes 786440 | tf_op jit(solution)/shard_map/ppermute | solution.py:156
  69.4 5.0 %collective-permute-start.17 = (f32[256,128]{1,0:T(8,128)S(1)}, f32[256,128]{1,0:T(8,128)S(1)}, u32[]{:S(2)}, u32[]{:S(2)}) collective-permute-start(f32[256,128]{1,0:T(8,128)S(1)} %get-tuple-element.45.refs_0_.own_f), channel_id=1, source_target_pairs={{0,1},{1,0},{2,3},{3,2},{4,5},{5,4},{6,7},{7,6},{8,9},{9,8},{10,11... | collective-permute-start | bytes 393224 | tf_op jit(solution)/shard_map/ppermute | solution.py:150
  71.2 7.8 %collective-permute-start.16 = (f32[256,128]{1,0:T(8,128)S(1)}, f32[256,128]{1,0:T(8,128)S(1)}, u32[]{:S(2)}, u32[]{:S(2)}) collective-permute-start(f32[256,128]{1,0:T(8,128)S(1)} %get-tuple-element.45.refs_0_.own_f), channel_id=1, source_target_pairs={{24,0},{16,8},{8,16},{0,24},{25,1},{17,9},{9,17},{1,25},{26,2},{18... | collective-permute-start | bytes 393224 | tf_op jit(solution)/shard_map/ppermute | solution.py:184
  71.2 8.6 %collective-permute-start.15 = (f32[256,128]{1,0:T(8,128)S(1)}, f32[256,128]{1,0:T(8,128)S(1)}, u32[]{:S(2)}, u32[]{:S(2)}) collective-permute-start(f32[256,128]{1,0:T(8,128)S(1)} %get-tuple-element.45.refs_0_.own_f), channel_id=1, source_target_pairs={{16,0},{24,8},{0,16},{8,24},{17,1},{25,9},{1,17},{9,25},{18,2},{26... | collective-permute-start | bytes 393224 | tf_op jit(solution)/shard_map/ppermute | solution.py:184
  72.7 7.1 %collective-permute-start.14 = (f32[256,128]{1,0:T(8,128)S(1)}, f32[256,128]{1,0:T(8,128)S(1)}, u32[]{:S(2)}, u32[]{:S(2)}) collective-permute-start(f32[256,128]{1,0:T(8,128)S(1)} %get-tuple-element.45.refs_0_.own_f), channel_id=1, source_target_pairs={{8,0},{0,8},{24,16},{16,24},{9,1},{1,9},{25,17},{17,25},{10,2},{2,... | collective-permute-start | bytes 393224 | tf_op jit(solution)/shard_map/ppermute | solution.py:184
  74.4 6.9 %collective-permute-start.18 = (f32[256,128]{1,0:T(8,128)S(1)}, f32[256,128]{1,0:T(8,128)S(1)}, u32[]{:S(2)}, u32[]{:S(2)}) collective-permute-start(f32[256,128]{1,0:T(8,128)S(1)} %collective-permute-done.17.first_f), channel_id=1, source_target_pairs={{0,2},{2,4},{4,6},{3,1},{5,3},{7,5},{8,10},{10,12},{12,14},{11,9},... | collective-permute-start | bytes 393224 | tf_op jit(solution)/shard_map/ppermute | solution.py:156
  85.1 1.4 %collective-permute-start.19 = (f32[288,128]{1,0:T(8,128)S(1)}, f32[288,128]{1,0:T(8,128)S(1)}, u32[]{:S(2)}, u32[]{:S(2)}) collective-permute-start(f32[288,128]{1,0:T(8,128)S(1)} %shard_map.81), channel_id=1, source_target_pairs={{0,8},{8,0},{16,24},{24,16},{1,9},{9,1},{17,25},{25,17},{2,10},{10... | collective-permute-start | bytes 442376 | tf_op jit(solution)/shard_map/ppermute | solution.py:172
  86.5 4.4 %collective-permute-start.20 = (f32[136,128]{1,0:T(8,128)S(1)}, f32[136,128]{1,0:T(8,128)S(1)}, u32[]{:S(2)}, u32[]{:S(2)}) collective-permute-start(f32[136,128]{1,0:T(8,128)S(1)} %pad_maximum_fusion.1), channel_id=1, source_target_pairs={{0,1},{1,0},{2,3},{3,2},{4,5},{5,4},{6,7},{7,6},{8,9},{9,8},{10,11... | collective-permute-start | bytes 208904 | tf_op jit(solution)/shard_map/ppermute | solution.py:195
  88.3 12.9 %collective-permute-start.23 = (f32[512,128]{1,0:T(8,128)S(1)}, f32[512,128]{1,0:T(8,128)S(1)}, u32[]{:S(2)}, u32[]{:S(2)}) collective-permute-start(f32[512,128]{1,0:T(8,128)S(1)} %pad_maximum_fusion), channel_id=1, source_target_pairs={{0,16},{8,24},{16,0},{24,8},{1,17},{9,25},{17,1},{25,9},{2,18},{10... | collective-permute-start | bytes 786440 | tf_op jit(solution)/shard_map/ppermute | solution.py:172
  90.9 4.8 %collective-permute-start.21 = (f32[136,128]{1,0:T(8,128)S(1)}, f32[136,128]{1,0:T(8,128)S(1)}, u32[]{:S(2)}, u32[]{:S(2)}) collective-permute-start(f32[136,128]{1,0:T(8,128)S(1)} %fusion.3), channel_id=1, source_target_pairs={{0,2},{1,3},{2,0},{3,1},{4,6},{5,7},{6,4},{7,5},{8,10},{9,11},{10,... | collective-permute-start | bytes 208904 | tf_op jit(solution)/shard_map/ppermute | solution.py:195
  95.7 5.4 %collective-permute-start.22 = (f32[136,128]{1,0:T(8,128)S(1)}, f32[136,128]{1,0:T(8,128)S(1)}, u32[]{:S(2)}, u32[]{:S(2)}) collective-permute-start(f32[136,128]{1,0:T(8,128)S(1)} %add.36), channel_id=1, source_target_pairs={{0,4},{1,5},{2,6},{3,7},{4,0},{5,1},{6,2},{7,3},{8,12},{9,13},{10,... | collective-permute-start | bytes 208904 | tf_op jit(solution)/shard_map/ppermute | solution.py:195
  101.2 7.8 %collective-permute-start.24 = (f32[64,128]{1,0:T(8,128)S(1)}, f32[64,128]{1,0:T(8,128)S(1)}, u32[]{:S(2)}, u32[]{:S(2)}) collective-permute-start(f32[64,128]{1,0:T(8,128)S(1)} %slice.50), channel_id=1, source_target_pairs={{0,16},{8,24},{16,0},{24,8},{1,17},{9,25},{17,1},{25,9},{2,18},{10... | collective-permute-start | bytes 98312 | tf_op jit(solution)/shard_map/ppermute | solution.py:172

commit v5 on v4

--- a/solution.py
+++ b/solution.py
@@ -36,8 +36,10 @@
     return both[:half] + both[half:] + dot(stacked[:half], low)
 
 
-def apply_three(stacked, value):
-    return dot_three(stacked, *split(value))
+def apply_wide(beside, value):
+    high, low = split(value)
+    depth = beside.shape[1] // 2
+    return dot(beside, jnp.concatenate([high, high], axis=0)) + dot(beside[:, :depth], low)
 
 
 def exact(left, right, contract):
@@ -229,11 +231,11 @@
         backward, rights = [], []
         for i in blocks:
             v = vec[i]
-            backward.append(jnp.concatenate(split(v.T), axis=0))
-            vec_st[i] = jnp.concatenate(split(v), axis=0)
+            backward.append(jnp.concatenate(split(v.T), axis=1))
+            vec_st[i] = jnp.concatenate(split(v), axis=1)
             vec_ts[i] = backward[i]
-            rights.append(split(spread(start[i * blk:(i + 1) * blk, :], mine_now, width)))
-        turned = [dot_three(backward[i], *rights[i]) for i in blocks]
+            rights.append(spread(start[i * blk:(i + 1) * blk, :], mine_now, width))
+        turned = [apply_wide(backward[i], rights[i]) for i in blocks]
         for i in blocks:
             spun[i] = turned[i]
             store_packed(packed, i, turned[i])
@@ -250,8 +252,8 @@
         (
             sds((blk_dev, blk, ncol), F32),
             sds((packs * blk + blk_dev, ncol), F32),
-            sds((blk_dev, 2 * blk, blk), BF16),
-            sds((blk_dev, 2 * blk, blk), BF16),
+            sds((blk_dev, blk, 2 * blk), BF16),
+            sds((blk_dev, blk, 2 * blk), BF16),
             sds((blk_dev, 2 * blk, nnb * blk), BF16),
         ),
         in_specs=[HBM()] * 3 + [VMEM()],
@@ -281,9 +283,9 @@
                 re, im = inverse_scale(column_of(pack[pl.ds(packs * blk + b, 1), :]))
                 vector = inputs[1 + h][j * blk:(j + 1) * blk, :]
                 names.append(b)
-                lefts.append(jnp.concatenate(split(vector), axis=0))
+                lefts.append(jnp.concatenate(split(vector), axis=1))
                 rights.append(jnp.concatenate([re * turned, im * turned], axis=1))
-        fields = [apply_three(left, right) for left, right in zip(lefts, rights)]
+        fields = [apply_wide(left, right) for left, right in zip(lefts, rights)]
         for b, field in zip(names, fields):
             put(xh, xl, b + offset, field)
 
@@ -300,7 +302,7 @@
             scale[i, :, :ncol] = re
             scale[i, :, ncol:] = im
             firsts.append(jnp.concatenate([re * turned, im * turned], axis=1))
-        fields = [apply_three(vec[i], firsts[i]) for i in range(blk_dev)]
+        fields = [apply_wide(vec[i], firsts[i]) for i in range(blk_dev)]
         for i in range(blk_dev):
             put(xh, xl, i, fields[i])
         fill_first(inputs, xh, xl, blk_dev)
@@ -343,10 +345,10 @@
         xl[:2 * rows_here, :] = tl[...]
         blocks = range(blk_dev)
         sums = [coupled(slots, c, xh, xl, i) for i in blocks]
-        turned = [apply_three(vec_t[i], sums[i]) for i in blocks]
+        turned = [apply_wide(vec_t[i], sums[i]) for i in blocks]
         for i in blocks:
             hats[i] = times(scale_ref[i], DAMPING * plus_real(turned[i], (1.0 + KEEP) * spun_ref[i]))
-        result = [apply_three(vec[i], hats[i]) for i in blocks]
+        result = [apply_wide(vec[i], hats[i]) for i in blocks]
         for i in blocks:
             q, j = spots[i]
             outs[q][j] = result[i]
@@ -374,14 +376,14 @@
         weight_im = lane_table(imag_parts / count, (1, ncol), width)
         blocks = range(blk_dev)
         sums = [coupled(slots, c, xh, xl, i) for i in blocks]
-        turned = [apply_three(vec_t[i], sums[i]) for i in blocks]
+        turned = [apply_wide(vec_t[i], sums[i]) for i in blocks]
         ends = []
         for i in blocks:
             hat = KEEP * hats_ref[i] + times(scale_ref[i], DAMPING * plus_real(turned[i], spun_ref[i]))
             term = fold(weight_re * hat[:, :ncol] - weight_im * hat[:, ncol:], width)
             energy = column_of(val[i:i + 1, :])
             ends.append(jnp.concatenate([term, energy * term], axis=1))
-        result = [apply_three(vec[i], ends[i]) for i in blocks]
+        result = [apply_wide(vec[i], ends[i]) for i in blocks]
         for i in blocks:
             diag_out[i] = result[i][:, ncol:]
             store_packed(packed_out, i, result[i][:, :ncol])
@@ -518,8 +520,9 @@
         inv = inverse[...]
         for i in range(blk_dev):
             raw[i * blk:(i + 1) * blk, :] = unpacked(pieces, block_rows(i), i % count)
-        basis_ref[...] = exact(full_ref[...], inv, ((1,), (1,)))
-        image_ref[...] = exact(raw[...], inv, ((1,), (1,)))
+        turned = inv.T
+        basis_ref[...] = apply_wide(jnp.concatenate(split(full_ref[...]), axis=1), turned)
+        image_ref[...] = apply_wide(jnp.concatenate(split(raw[...]), axis=1), turned)
 
     inverse, basis, basis_image = call(
         factor_of,

time: 111 us -> 110 us (level)
  no operation moved by 1% of the time
where the time goes in v5:
time: 110 us
  starting transfers between devices  52.2 us (47%)
  Pallas kernels  27.8 us (25%)
  waiting for transfers between devices  27 us (25%)
  local copies, waits for them, and re-layouts  1.73 us (2%)
    ppermute x7, starting transfers between devices, pass_on(): return lax.ppermute(arrived, 'rows', pairs)  29.1 us
    ppermute x7, starting transfers between devices, swap(): return lax.ppermute(value, 'rows', [(i, i ^ 1) for i in range(nrows)])  10.6 us
    ppermute x7, waiting for transfers between devices, swap(): return lax.ppermute(value, 'rows', [(i, i ^ 1) for i in range(nrows)])  9.91 us
    ppermute x7, waiting for transfers between devices, pass_on(): return lax.ppermute(arrived, 'rows', pairs)  9.4 us
    ppermute x3, starting transfers between devices, sum_rows(): lax.ppermute(value, 'rows', [(i, i ^ step) for i in range(nrows)])  7.32 us
    pallas_call x1, Pallas kernels, per_device(): call(factor_of, (sds((ncol, ncol), F32), sds((rows_here, ncol), F32), sds...  5.94 us
    ppermute x3, waiting for transfers between devices, sum_rows(): lax.ppermute(value, 'rows', [(i, i ^ step) for i in range(nrows)])  5.63 us
    pallas_call x1, Pallas kernels, per_device(): call(prepare, (sds((blk_dev, blk, ncol), F32), sds((packs * blk + blk_dev...  5.45 us
  transfers between devices with their start and end apart: 25, of which 15 were waited for; matrix products, arithmetic and copies ran while one was open for 0% of the time, Pallas kernels for 13%

profile of v5, /device:TPU:0, one launch (start us, length us, event | category | flops | bytes accessed | tf_op | source)
XLA Modules:
  0.0 109.7 jit_solution(12045612457570843165)
XLA Ops:
  1.6 3.0 %collective-permute-start = (f32[512,128]{1,0:T(8,128)S(1)}, f32[512,128]{1,0:T(8,128)S(1)}, u32[]{:S(2)}, u32[]{:S(2)}) collective-permute-start(f32[512,128]{1,0:T(8,128)S(1)} %bitcast.1), channel_id=1, source_target_pairs={{0,1},{1,0},{2,3},{3,2},{4,5},{5,4},{6,7},{7,6},{8,9},{9,8},{10,11... | collective-permute-start | bytes 786440 | tf_op jit(solution)/shard_map/ppermute | solution.py:152
  5.3 5.4 %shard_map.76 = (f32[8,128,128]{2,1,0:T(8,128)S(1)}, f32[264,128]{1,0:T(8,128)S(1)}, bf16[8,128,256]{2,1,0:T(8,128)(2,1)S(1)}, bf16[8,128,256]{2,1,0:T(8,128)(2,1)S(1)}, bf16[8,256,1024]{2,1,0:T(8,128)(2,1)}) custom-call(f32[1024,128]{1,0:T(8,128)} %start_hbm.1, f32[8,128,128]{2,1,0:T(8,128)} %vec_hbm.1, f32[8,8,128,128]{3,2,1,0:T(8,128)} %coup_hbm.1, ...), custom_call_target="tpu_custom_call" | custom-call | flops 22000001024 | tf_op jit(solution)/shard_map/pallas_call | solution.py:250
  11.0 1.7 %collective-permute-start.1 = (f32[264,128]{1,0:T(8,128)S(1)}, f32[264,128]{1,0:T(8,128)S(1)}, u32[]{:S(2)}, u32[]{:S(2)}) collective-permute-start(f32[264,128]{1,0:T(8,128)S(1)} %get-tuple-element.32), channel_id=1, source_target_pairs={{0,1},{1,0},{2,3},{3,2},{4,5},{5,4},{6,7},{7,6},{8,9},{9,8},{10,11... | collective-permute-start | bytes 405512 | tf_op jit(solution)/shard_map/ppermute | solution.py:152
  12.7 3.5 %collective-permute-start.4 = (f32[512,128]{1,0:T(8,128)S(1)}, f32[512,128]{1,0:T(8,128)S(1)}, u32[]{:S(2)}, u32[]{:S(2)}) collective-permute-start(f32[512,128]{1,0:T(8,128)S(1)} %collective-permute-done.refs_4_), channel_id=1, source_target_pairs={{0,2},{2,4},{4,6},{3,1},{5,3},{7,5},{8,10},{10,12},{12,14},{11,9},... | collective-permute-start | bytes 786440 | tf_op jit(solution)/shard_map/ppermute | solution.py:158
  16.2 3.5 %collective-permute-start.3 = (f32[264,128]{1,0:T(8,128)S(1)}, f32[264,128]{1,0:T(8,128)S(1)}, u32[]{:S(2)}, u32[]{:S(2)}) collective-permute-start(f32[264,128]{1,0:T(8,128)S(1)} %collective-permute-done.1.refs_3_), channel_id=1, source_target_pairs={{0,2},{2,4},{4,6},{3,1},{5,3},{7,5},{8,10},{10,12},{12,14},{11,9},... | collective-permute-start | bytes 405512 | tf_op jit(solution)/shard_map/ppermute | solution.py:158
  19.8 2.2 %collective-permute-done.4.refs_9_ = f32[512,128]{1,0:T(8,128)S(1)} collective-permute-done((f32[512,128]{1,0:T(8,128)S(1)}, f32[512,128]{1,0:T(8,128)S(1)}, u32[]{:S(2)}, u32[]{:S(2)}) %collective-permute-start.4) | collective-permute-done | bytes 262176 | tf_op jit(solution)/shard_map/ppermute | solution.py:158
  22.0 1.4 %collective-permute-done.3.refs_8_ = f32[264,128]{1,0:T(8,128)S(1)} collective-permute-done((f32[264,128]{1,0:T(8,128)S(1)}, f32[264,128]{1,0:T(8,128)S(1)}, u32[]{:S(2)}, u32[]{:S(2)}) %collective-permute-start.3) | collective-permute-done | bytes 135200 | tf_op jit(solution)/shard_map/ppermute | solution.py:158
  23.5 1.7 %shard_map.77 = (bf16[2048,256]{1,0:T(8,128)(2,1)S(1)}, bf16[2048,256]{1,0:T(8,128)(2,1)S(1)}, f32[8,128,256]{2,1,0:T(8,128)S(1)}) custom-call(f32[8,128,128]{2,1,0:T(8,128)S(1)} %get-tuple-element.28.refs_0_.refs_6_.refs_17_, f32[8,128]{1,0:T(8,128)S(1)} %copy-done.1, bf16[8,128,256]{2,1,0:T(8,128)(2,1)S(1)} %get-tuple-element.29.refs_2_.refs_4_.refs_15_, ...), custom_call_target="tpu_custom_call" | custom-call | flops 2200000000 | tf_op jit(solution)/shard_map/pallas_call | solution.py:311
  25.2 4.6 %shard_map.78 = (f32[2,128,256]{2,1,0:T(8,128)S(1)}, f32[2,128,256]{2,1,0:T(8,128)S(1)}, f32[2,128,256]{2,1,0:T(8,128)S(1)}, f32[2,128,256]{2,1,0:T(8,128)S(1)}, f32[8,128,256]{2,1,0:T(8,128)S(1)}) custom-call(s32[8,8]{1,0:T(8,128)S(1)} %fusion.refs_0_.slots, bf16[2048,256]{1,0:T(8,128)(2,1)S(1)} %get-tuple-element.34.refs_1_, ...), custom_call_target="tpu_custom_call" | custom-call | flops 6600000000 | tf_op jit(solution)/shard_map/pallas_call | solution.py:357
  29.8 1.8 %collective-permute-start.6 = (f32[2,128,256]{2,1,0:T(8,128)S(1)}, f32[2,128,256]{2,1,0:T(8,128)S(1)}, u32[]{:S(2)}, u32[]{:S(2)}) collective-permute-start(f32[2,128,256]{2,1,0:T(8,128)S(1)} %get-tuple-element.40.refs_1_), channel_id=1, source_target_pairs={{0,1},{1,0},{2,3},{3,2},{4,5},{5,4},{6,7},{7,6},{8,9},{9,8},{10,11... | collective-permute-start | bytes 786440 | tf_op jit(solution)/shard_map/ppermute | solution.py:152
  31.9 1.7 %collective-permute-start.8 = (f32[2,128,256]{2,1,0:T(8,128)S(1)}, f32[2,128,256]{2,1,0:T(8,128)S(1)}, u32[]{:S(2)}, u32[]{:S(2)}) collective-permute-start(f32[2,128,256]{2,1,0:T(8,128)S(1)} %get-tuple-element.42.refs_3_), channel_id=1, source_target_pairs={{0,1},{1,0},{2,3},{3,2},{4,5},{5,4},{6,7},{7,6},{8,9},{9,8},{10,11... | collective-permute-start | bytes 786440 | tf_op jit(solution)/shard_map/ppermute | solution.py:152
  33.9 5.0 %collective-permute-done.6.refs_5_ = f32[2,128,256]{2,1,0:T(8,128)S(1)} collective-permute-done((f32[2,128,256]{2,1,0:T(8,128)S(1)}, f32[2,128,256]{2,1,0:T(8,128)S(1)}, u32[]{:S(2)}, u32[]{:S(2)}) %collective-permute-start.6) | collective-permute-done | bytes 262176 | tf_op jit(solution)/shard_map/ppermute | solution.py:152
  38.9 4.4 %collective-permute-start.10 = (f32[2,128,256]{2,1,0:T(8,128)S(1)}, f32[2,128,256]{2,1,0:T(8,128)S(1)}, u32[]{:S(2)}, u32[]{:S(2)}) collective-permute-start(f32[2,128,256]{2,1,0:T(8,128)S(1)} %collective-permute-done.6.refs_5_), channel_id=1, source_target_pairs={{0,2},{2,4},{4,6},{3,1},{5,3},{7,5},{8,10},{10,12},{12,14},{11,9},... | collective-permute-start | bytes 786440 | tf_op jit(solution)/shard_map/ppermute | solution.py:158
  44.5 4.4 %collective-permute-start.11 = (f32[2,128,256]{2,1,0:T(8,128)S(1)}, f32[2,128,256]{2,1,0:T(8,128)S(1)}, u32[]{:S(2)}, u32[]{:S(2)}) collective-permute-start(f32[2,128,256]{2,1,0:T(8,128)S(1)} %collective-permute-done.7.refs_6_), channel_id=1, source_target_pairs={{0,2},{2,4},{4,6},{3,1},{5,3},{7,5},{8,10},{10,12},{12,14},{11,9},... | collective-permute-start | bytes 786440 | tf_op jit(solution)/shard_map/ppermute | solution.py:158
  50.2 4.4 %collective-permute-start.12 = (f32[2,128,256]{2,1,0:T(8,128)S(1)}, f32[2,128,256]{2,1,0:T(8,128)S(1)}, u32[]{:S(2)}, u32[]{:S(2)}) collective-permute-start(f32[2,128,256]{2,1,0:T(8,128)S(1)} %collective-permute-done.8.refs_7_), channel_id=1, source_target_pairs={{0,2},{2,4},{4,6},{3,1},{5,3},{7,5},{8,10},{10,12},{12,14},{11,9},... | collective-permute-start | bytes 786440 | tf_op jit(solution)/shard_map/ppermute | solution.py:158
  55.4 4.4 %collective-permute-start.13 = (f32[2,128,256]{2,1,0:T(8,128)S(1)}, f32[2,128,256]{2,1,0:T(8,128)S(1)}, u32[]{:S(2)}, u32[]{:S(2)}) collective-permute-start(f32[2,128,256]{2,1,0:T(8,128)S(1)} %collective-permute-done.9.refs_8_), channel_id=1, source_target_pairs={{0,2},{2,4},{4,6},{3,1},{5,3},{7,5},{8,10},{10,12},{12,14},{11,9},... | collective-permute-start | bytes 786440 | tf_op jit(solution)/shard_map/ppermute | solution.py:158
  59.8 5.4 %collective-permute-done.13.refs_12_ = f32[2,128,256]{2,1,0:T(8,128)S(1)} collective-permute-done((f32[2,128,256]{2,1,0:T(8,128)S(1)}, f32[2,128,256]{2,1,0:T(8,128)S(1)}, u32[]{:S(2)}, u32[]{:S(2)}) %collective-permute-start.13) | collective-permute-done | bytes 262176 | tf_op jit(solution)/shard_map/ppermute | solution.py:158
  65.2 3.9 %shard_map.79 = (f32[256,128]{1,0:T(8,128)S(1)}, f32[8,128,128]{2,1,0:T(8,128)S(1)}) custom-call(s32[8,8]{1,0:T(8,128)S(1)} %fusion.refs_0_.slots, f32[2,128,256]{2,1,0:T(8,128)S(1)} %get-tuple-element.40.refs_1_, f32[2,128,256]{2,1,0:T(8,128)S(1)} %get-tuple-element.41.refs_2_, f32[2,128,256]{2,1,0:T(8,128)S(1)} %get-tuple-element.42.refs_3_, ...), custom_call_target="tpu_custom_call" | custom-call | flops 6600000000 | tf_op jit(solution)/shard_map/pallas_call | solution.py:391
  69.1 1.8 %collective-permute-start.17 = (f32[256,128]{1,0:T(8,128)S(1)}, f32[256,128]{1,0:T(8,128)S(1)}, u32[]{:S(2)}, u32[]{:S(2)}) collective-permute-start(f32[256,128]{1,0:T(8,128)S(1)} %get-tuple-element.45.refs_0_.own_f), channel_id=1, source_target_pairs={{0,1},{1,0},{2,3},{3,2},{4,5},{5,4},{6,7},{7,6},{8,9},{9,8},{10,11... | collective-permute-start | bytes 393224 | tf_op jit(solution)/shard_map/ppermute | solution.py:152
  70.9 1.5 %collective-permute-start.15 = (f32[256,128]{1,0:T(8,128)S(1)}, f32[256,128]{1,0:T(8,128)S(1)}, u32[]{:S(2)}, u32[]{:S(2)}) collective-permute-start(f32[256,128]{1,0:T(8,128)S(1)} %get-tuple-element.45.refs_0_.own_f), channel_id=1, source_target_pairs={{16,0},{24,8},{0,16},{8,24},{17,1},{25,9},{1,17},{9,25},{18,2},{26... | collective-permute-start | bytes 393224 | tf_op jit(solution)/shard_map/ppermute | solution.py:186
  72.8 1.4 %collective-permute-done.17.first_f = f32[256,128]{1,0:T(8,128)S(1)} collective-permute-done((f32[256,128]{1,0:T(8,128)S(1)}, f32[256,128]{1,0:T(8,128)S(1)}, u32[]{:S(2)}, u32[]{:S(2)}) %collective-permute-start.17) | collective-permute-done | bytes 131104 | tf_op jit(solution)/shard_map/ppermute | solution.py:152
  74.2 4.6 %collective-permute-start.18 = (f32[256,128]{1,0:T(8,128)S(1)}, f32[256,128]{1,0:T(8,128)S(1)}, u32[]{:S(2)}, u32[]{:S(2)}) collective-permute-start(f32[256,128]{1,0:T(8,128)S(1)} %collective-permute-done.17.first_f), channel_id=1, source_target_pairs={{0,2},{2,4},{4,6},{3,1},{5,3},{7,5},{8,10},{10,12},{12,14},{11,9},... | collective-permute-start | bytes 393224 | tf_op jit(solution)/shard_map/ppermute | solution.py:158
  81.1 3.7 %shard_map.81 = f32[288,128]{1,0:T(8,128)S(1)} custom-call(s32[8,8]{1,0:T(8,128)S(1)} %fusion.refs_0_.slots, f32[256,128]{1,0:T(8,128)S(1)} %get-tuple-element.45.refs_0_.own_f, f32[256,128]{1,0:T(8,128)S(1)} %collective-permute-done.17.first_f, f32[256,128]{1,0:T(8,128)S(1)} %collective-permute-done.18.second_f, ...), custom_call_target="tpu_custom_call" | custom-call | flops 4180000000 | tf_op jit(solution)/shard_map/pallas_call | solution.py:465
  84.9 1.3 %collective-permute-done.19 = f32[288,128]{1,0:T(8,128)S(1)} collective-permute-done((f32[288,128]{1,0:T(8,128)S(1)}, f32[288,128]{1,0:T(8,128)S(1)}, u32[]{:S(2)}, u32[]{:S(2)}) %collective-permute-start.19) | collective-permute-done | bytes 147488 | tf_op jit(solution)/shard_map/ppermute | solution.py:174
  86.3 1.7 %collective-permute-start.20 = (f32[136,128]{1,0:T(8,128)S(1)}, f32[136,128]{1,0:T(8,128)S(1)}, u32[]{:S(2)}, u32[]{:S(2)}) collective-permute-start(f32[136,128]{1,0:T(8,128)S(1)} %pad_maximum_fusion.1), channel_id=1, source_target_pairs={{0,1},{1,0},{2,3},{3,2},{4,5},{5,4},{6,7},{7,6},{8,9},{9,8},{10,11... | collective-permute-start | bytes 208904 | tf_op jit(solution)/shard_map/ppermute | solution.py:197
  88.0 1.6 %collective-permute-start.23 = (f32[512,128]{1,0:T(8,128)S(1)}, f32[512,128]{1,0:T(8,128)S(1)}, u32[]{:S(2)}, u32[]{:S(2)}) collective-permute-start(f32[512,128]{1,0:T(8,128)S(1)} %pad_maximum_fusion), channel_id=1, source_target_pairs={{0,16},{8,24},{16,0},{24,8},{1,17},{9,25},{17,1},{25,9},{2,18},{10... | collective-permute-start | bytes 786440 | tf_op jit(solution)/shard_map/ppermute | solution.py:174
  90.7 2.5 %collective-permute-start.21 = (f32[136,128]{1,0:T(8,128)S(1)}, f32[136,128]{1,0:T(8,128)S(1)}, u32[]{:S(2)}, u32[]{:S(2)}) collective-permute-start(f32[136,128]{1,0:T(8,128)S(1)} %fusion.3), channel_id=1, source_target_pairs={{0,2},{1,3},{2,0},{3,1},{4,6},{5,7},{6,4},{7,5},{8,10},{9,11},{10,... | collective-permute-start | bytes 208904 | tf_op jit(solution)/shard_map/ppermute | solution.py:197
  93.2 2.3 %collective-permute-done.21 = f32[136,128]{1,0:T(8,128)S(1)} collective-permute-done((f32[136,128]{1,0:T(8,128)S(1)}, f32[136,128]{1,0:T(8,128)S(1)}, u32[]{:S(2)}, u32[]{:S(2)}) %collective-permute-start.21) | collective-permute-done | bytes 69664 | tf_op jit(solution)/shard_map/ppermute | solution.py:197
  95.5 3.1 %collective-permute-start.22 = (f32[136,128]{1,0:T(8,128)S(1)}, f32[136,128]{1,0:T(8,128)S(1)}, u32[]{:S(2)}, u32[]{:S(2)}) collective-permute-start(f32[136,128]{1,0:T(8,128)S(1)} %add.36), channel_id=1, source_target_pairs={{0,4},{1,5},{2,6},{3,7},{4,0},{5,1},{6,2},{7,3},{8,12},{9,13},{10,... | collective-permute-start | bytes 208904 | tf_op jit(solution)/shard_map/ppermute | solution.py:197
  98.5 2.3 %collective-permute-done.22 = f32[136,128]{1,0:T(8,128)S(1)} collective-permute-done((f32[136,128]{1,0:T(8,128)S(1)}, f32[136,128]{1,0:T(8,128)S(1)}, u32[]{:S(2)}, u32[]{:S(2)}) %collective-permute-start.22) | collective-permute-done | bytes 69664 | tf_op jit(solution)/shard_map/ppermute | solution.py:197
  100.9 1.6 %collective-permute-start.24 = (f32[64,128]{1,0:T(8,128)S(1)}, f32[64,128]{1,0:T(8,128)S(1)}, u32[]{:S(2)}, u32[]{:S(2)}) collective-permute-start(f32[64,128]{1,0:T(8,128)S(1)} %slice.50), channel_id=1, source_target_pairs={{0,16},{8,24},{16,0},{24,8},{1,17},{9,25},{17,1},{25,9},{2,18},{10... | collective-permute-start | bytes 98312 | tf_op jit(solution)/shard_map/ppermute | solution.py:174
  102.5 5.9 %shard_map.82 = (f32[128,128]{1,0:T(8,128)S(1)}, f32[1024,128]{1,0:T(8,128)}, f32[1024,128]{1,0:T(8,128)}) custom-call(f32[136,128]{1,0:T(8,128)S(1)} %add.37.refs_0_, f32[1024,128]{1,0:T(8,128)S(1)} %get-tuple-element.47.full_ref.refs_1_, f32[256,128]{1,0:T(8,128)S(1)} %slice.46.refs_2_, f32[256,128]{1,0:T(8,128)S(1)} %slice.47.refs_3_, ...), custom_call_target="tpu_custom_call" | custom-call | flops 550000000 | tf_op jit(solution)/shard_map/pallas_call | solution.py:527
  (49 shorter events, 11.0 us)
Async XLA Ops:
  1.6 9.3 %collective-permute-start = (f32[512,128]{1,0:T(8,128)S(1)}, f32[512,128]{1,0:T(8,128)S(1)}, u32[]{:S(2)}, u32[]{:S(2)}) collective-permute-start(f32[512,128]{1,0:T(8,128)S(1)} %bitcast.1), channel_id=1, source_target_pairs={{0,1},{1,0},{2,3},{3,2},{4,5},{5,4},{6,7},{7,6},{8,9},{9,8},{10,11... | collective-permute-start | bytes 786440 | tf_op jit(solution)/shard_map/ppermute | solution.py:152
  4.7 0.7 copy-start
  5.3 18.1 %copy-start.3 = (s32[8,8]{1,0:T(8,128)S(1)}, s32[8,8]{1,0:T(8,128)}, u32[]{:S(2)}) copy-start(s32[8,8]{1,0:T(8,128)} %param.5) | copy-start | bytes 772
  5.3 18.2 %copy-start.1 = (f32[8,128]{1,0:T(8,128)S(1)}, f32[8,128]{1,0:T(8,128)}, u32[]{:S(2)}) copy-start(f32[8,128]{1,0:T(8,128)} %refs_19_.1) | copy-start | bytes 12292
  11.0 5.2 %collective-permute-start.1 = (f32[264,128]{1,0:T(8,128)S(1)}, f32[264,128]{1,0:T(8,128)S(1)}, u32[]{:S(2)}, u32[]{:S(2)}) collective-permute-start(f32[264,128]{1,0:T(8,128)S(1)} %get-tuple-element.32), channel_id=1, source_target_pairs={{0,1},{1,0},{2,3},{3,2},{4,5},{5,4},{6,7},{7,6},{8,9},{9,8},{10,11... | collective-permute-start | bytes 405512 | tf_op jit(solution)/shard_map/ppermute | solution.py:152
  12.7 9.3 %collective-permute-start.4 = (f32[512,128]{1,0:T(8,128)S(1)}, f32[512,128]{1,0:T(8,128)S(1)}, u32[]{:S(2)}, u32[]{:S(2)}) collective-permute-start(f32[512,128]{1,0:T(8,128)S(1)} %collective-permute-done.refs_4_), channel_id=1, source_target_pairs={{0,2},{2,4},{4,6},{3,1},{5,3},{7,5},{8,10},{10,12},{12,14},{11,9},... | collective-permute-start | bytes 786440 | tf_op jit(solution)/shard_map/ppermute | solution.py:158
  16.2 7.3 %collective-permute-start.3 = (f32[264,128]{1,0:T(8,128)S(1)}, f32[264,128]{1,0:T(8,128)S(1)}, u32[]{:S(2)}, u32[]{:S(2)}) collective-permute-start(f32[264,128]{1,0:T(8,128)S(1)} %collective-permute-done.1.refs_3_), channel_id=1, source_target_pairs={{0,2},{2,4},{4,6},{3,1},{5,3},{7,5},{8,10},{10,12},{12,14},{11,9},... | collective-permute-start | bytes 405512 | tf_op jit(solution)/shard_map/ppermute | solution.py:158
  19.7 3.8 %collective-permute-start.2 = (f32[512,128]{1,0:T(8,128)S(1)}, f32[512,128]{1,0:T(8,128)S(1)}, u32[]{:S(2)}, u32[]{:S(2)}) collective-permute-start(f32[512,128]{1,0:T(8,128)S(1)} %collective-permute-done.refs_4_), channel_id=1, source_target_pairs={{0,8},{8,0},{16,24},{24,16},{1,9},{9,1},{17,25},{25,17},{2,10},{10... | collective-permute-start | bytes 786440 | tf_op jit(solution)/shard_map/ppermute | solution.py:170
  19.8 5.4 %copy-start.2 = (bf16[8,256,1024]{2,1,0:T(8,128)(2,1)S(1)}, bf16[8,256,1024]{2,1,0:T(8,128)(2,1)}, u32[]{:S(2)}) copy-start(bf16[8,256,1024]{2,1,0:T(8,128)(2,1)} %get-tuple-element.36.refs_3_.refs_14_.c) | copy-start | bytes 12582916
  23.5 1.7 %collective-permute-start.5 = (f32[512,128]{1,0:T(8,128)S(1)}, f32[512,128]{1,0:T(8,128)S(1)}, u32[]{:S(2)}, u32[]{:S(2)}) collective-permute-start(f32[512,128]{1,0:T(8,128)S(1)} %collective-permute-done.4.refs_9_), channel_id=1, source_target_pairs={{0,8},{8,0},{16,24},{24,16},{1,9},{9,1},{17,25},{25,17},{2,10},{10... | collective-permute-start | bytes 786440 | tf_op jit(solution)/shard_map/ppermute | solution.py:170
  29.8 9.2 %collective-permute-start.6 = (f32[2,128,256]{2,1,0:T(8,128)S(1)}, f32[2,128,256]{2,1,0:T(8,128)S(1)}, u32[]{:S(2)}, u32[]{:S(2)}) collective-permute-start(f32[2,128,256]{2,1,0:T(8,128)S(1)} %get-tuple-element.40.refs_1_), channel_id=1, source_target_pairs={{0,1},{1,0},{2,3},{3,2},{4,5},{5,4},{6,7},{7,6},{8,9},{9,8},{10,11... | collective-permute-start | bytes 786440 | tf_op jit(solution)/shard_map/ppermute | solution.py:152
  31.5 13.0 %collective-permute-start.7 = (f32[2,128,256]{2,1,0:T(8,128)S(1)}, f32[2,128,256]{2,1,0:T(8,128)S(1)}, u32[]{:S(2)}, u32[]{:S(2)}) collective-permute-start(f32[2,128,256]{2,1,0:T(8,128)S(1)} %get-tuple-element.41.refs_2_), channel_id=1, source_target_pairs={{0,1},{1,0},{2,3},{3,2},{4,5},{5,4},{6,7},{7,6},{8,9},{9,8},{10,11... | collective-permute-start | bytes 786440 | tf_op jit(solution)/shard_map/ppermute | solution.py:152
  31.9 18.3 %collective-permute-start.8 = (f32[2,128,256]{2,1,0:T(8,128)S(1)}, f32[2,128,256]{2,1,0:T(8,128)S(1)}, u32[]{:S(2)}, u32[]{:S(2)}) collective-permute-start(f32[2,128,256]{2,1,0:T(8,128)S(1)} %get-tuple-element.42.refs_3_), channel_id=1, source_target_pairs={{0,1},{1,0},{2,3},{3,2},{4,5},{5,4},{6,7},{7,6},{8,9},{9,8},{10,11... | collective-permute-start | bytes 786440 | tf_op jit(solution)/shard_map/ppermute | solution.py:152
  33.6 21.8 %collective-permute-start.9 = (f32[2,128,256]{2,1,0:T(8,128)S(1)}, f32[2,128,256]{2,1,0:T(8,128)S(1)}, u32[]{:S(2)}, u32[]{:S(2)}) collective-permute-start(f32[2,128,256]{2,1,0:T(8,128)S(1)} %get-tuple-element.43.refs_4_), channel_id=1, source_target_pairs={{0,1},{1,0},{2,3},{3,2},{4,5},{5,4},{6,7},{7,6},{8,9},{9,8},{10,11... | collective-permute-start | bytes 786440 | tf_op jit(solution)/shard_map/ppermute | solution.py:152
  38.9 20.9 %collective-permute-start.10 = (f32[2,128,256]{2,1,0:T(8,128)S(1)}, f32[2,128,256]{2,1,0:T(8,128)S(1)}, u32[]{:S(2)}, u32[]{:S(2)}) collective-permute-start(f32[2,128,256]{2,1,0:T(8,128)S(1)} %collective-permute-done.6.refs_5_), channel_id=1, source_target_pairs={{0,2},{2,4},{4,6},{3,1},{5,3},{7,5},{8,10},{10,12},{12,14},{11,9},... | collective-permute-start | bytes 786440 | tf_op jit(solution)/shard_map/ppermute | solution.py:158
  44.5 15.3 %collective-permute-start.11 = (f32[2,128,256]{2,1,0:T(8,128)S(1)}, f32[2,128,256]{2,1,0:T(8,128)S(1)}, u32[]{:S(2)}, u32[]{:S(2)}) collective-permute-start(f32[2,128,256]{2,1,0:T(8,128)S(1)} %collective-permute-done.7.refs_6_), channel_id=1, source_target_pairs={{0,2},{2,4},{4,6},{3,1},{5,3},{7,5},{8,10},{10,12},{12,14},{11,9},... | collective-permute-start | bytes 786440 | tf_op jit(solution)/shard_map/ppermute | solution.py:158
  50.2 9.7 %collective-permute-start.12 = (f32[2,128,256]{2,1,0:T(8,128)S(1)}, f32[2,128,256]{2,1,0:T(8,128)S(1)}, u32[]{:S(2)}, u32[]{:S(2)}) collective-permute-start(f32[2,128,256]{2,1,0:T(8,128)S(1)} %collective-permute-done.8.refs_7_), channel_id=1, source_target_pairs={{0,2},{2,4},{4,6},{3,1},{5,3},{7,5},{8,10},{10,12},{12,14},{11,9},... | collective-permute-start | bytes 786440 | tf_op jit(solution)/shard_map/ppermute | solution.py:158
  55.4 9.8 %collective-permute-start.13 = (f32[2,128,256]{2,1,0:T(8,128)S(1)}, f32[2,128,256]{2,1,0:T(8,128)S(1)}, u32[]{:S(2)}, u32[]{:S(2)}) collective-permute-start(f32[2,128,256]{2,1,0:T(8,128)S(1)} %collective-permute-done.9.refs_8_), channel_id=1, source_target_pairs={{0,2},{2,4},{4,6},{3,1},{5,3},{7,5},{8,10},{10,12},{12,14},{11,9},... | collective-permute-start | bytes 786440 | tf_op jit(solution)/shard_map/ppermute | solution.py:158
  69.1 5.0 %collective-permute-start.17 = (f32[256,128]{1,0:T(8,128)S(1)}, f32[256,128]{1,0:T(8,128)S(1)}, u32[]{:S(2)}, u32[]{:S(2)}) collective-permute-start(f32[256,128]{1,0:T(8,128)S(1)} %get-tuple-element.45.refs_0_.own_f), channel_id=1, source_target_pairs={{0,1},{1,0},{2,3},{3,2},{4,5},{5,4},{6,7},{7,6},{8,9},{9,8},{10,11... | collective-permute-start | bytes 393224 | tf_op jit(solution)/shard_map/ppermute | solution.py:152
  70.9 7.8 %collective-permute-start.16 = (f32[256,128]{1,0:T(8,128)S(1)}, f32[256,128]{1,0:T(8,128)S(1)}, u32[]{:S(2)}, u32[]{:S(2)}) collective-permute-start(f32[256,128]{1,0:T(8,128)S(1)} %get-tuple-element.45.refs_0_.own_f), channel_id=1, source_target_pairs={{24,0},{16,8},{8,16},{0,24},{25,1},{17,9},{9,17},{1,25},{26,2},{18... | collective-permute-start | bytes 393224 | tf_op jit(solution)/shard_map/ppermute | solution.py:186
  70.9 8.6 %collective-permute-start.15 = (f32[256,128]{1,0:T(8,128)S(1)}, f32[256,128]{1,0:T(8,128)S(1)}, u32[]{:S(2)}, u32[]{:S(2)}) collective-permute-start(f32[256,128]{1,0:T(8,128)S(1)} %get-tuple-element.45.refs_0_.own_f), channel_id=1, source_target_pairs={{16,0},{24,8},{0,16},{8,24},{17,1},{25,9},{1,17},{9,25},{18,2},{26... | collective-permute-start | bytes 393224 | tf_op jit(solution)/shard_map/ppermute | solution.py:186
  72.4 7.1 %collective-permute-start.14 = (f32[256,128]{1,0:T(8,128)S(1)}, f32[256,128]{1,0:T(8,128)S(1)}, u32[]{:S(2)}, u32[]{:S(2)}) collective-permute-start(f32[256,128]{1,0:T(8,128)S(1)} %get-tuple-element.45.refs_0_.own_f), channel_id=1, source_target_pairs={{8,0},{0,8},{24,16},{16,24},{9,1},{1,9},{25,17},{17,25},{10,2},{2,... | collective-permute-start | bytes 393224 | tf_op jit(solution)/shard_map/ppermute | solution.py:186
  74.2 6.9 %collective-permute-start.18 = (f32[256,128]{1,0:T(8,128)S(1)}, f32[256,128]{1,0:T(8,128)S(1)}, u32[]{:S(2)}, u32[]{:S(2)}) collective-permute-start(f32[256,128]{1,0:T(8,128)S(1)} %collective-permute-done.17.first_f), channel_id=1, source_target_pairs={{0,2},{2,4},{4,6},{3,1},{5,3},{7,5},{8,10},{10,12},{12,14},{11,9},... | collective-permute-start | bytes 393224 | tf_op jit(solution)/shard_map/ppermute | solution.py:158
  84.8 1.4 %collective-permute-start.19 = (f32[288,128]{1,0:T(8,128)S(1)}, f32[288,128]{1,0:T(8,128)S(1)}, u32[]{:S(2)}, u32[]{:S(2)}) collective-permute-start(f32[288,128]{1,0:T(8,128)S(1)} %shard_map.81), channel_id=1, source_target_pairs={{0,8},{8,0},{16,24},{24,16},{1,9},{9,1},{17,25},{25,17},{2,10},{10... | collective-permute-start | bytes 442376 | tf_op jit(solution)/shard_map/ppermute | solution.py:174
  86.3 4.4 %collective-permute-start.20 = (f32[136,128]{1,0:T(8,128)S(1)}, f32[136,128]{1,0:T(8,128)S(1)}, u32[]{:S(2)}, u32[]{:S(2)}) collective-permute-start(f32[136,128]{1,0:T(8,128)S(1)} %pad_maximum_fusion.1), channel_id=1, source_target_pairs={{0,1},{1,0},{2,3},{3,2},{4,5},{5,4},{6,7},{7,6},{8,9},{9,8},{10,11... | collective-permute-start | bytes 208904 | tf_op jit(solution)/shard_map/ppermute | solution.py:197
  88.0 12.8 %collective-permute-start.23 = (f32[512,128]{1,0:T(8,128)S(1)}, f32[512,128]{1,0:T(8,128)S(1)}, u32[]{:S(2)}, u32[]{:S(2)}) collective-permute-start(f32[512,128]{1,0:T(8,128)S(1)} %pad_maximum_fusion), channel_id=1, source_target_pairs={{0,16},{8,24},{16,0},{24,8},{1,17},{9,25},{17,1},{25,9},{2,18},{10... | collective-permute-start | bytes 786440 | tf_op jit(solution)/shard_map/ppermute | solution.py:174
  90.7 4.8 %collective-permute-start.21 = (f32[136,128]{1,0:T(8,128)S(1)}, f32[136,128]{1,0:T(8,128)S(1)}, u32[]{:S(2)}, u32[]{:S(2)}) collective-permute-start(f32[136,128]{1,0:T(8,128)S(1)} %fusion.3), channel_id=1, source_target_pairs={{0,2},{1,3},{2,0},{3,1},{4,6},{5,7},{6,4},{7,5},{8,10},{9,11},{10,... | collective-permute-start | bytes 208904 | tf_op jit(solution)/shard_map/ppermute | solution.py:197
  95.5 5.4 %collective-permute-start.22 = (f32[136,128]{1,0:T(8,128)S(1)}, f32[136,128]{1,0:T(8,128)S(1)}, u32[]{:S(2)}, u32[]{:S(2)}) collective-permute-start(f32[136,128]{1,0:T(8,128)S(1)} %add.36), channel_id=1, source_target_pairs={{0,4},{1,5},{2,6},{3,7},{4,0},{5,1},{6,2},{7,3},{8,12},{9,13},{10,... | collective-permute-start | bytes 208904 | tf_op jit(solution)/shard_map/ppermute | solution.py:197
  100.9 7.5 %collective-permute-start.24 = (f32[64,128]{1,0:T(8,128)S(1)}, f32[64,128]{1,0:T(8,128)S(1)}, u32[]{:S(2)}, u32[]{:S(2)}) collective-permute-start(f32[64,128]{1,0:T(8,128)S(1)} %slice.50), channel_id=1, source_target_pairs={{0,16},{8,24},{16,0},{24,8},{1,17},{9,25},{17,1},{25,9},{2,18},{10... | collective-permute-start | bytes 98312 | tf_op jit(solution)/shard_map/ppermute | solution.py:174

commit v6 on v5

--- a/solution.py
+++ b/solution.py
@@ -480,9 +480,7 @@
     image_all = rest_of_pairs(jnp.concatenate([piece[:packs * blk] for piece in pieces], axis=0), parts)
     moment_all = rest_of_pairs(after(sums[half_col + 8:], *image_all), parts)
 
-    def factor_of(*refs):
-        sums_ref, full_ref, pieces = refs[0], refs[1], refs[2:2 + count]
-        inverse, basis_ref, image_ref, raw = refs[2 + count:]
+    def factor_of(sums_ref, inverse):
         tiles = ncol // 8
         gram_now = whole_of(sums_ref[:half_col, :], sums_ref[half_col:half_col + 1, :]) * (1.0 / total)
         a = [gram_now[t * 8:(t + 1) * 8, :] for t in range(tiles)]
@@ -517,32 +515,30 @@
             pivot = jnp.sum(jnp.where(lanes == subs + t * 8, a[t], 0.0), axis=1, keepdims=True)
             inverse[t * 8:(t + 1) * 8, :] = e[t] * (1.0 / jnp.sqrt(pivot))
 
-        inv = inverse[...]
+
+    inverse = call(factor_of, sds((ncol, ncol), F32), in_specs=[VMEM()], micros=0.5)(after(sums, *image_all))
+
+    def finish(*refs):
+        full_ref, pieces, moments, inv_ref = refs[0], refs[1:1 + count], refs[1 + count:1 + 2 * count], refs[1 + 2 * count]
+        basis_ref, image_ref, projected_ref, raw = refs[2 + 2 * count:]
+        inv = inv_ref[...]
+        turned = inv.T
+        strips = [unpacked(moments, slice(0, span), g) for g in range(count)]
+        m = jnp.concatenate(strips, axis=0) * (1.0 / total)
+        half = exact(inv, m, ((1,), (0,)))
         for i in range(blk_dev):
             raw[i * blk:(i + 1) * blk, :] = unpacked(pieces, block_rows(i), i % count)
-        turned = inv.T
         basis_ref[...] = apply_wide(jnp.concatenate(split(full_ref[...]), axis=1), turned)
         image_ref[...] = apply_wide(jnp.concatenate(split(raw[...]), axis=1), turned)
-
-    inverse, basis, basis_image = call(
-        factor_of,
-        (sds((ncol, ncol), F32), sds((rows_here, ncol), F32), sds((rows_here, ncol), F32)),
-        in_specs=[VMEM()] * (2 + count),
+        projected_ref[...] = exact(half, turned, ((1,), (0,)))
+
+    return call(
+        finish,
+        (sds((rows_here, ncol), F32), sds((rows_here, ncol), F32), sds((ncol, ncol), F32)),
+        in_specs=[VMEM()] * (2 + 2 * count),
         scratch=[pltpu.VMEM((rows_here, ncol), F32)],
-        micros=0.5,
-    )(sums, full, *image_all)
-
-    def project(*refs):
-        moments, inv_ref, projected_ref = refs[:count], refs[count], refs[count + 1]
-        inv = inv_ref[...]
-        strips = [unpacked(moments, slice(0, span), g) for g in range(count)]
-        m = jnp.concatenate(strips, axis=0) * (1.0 / total)
-        projected_ref[...] = exact(exact(inv, m, ((1,), (0,))), inv, ((1,), (1,)))
-
-    projected = call(
-        project, sds((ncol, ncol), F32), in_specs=[VMEM()] * (count + 1), micros=1.0,
-    )(*moment_all, inverse)
-    return (basis, basis_image, projected)
+        micros=3.0,
+    )(full, *image_all, *moment_all, inverse)
 
 
 def solution(mesh):

time: 110 us -> 109 us (level)
  Pallas kernels: 27.8 us -> 26.6 us
    pallas_call x2, Pallas kernels: 7.2 us -> 6.06 us  [the longest x1 4.11 us: per_device(): call(factor_of, sds((ncol, ncol), F32), in_specs=[VMEM()], micros=0.5)]
  transfers between devices with their start and end apart: 25 -> 25, of which waited for: 15 -> 15; matrix products, arithmetic and copies ran while one was open for 0% -> 0% of each run, Pallas kernels for 13% -> 11%
where the time goes in v6:
time: 109 us
  starting transfers between devices  52.1 us (48%)
  waiting for transfers between devices  27.1 us (25%)
  Pallas kernels  26.6 us (24%)
  local copies, waits for them, and re-layouts  1.74 us (2%)
    ppermute x7, starting transfers between devices, pass_on(): return lax.ppermute(arrived, 'rows', pairs)  29.1 us
    ppermute x7, starting transfers between devices, swap(): return lax.ppermute(value, 'rows', [(i, i ^ 1) for i in range(nrows)])  10.6 us
    ppermute x7, waiting for transfers between devices, swap(): return lax.ppermute(value, 'rows', [(i, i ^ 1) for i in range(nrows)])  9.94 us
    ppermute x7, waiting for transfers between devices, pass_on(): return lax.ppermute(arrived, 'rows', pairs)  9.42 us
    ppermute x3, starting transfers between devices, sum_rows(): lax.ppermute(value, 'rows', [(i, i ^ step) for i in range(nrows)])  7.29 us
    ppermute x3, waiting for transfers between devices, sum_rows(): lax.ppermute(value, 'rows', [(i, i ^ step) for i in range(nrows)])  5.65 us
    pallas_call x1, Pallas kernels, per_device(): call(prepare, (sds((blk_dev, blk, ncol), F32), sds((packs * blk + blk_dev...  5.43 us
    pallas_call x1, Pallas kernels, per_device(): call(second_iterate, [sds((size, blk, wide), F32) for size in sizes] + [s...  4.55 us
  transfers between devices with their start and end apart: 25, of which 15 were waited for; matrix products, arithmetic and copies ran while one was open for 0% of the time, Pallas kernels for 11%

profile of v6, /device:TPU:0, one launch (start us, length us, event | category | flops | bytes accessed | tf_op | source)
XLA Modules:
  0.0 108.6 jit_solution(230300506499392272)
XLA Ops:
  1.6 3.0 %collective-permute-start = (f32[512,128]{1,0:T(8,128)S(1)}, f32[512,128]{1,0:T(8,128)S(1)}, u32[]{:S(2)}, u32[]{:S(2)}) collective-permute-start(f32[512,128]{1,0:T(8,128)S(1)} %bitcast.1), channel_id=1, source_target_pairs={{0,1},{1,0},{2,3},{3,2},{4,5},{5,4},{6,7},{7,6},{8,9},{9,8},{10,11... | collective-permute-start | bytes 786440 | tf_op jit(solution)/shard_map/ppermute | solution.py:152
  5.3 5.4 %shard_map.76 = (f32[8,128,128]{2,1,0:T(8,128)S(1)}, f32[264,128]{1,0:T(8,128)S(1)}, bf16[8,128,256]{2,1,0:T(8,128)(2,1)S(1)}, bf16[8,128,256]{2,1,0:T(8,128)(2,1)S(1)}, bf16[8,256,1024]{2,1,0:T(8,128)(2,1)}) custom-call(f32[1024,128]{1,0:T(8,128)} %start_hbm.1, f32[8,128,128]{2,1,0:T(8,128)} %vec_hbm.1, f32[8,8,128,128]{3,2,1,0:T(8,128)} %coup_hbm.1, ...), custom_call_target="tpu_custom_call" | custom-call | flops 22000001024 | tf_op jit(solution)/shard_map/pallas_call | solution.py:250
  11.0 1.7 %collective-permute-start.1 = (f32[264,128]{1,0:T(8,128)S(1)}, f32[264,128]{1,0:T(8,128)S(1)}, u32[]{:S(2)}, u32[]{:S(2)}) collective-permute-start(f32[264,128]{1,0:T(8,128)S(1)} %get-tuple-element.30), channel_id=1, source_target_pairs={{0,1},{1,0},{2,3},{3,2},{4,5},{5,4},{6,7},{7,6},{8,9},{9,8},{10,11... | collective-permute-start | bytes 405512 | tf_op jit(solution)/shard_map/ppermute | solution.py:152
  12.7 3.5 %collective-permute-start.4 = (f32[512,128]{1,0:T(8,128)S(1)}, f32[512,128]{1,0:T(8,128)S(1)}, u32[]{:S(2)}, u32[]{:S(2)}) collective-permute-start(f32[512,128]{1,0:T(8,128)S(1)} %collective-permute-done.refs_4_), channel_id=1, source_target_pairs={{0,2},{2,4},{4,6},{3,1},{5,3},{7,5},{8,10},{10,12},{12,14},{11,9},... | collective-permute-start | bytes 786440 | tf_op jit(solution)/shard_map/ppermute | solution.py:158
  16.2 3.5 %collective-permute-start.3 = (f32[264,128]{1,0:T(8,128)S(1)}, f32[264,128]{1,0:T(8,128)S(1)}, u32[]{:S(2)}, u32[]{:S(2)}) collective-permute-start(f32[264,128]{1,0:T(8,128)S(1)} %collective-permute-done.1.refs_3_), channel_id=1, source_target_pairs={{0,2},{2,4},{4,6},{3,1},{5,3},{7,5},{8,10},{10,12},{12,14},{11,9},... | collective-permute-start | bytes 405512 | tf_op jit(solution)/shard_map/ppermute | solution.py:158
  19.8 2.2 %collective-permute-done.4.refs_9_ = f32[512,128]{1,0:T(8,128)S(1)} collective-permute-done((f32[512,128]{1,0:T(8,128)S(1)}, f32[512,128]{1,0:T(8,128)S(1)}, u32[]{:S(2)}, u32[]{:S(2)}) %collective-permute-start.4) | collective-permute-done | bytes 262176 | tf_op jit(solution)/shard_map/ppermute | solution.py:158
  22.0 1.4 %collective-permute-done.3.refs_8_ = f32[264,128]{1,0:T(8,128)S(1)} collective-permute-done((f32[264,128]{1,0:T(8,128)S(1)}, f32[264,128]{1,0:T(8,128)S(1)}, u32[]{:S(2)}, u32[]{:S(2)}) %collective-permute-start.3) | collective-permute-done | bytes 135200 | tf_op jit(solution)/shard_map/ppermute | solution.py:158
  23.5 1.7 %shard_map.77 = (bf16[2048,256]{1,0:T(8,128)(2,1)S(1)}, bf16[2048,256]{1,0:T(8,128)(2,1)S(1)}, f32[8,128,256]{2,1,0:T(8,128)S(1)}) custom-call(f32[8,128,128]{2,1,0:T(8,128)S(1)} %get-tuple-element.26.refs_0_.refs_6_.refs_17_, f32[8,128]{1,0:T(8,128)S(1)} %copy-done.1, bf16[8,128,256]{2,1,0:T(8,128)(2,1)S(1)} %get-tuple-element.27.refs_2_.refs_4_.refs_15_, ...), custom_call_target="tpu_custom_call" | custom-call | flops 2200000000 | tf_op jit(solution)/shard_map/pallas_call | solution.py:311
  25.2 4.6 %shard_map.78 = (f32[2,128,256]{2,1,0:T(8,128)S(1)}, f32[2,128,256]{2,1,0:T(8,128)S(1)}, f32[2,128,256]{2,1,0:T(8,128)S(1)}, f32[2,128,256]{2,1,0:T(8,128)S(1)}, f32[8,128,256]{2,1,0:T(8,128)S(1)}) custom-call(s32[8,8]{1,0:T(8,128)S(1)} %fusion.refs_0_.slots, bf16[2048,256]{1,0:T(8,128)(2,1)S(1)} %get-tuple-element.32.refs_1_, ...), custom_call_target="tpu_custom_call" | custom-call | flops 6600000000 | tf_op jit(solution)/shard_map/pallas_call | solution.py:357
  29.8 1.8 %collective-permute-start.6 = (f32[2,128,256]{2,1,0:T(8,128)S(1)}, f32[2,128,256]{2,1,0:T(8,128)S(1)}, u32[]{:S(2)}, u32[]{:S(2)}) collective-permute-start(f32[2,128,256]{2,1,0:T(8,128)S(1)} %get-tuple-element.38.refs_1_), channel_id=1, source_target_pairs={{0,1},{1,0},{2,3},{3,2},{4,5},{5,4},{6,7},{7,6},{8,9},{9,8},{10,11... | collective-permute-start | bytes 786440 | tf_op jit(solution)/shard_map/ppermute | solution.py:152
  31.9 1.7 %collective-permute-start.8 = (f32[2,128,256]{2,1,0:T(8,128)S(1)}, f32[2,128,256]{2,1,0:T(8,128)S(1)}, u32[]{:S(2)}, u32[]{:S(2)}) collective-permute-start(f32[2,128,256]{2,1,0:T(8,128)S(1)} %get-tuple-element.40.refs_3_), channel_id=1, source_target_pairs={{0,1},{1,0},{2,3},{3,2},{4,5},{5,4},{6,7},{7,6},{8,9},{9,8},{10,11... | collective-permute-start | bytes 786440 | tf_op jit(solution)/shard_map/ppermute | solution.py:152
  33.9 5.0 %collective-permute-done.6.refs_5_ = f32[2,128,256]{2,1,0:T(8,128)S(1)} collective-permute-done((f32[2,128,256]{2,1,0:T(8,128)S(1)}, f32[2,128,256]{2,1,0:T(8,128)S(1)}, u32[]{:S(2)}, u32[]{:S(2)}) %collective-permute-start.6) | collective-permute-done | bytes 262176 | tf_op jit(solution)/shard_map/ppermute | solution.py:152
  38.9 4.4 %collective-permute-start.10 = (f32[2,128,256]{2,1,0:T(8,128)S(1)}, f32[2,128,256]{2,1,0:T(8,128)S(1)}, u32[]{:S(2)}, u32[]{:S(2)}) collective-permute-start(f32[2,128,256]{2,1,0:T(8,128)S(1)} %collective-permute-done.6.refs_5_), channel_id=1, source_target_pairs={{0,2},{2,4},{4,6},{3,1},{5,3},{7,5},{8,10},{10,12},{12,14},{11,9},... | collective-permute-start | bytes 786440 | tf_op jit(solution)/shard_map/ppermute | solution.py:158
  44.5 4.4 %collective-permute-start.11 = (f32[2,128,256]{2,1,0:T(8,128)S(1)}, f32[2,128,256]{2,1,0:T(8,128)S(1)}, u32[]{:S(2)}, u32[]{:S(2)}) collective-permute-start(f32[2,128,256]{2,1,0:T(8,128)S(1)} %collective-permute-done.7.refs_6_), channel_id=1, source_target_pairs={{0,2},{2,4},{4,6},{3,1},{5,3},{7,5},{8,10},{10,12},{12,14},{11,9},... | collective-permute-start | bytes 786440 | tf_op jit(solution)/shard_map/ppermute | solution.py:158
  50.2 4.4 %collective-permute-start.12 = (f32[2,128,256]{2,1,0:T(8,128)S(1)}, f32[2,128,256]{2,1,0:T(8,128)S(1)}, u32[]{:S(2)}, u32[]{:S(2)}) collective-permute-start(f32[2,128,256]{2,1,0:T(8,128)S(1)} %collective-permute-done.8.refs_7_), channel_id=1, source_target_pairs={{0,2},{2,4},{4,6},{3,1},{5,3},{7,5},{8,10},{10,12},{12,14},{11,9},... | collective-permute-start | bytes 786440 | tf_op jit(solution)/shard_map/ppermute | solution.py:158
  55.4 4.4 %collective-permute-start.13 = (f32[2,128,256]{2,1,0:T(8,128)S(1)}, f32[2,128,256]{2,1,0:T(8,128)S(1)}, u32[]{:S(2)}, u32[]{:S(2)}) collective-permute-start(f32[2,128,256]{2,1,0:T(8,128)S(1)} %collective-permute-done.9.refs_8_), channel_id=1, source_target_pairs={{0,2},{2,4},{4,6},{3,1},{5,3},{7,5},{8,10},{10,12},{12,14},{11,9},... | collective-permute-start | bytes 786440 | tf_op jit(solution)/shard_map/ppermute | solution.py:158
  59.8 5.4 %collective-permute-done.13.refs_12_ = f32[2,128,256]{2,1,0:T(8,128)S(1)} collective-permute-done((f32[2,128,256]{2,1,0:T(8,128)S(1)}, f32[2,128,256]{2,1,0:T(8,128)S(1)}, u32[]{:S(2)}, u32[]{:S(2)}) %collective-permute-start.13) | collective-permute-done | bytes 262176 | tf_op jit(solution)/shard_map/ppermute | solution.py:158
  65.2 3.9 %shard_map.79 = (f32[256,128]{1,0:T(8,128)S(1)}, f32[8,128,128]{2,1,0:T(8,128)S(1)}) custom-call(s32[8,8]{1,0:T(8,128)S(1)} %fusion.refs_0_.slots, f32[2,128,256]{2,1,0:T(8,128)S(1)} %get-tuple-element.38.refs_1_, f32[2,128,256]{2,1,0:T(8,128)S(1)} %get-tuple-element.39.refs_2_, f32[2,128,256]{2,1,0:T(8,128)S(1)} %get-tuple-element.40.refs_3_, ...), custom_call_target="tpu_custom_call" | custom-call | flops 6600000000 | tf_op jit(solution)/shard_map/pallas_call | solution.py:391
  69.1 1.7 %collective-permute-start.17 = (f32[256,128]{1,0:T(8,128)S(1)}, f32[256,128]{1,0:T(8,128)S(1)}, u32[]{:S(2)}, u32[]{:S(2)}) collective-permute-start(f32[256,128]{1,0:T(8,128)S(1)} %get-tuple-element.43.refs_0_.own_f), channel_id=1, source_target_pairs={{0,1},{1,0},{2,3},{3,2},{4,5},{5,4},{6,7},{7,6},{8,9},{9,8},{10,11... | collective-permute-start | bytes 393224 | tf_op jit(solution)/shard_map/ppermute | solution.py:152
  70.9 1.5 %collective-permute-start.15 = (f32[256,128]{1,0:T(8,128)S(1)}, f32[256,128]{1,0:T(8,128)S(1)}, u32[]{:S(2)}, u32[]{:S(2)}) collective-permute-start(f32[256,128]{1,0:T(8,128)S(1)} %get-tuple-element.43.refs_0_.own_f), channel_id=1, source_target_pairs={{16,0},{24,8},{0,16},{8,24},{17,1},{25,9},{1,17},{9,25},{18,2},{26... | collective-permute-start | bytes 393224 | tf_op jit(solution)/shard_map/ppermute | solution.py:186
  72.7 1.4 %collective-permute-done.17.first_f = f32[256,128]{1,0:T(8,128)S(1)} collective-permute-done((f32[256,128]{1,0:T(8,128)S(1)}, f32[256,128]{1,0:T(8,128)S(1)}, u32[]{:S(2)}, u32[]{:S(2)}) %collective-permute-start.17) | collective-permute-done | bytes 131104 | tf_op jit(solution)/shard_map/ppermute | solution.py:152
  74.2 4.6 %collective-permute-start.18 = (f32[256,128]{1,0:T(8,128)S(1)}, f32[256,128]{1,0:T(8,128)S(1)}, u32[]{:S(2)}, u32[]{:S(2)}) collective-permute-start(f32[256,128]{1,0:T(8,128)S(1)} %collective-permute-done.17.first_f), channel_id=1, source_target_pairs={{0,2},{2,4},{4,6},{3,1},{5,3},{7,5},{8,10},{10,12},{12,14},{11,9},... | collective-permute-start | bytes 393224 | tf_op jit(solution)/shard_map/ppermute | solution.py:158
  81.1 3.7 %shard_map.81 = f32[288,128]{1,0:T(8,128)S(1)} custom-call(s32[8,8]{1,0:T(8,128)S(1)} %fusion.refs_0_.slots, f32[256,128]{1,0:T(8,128)S(1)} %get-tuple-element.43.refs_0_.own_f, f32[256,128]{1,0:T(8,128)S(1)} %collective-permute-done.17.first_f, f32[256,128]{1,0:T(8,128)S(1)} %collective-permute-done.18.second_f, ...), custom_call_target="tpu_custom_call" | custom-call | flops 4180000000 | tf_op jit(solution)/shard_map/pallas_call | solution.py:465
  86.3 1.7 %collective-permute-start.21 = (f32[136,128]{1,0:T(8,128)S(1)}, f32[136,128]{1,0:T(8,128)S(1)}, u32[]{:S(2)}, u32[]{:S(2)}) collective-permute-start(f32[136,128]{1,0:T(8,128)S(1)} %pad_maximum_fusion.1), channel_id=1, source_target_pairs={{0,1},{1,0},{2,3},{3,2},{4,5},{5,4},{6,7},{7,6},{8,9},{9,8},{10,11... | collective-permute-start | bytes 208904 | tf_op jit(solution)/shard_map/ppermute | solution.py:197
  88.0 1.6 %collective-permute-start.20 = (f32[512,128]{1,0:T(8,128)S(1)}, f32[512,128]{1,0:T(8,128)S(1)}, u32[]{:S(2)}, u32[]{:S(2)}) collective-permute-start(f32[512,128]{1,0:T(8,128)S(1)} %pad_maximum_fusion), channel_id=1, source_target_pairs={{0,16},{8,24},{16,0},{24,8},{1,17},{9,25},{17,1},{25,9},{2,18},{10... | collective-permute-start | bytes 786440 | tf_op jit(solution)/shard_map/ppermute | solution.py:174
  90.7 2.5 %collective-permute-start.22 = (f32[136,128]{1,0:T(8,128)S(1)}, f32[136,128]{1,0:T(8,128)S(1)}, u32[]{:S(2)}, u32[]{:S(2)}) collective-permute-start(f32[136,128]{1,0:T(8,128)S(1)} %fusion.3), channel_id=1, source_target_pairs={{0,2},{1,3},{2,0},{3,1},{4,6},{5,7},{6,4},{7,5},{8,10},{9,11},{10,... | collective-permute-start | bytes 208904 | tf_op jit(solution)/shard_map/ppermute | solution.py:197
  93.2 2.3 %collective-permute-done.22 = f32[136,128]{1,0:T(8,128)S(1)} collective-permute-done((f32[136,128]{1,0:T(8,128)S(1)}, f32[136,128]{1,0:T(8,128)S(1)}, u32[]{:S(2)}, u32[]{:S(2)}) %collective-permute-start.22) | collective-permute-done | bytes 69664 | tf_op jit(solution)/shard_map/ppermute | solution.py:197
  95.5 3.1 %collective-permute-start.23 = (f32[136,128]{1,0:T(8,128)S(1)}, f32[136,128]{1,0:T(8,128)S(1)}, u32[]{:S(2)}, u32[]{:S(2)}) collective-permute-start(f32[136,128]{1,0:T(8,128)S(1)} %add.36), channel_id=1, source_target_pairs={{0,4},{1,5},{2,6},{3,7},{4,0},{5,1},{6,2},{7,3},{8,12},{9,13},{10,... | collective-permute-start | bytes 208904 | tf_op jit(solution)/shard_map/ppermute | solution.py:197
  98.5 2.3 %collective-permute-done.23 = f32[136,128]{1,0:T(8,128)S(1)} collective-permute-done((f32[136,128]{1,0:T(8,128)S(1)}, f32[136,128]{1,0:T(8,128)S(1)}, u32[]{:S(2)}, u32[]{:S(2)}) %collective-permute-start.23) | collective-permute-done | bytes 69664 | tf_op jit(solution)/shard_map/ppermute | solution.py:197
  100.9 1.6 %collective-permute-start.24 = (f32[64,128]{1,0:T(8,128)S(1)}, f32[64,128]{1,0:T(8,128)S(1)}, u32[]{:S(2)}, u32[]{:S(2)}) collective-permute-start(f32[64,128]{1,0:T(8,128)S(1)} %slice.50), channel_id=1, source_target_pairs={{0,16},{8,24},{16,0},{24,8},{1,17},{9,25},{17,1},{25,9},{2,18},{10... | collective-permute-start | bytes 98312 | tf_op jit(solution)/shard_map/ppermute | solution.py:174
  102.5 4.1 %shard_map.82.refs_9_ = f32[128,128]{1,0:T(8,128)S(1)} custom-call(f32[136,128]{1,0:T(8,128)S(1)} %add.37.sums_ref), custom_call_target="tpu_custom_call" | custom-call | flops 550000000 | tf_op jit(solution)/shard_map/pallas_call | solution.py:519
  106.6 1.9 %shard_map.83 = (f32[1024,128]{1,0:T(8,128)}, f32[1024,128]{1,0:T(8,128)}, f32[128,128]{1,0:T(8,128)}) custom-call(f32[1024,128]{1,0:T(8,128)S(1)} %get-tuple-element.44.full_ref.refs_0_, f32[256,128]{1,0:T(8,128)S(1)} %slice.44.refs_1_, f32[256,128]{1,0:T(8,128)S(1)} %slice.45.refs_2_, f32[256,128]{1,0:T(8,128)S(1)} %get-tuple-element.50.refs_3_, ...), custom_call_target="tpu_custom_call" | custom-call | flops 3300000000 | tf_op jit(solution)/shard_map/pallas_call | solution.py:535
  (49 shorter events, 11.2 us)
Async XLA Ops:
  1.6 9.3 %collective-permute-start = (f32[512,128]{1,0:T(8,128)S(1)}, f32[512,128]{1,0:T(8,128)S(1)}, u32[]{:S(2)}, u32[]{:S(2)}) collective-permute-start(f32[512,128]{1,0:T(8,128)S(1)} %bitcast.1), channel_id=1, source_target_pairs={{0,1},{1,0},{2,3},{3,2},{4,5},{5,4},{6,7},{7,6},{8,9},{9,8},{10,11... | collective-permute-start | bytes 786440 | tf_op jit(solution)/shard_map/ppermute | solution.py:152
  4.7 0.7 copy-start
  5.3 18.1 %copy-start.3 = (s32[8,8]{1,0:T(8,128)S(1)}, s32[8,8]{1,0:T(8,128)}, u32[]{:S(2)}) copy-start(s32[8,8]{1,0:T(8,128)} %param.5) | copy-start | bytes 772
  5.3 18.2 %copy-start.1 = (f32[8,128]{1,0:T(8,128)S(1)}, f32[8,128]{1,0:T(8,128)}, u32[]{:S(2)}) copy-start(f32[8,128]{1,0:T(8,128)} %refs_19_.1) | copy-start | bytes 12292
  11.0 5.2 %collective-permute-start.1 = (f32[264,128]{1,0:T(8,128)S(1)}, f32[264,128]{1,0:T(8,128)S(1)}, u32[]{:S(2)}, u32[]{:S(2)}) collective-permute-start(f32[264,128]{1,0:T(8,128)S(1)} %get-tuple-element.30), channel_id=1, source_target_pairs={{0,1},{1,0},{2,3},{3,2},{4,5},{5,4},{6,7},{7,6},{8,9},{9,8},{10,11... | collective-permute-start | bytes 405512 | tf_op jit(solution)/shard_map/ppermute | solution.py:152
  12.7 9.3 %collective-permute-start.4 = (f32[512,128]{1,0:T(8,128)S(1)}, f32[512,128]{1,0:T(8,128)S(1)}, u32[]{:S(2)}, u32[]{:S(2)}) collective-permute-start(f32[512,128]{1,0:T(8,128)S(1)} %collective-permute-done.refs_4_), channel_id=1, source_target_pairs={{0,2},{2,4},{4,6},{3,1},{5,3},{7,5},{8,10},{10,12},{12,14},{11,9},... | collective-permute-start | bytes 786440 | tf_op jit(solution)/shard_map/ppermute | solution.py:158
  16.2 7.3 %collective-permute-start.3 = (f32[264,128]{1,0:T(8,128)S(1)}, f32[264,128]{1,0:T(8,128)S(1)}, u32[]{:S(2)}, u32[]{:S(2)}) collective-permute-start(f32[264,128]{1,0:T(8,128)S(1)} %collective-permute-done.1.refs_3_), channel_id=1, source_target_pairs={{0,2},{2,4},{4,6},{3,1},{5,3},{7,5},{8,10},{10,12},{12,14},{11,9},... | collective-permute-start | bytes 405512 | tf_op jit(solution)/shard_map/ppermute | solution.py:158
  19.7 3.8 %collective-permute-start.2 = (f32[512,128]{1,0:T(8,128)S(1)}, f32[512,128]{1,0:T(8,128)S(1)}, u32[]{:S(2)}, u32[]{:S(2)}) collective-permute-start(f32[512,128]{1,0:T(8,128)S(1)} %collective-permute-done.refs_4_), channel_id=1, source_target_pairs={{0,8},{8,0},{16,24},{24,16},{1,9},{9,1},{17,25},{25,17},{2,10},{10... | collective-permute-start | bytes 786440 | tf_op jit(solution)/shard_map/ppermute | solution.py:170
  19.8 5.4 %copy-start.2 = (bf16[8,256,1024]{2,1,0:T(8,128)(2,1)S(1)}, bf16[8,256,1024]{2,1,0:T(8,128)(2,1)}, u32[]{:S(2)}) copy-start(bf16[8,256,1024]{2,1,0:T(8,128)(2,1)} %get-tuple-element.34.refs_3_.refs_14_.c) | copy-start | bytes 12582916
  23.5 1.7 %collective-permute-start.5 = (f32[512,128]{1,0:T(8,128)S(1)}, f32[512,128]{1,0:T(8,128)S(1)}, u32[]{:S(2)}, u32[]{:S(2)}) collective-permute-start(f32[512,128]{1,0:T(8,128)S(1)} %collective-permute-done.4.refs_9_), channel_id=1, source_target_pairs={{0,8},{8,0},{16,24},{24,16},{1,9},{9,1},{17,25},{25,17},{2,10},{10... | collective-permute-start | bytes 786440 | tf_op jit(solution)/shard_map/ppermute | solution.py:170
  29.8 9.2 %collective-permute-start.6 = (f32[2,128,256]{2,1,0:T(8,128)S(1)}, f32[2,128,256]{2,1,0:T(8,128)S(1)}, u32[]{:S(2)}, u32[]{:S(2)}) collective-permute-start(f32[2,128,256]{2,1,0:T(8,128)S(1)} %get-tuple-element.38.refs_1_), channel_id=1, source_target_pairs={{0,1},{1,0},{2,3},{3,2},{4,5},{5,4},{6,7},{7,6},{8,9},{9,8},{10,11... | collective-permute-start | bytes 786440 | tf_op jit(solution)/shard_map/ppermute | solution.py:152
  31.5 13.0 %collective-permute-start.7 = (f32[2,128,256]{2,1,0:T(8,128)S(1)}, f32[2,128,256]{2,1,0:T(8,128)S(1)}, u32[]{:S(2)}, u32[]{:S(2)}) collective-permute-start(f32[2,128,256]{2,1,0:T(8,128)S(1)} %get-tuple-element.39.refs_2_), channel_id=1, source_target_pairs={{0,1},{1,0},{2,3},{3,2},{4,5},{5,4},{6,7},{7,6},{8,9},{9,8},{10,11... | collective-permute-start | bytes 786440 | tf_op jit(solution)/shard_map/ppermute | solution.py:152
  31.9 18.3 %collective-permute-start.8 = (f32[2,128,256]{2,1,0:T(8,128)S(1)}, f32[2,128,256]{2,1,0:T(8,128)S(1)}, u32[]{:S(2)}, u32[]{:S(2)}) collective-permute-start(f32[2,128,256]{2,1,0:T(8,128)S(1)} %get-tuple-element.40.refs_3_), channel_id=1, source_target_pairs={{0,1},{1,0},{2,3},{3,2},{4,5},{5,4},{6,7},{7,6},{8,9},{9,8},{10,11... | collective-permute-start | bytes 786440 | tf_op jit(solution)/shard_map/ppermute | solution.py:152
  33.5 21.9 %collective-permute-start.9 = (f32[2,128,256]{2,1,0:T(8,128)S(1)}, f32[2,128,256]{2,1,0:T(8,128)S(1)}, u32[]{:S(2)}, u32[]{:S(2)}) collective-permute-start(f32[2,128,256]{2,1,0:T(8,128)S(1)} %get-tuple-element.41.refs_4_), channel_id=1, source_target_pairs={{0,1},{1,0},{2,3},{3,2},{4,5},{5,4},{6,7},{7,6},{8,9},{9,8},{10,11... | collective-permute-start | bytes 786440 | tf_op jit(solution)/shard_map/ppermute | solution.py:152
  38.9 20.9 %collective-permute-start.10 = (f32[2,128,256]{2,1,0:T(8,128)S(1)}, f32[2,128,256]{2,1,0:T(8,128)S(1)}, u32[]{:S(2)}, u32[]{:S(2)}) collective-permute-start(f32[2,128,256]{2,1,0:T(8,128)S(1)} %collective-permute-done.6.refs_5_), channel_id=1, source_target_pairs={{0,2},{2,4},{4,6},{3,1},{5,3},{7,5},{8,10},{10,12},{12,14},{11,9},... | collective-permute-start | bytes 786440 | tf_op jit(solution)/shard_map/ppermute | solution.py:158
  44.5 15.3 %collective-permute-start.11 = (f32[2,128,256]{2,1,0:T(8,128)S(1)}, f32[2,128,256]{2,1,0:T(8,128)S(1)}, u32[]{:S(2)}, u32[]{:S(2)}) collective-permute-start(f32[2,128,256]{2,1,0:T(8,128)S(1)} %collective-permute-done.7.refs_6_), channel_id=1, source_target_pairs={{0,2},{2,4},{4,6},{3,1},{5,3},{7,5},{8,10},{10,12},{12,14},{11,9},... | collective-permute-start | bytes 786440 | tf_op jit(solution)/shard_map/ppermute | solution.py:158
  50.2 9.7 %collective-permute-start.12 = (f32[2,128,256]{2,1,0:T(8,128)S(1)}, f32[2,128,256]{2,1,0:T(8,128)S(1)}, u32[]{:S(2)}, u32[]{:S(2)}) collective-permute-start(f32[2,128,256]{2,1,0:T(8,128)S(1)} %collective-permute-done.8.refs_7_), channel_id=1, source_target_pairs={{0,2},{2,4},{4,6},{3,1},{5,3},{7,5},{8,10},{10,12},{12,14},{11,9},... | collective-permute-start | bytes 786440 | tf_op jit(solution)/shard_map/ppermute | solution.py:158
  55.4 9.8 %collective-permute-start.13 = (f32[2,128,256]{2,1,0:T(8,128)S(1)}, f32[2,128,256]{2,1,0:T(8,128)S(1)}, u32[]{:S(2)}, u32[]{:S(2)}) collective-permute-start(f32[2,128,256]{2,1,0:T(8,128)S(1)} %collective-permute-done.9.refs_8_), channel_id=1, source_target_pairs={{0,2},{2,4},{4,6},{3,1},{5,3},{7,5},{8,10},{10,12},{12,14},{11,9},... | collective-permute-start | bytes 786440 | tf_op jit(solution)/shard_map/ppermute | solution.py:158
  69.1 5.0 %collective-permute-start.17 = (f32[256,128]{1,0:T(8,128)S(1)}, f32[256,128]{1,0:T(8,128)S(1)}, u32[]{:S(2)}, u32[]{:S(2)}) collective-permute-start(f32[256,128]{1,0:T(8,128)S(1)} %get-tuple-element.43.refs_0_.own_f), channel_id=1, source_target_pairs={{0,1},{1,0},{2,3},{3,2},{4,5},{5,4},{6,7},{7,6},{8,9},{9,8},{10,11... | collective-permute-start | bytes 393224 | tf_op jit(solution)/shard_map/ppermute | solution.py:152
  70.9 7.9 %collective-permute-start.16 = (f32[256,128]{1,0:T(8,128)S(1)}, f32[256,128]{1,0:T(8,128)S(1)}, u32[]{:S(2)}, u32[]{:S(2)}) collective-permute-start(f32[256,128]{1,0:T(8,128)S(1)} %get-tuple-element.43.refs_0_.own_f), channel_id=1, source_target_pairs={{24,0},{16,8},{8,16},{0,24},{25,1},{17,9},{9,17},{1,25},{26,2},{18... | collective-permute-start | bytes 393224 | tf_op jit(solution)/shard_map/ppermute | solution.py:186
  70.9 8.6 %collective-permute-start.15 = (f32[256,128]{1,0:T(8,128)S(1)}, f32[256,128]{1,0:T(8,128)S(1)}, u32[]{:S(2)}, u32[]{:S(2)}) collective-permute-start(f32[256,128]{1,0:T(8,128)S(1)} %get-tuple-element.43.refs_0_.own_f), channel_id=1, source_target_pairs={{16,0},{24,8},{0,16},{8,24},{17,1},{25,9},{1,17},{9,25},{18,2},{26... | collective-permute-start | bytes 393224 | tf_op jit(solution)/shard_map/ppermute | solution.py:186
  72.4 7.1 %collective-permute-start.14 = (f32[256,128]{1,0:T(8,128)S(1)}, f32[256,128]{1,0:T(8,128)S(1)}, u32[]{:S(2)}, u32[]{:S(2)}) collective-permute-start(f32[256,128]{1,0:T(8,128)S(1)} %get-tuple-element.43.refs_0_.own_f), channel_id=1, source_target_pairs={{8,0},{0,8},{24,16},{16,24},{9,1},{1,9},{25,17},{17,25},{10,2},{2,... | collective-permute-start | bytes 393224 | tf_op jit(solution)/shard_map/ppermute | solution.py:186
  74.2 6.9 %collective-permute-start.18 = (f32[256,128]{1,0:T(8,128)S(1)}, f32[256,128]{1,0:T(8,128)S(1)}, u32[]{:S(2)}, u32[]{:S(2)}) collective-permute-start(f32[256,128]{1,0:T(8,128)S(1)} %collective-permute-done.17.first_f), channel_id=1, source_target_pairs={{0,2},{2,4},{4,6},{3,1},{5,3},{7,5},{8,10},{10,12},{12,14},{11,9},... | collective-permute-start | bytes 393224 | tf_op jit(solution)/shard_map/ppermute | solution.py:158
  84.8 1.4 %collective-permute-start.19 = (f32[288,128]{1,0:T(8,128)S(1)}, f32[288,128]{1,0:T(8,128)S(1)}, u32[]{:S(2)}, u32[]{:S(2)}) collective-permute-start(f32[288,128]{1,0:T(8,128)S(1)} %shard_map.81), channel_id=1, source_target_pairs={{0,8},{8,0},{16,24},{24,16},{1,9},{9,1},{17,25},{25,17},{2,10},{10... | collective-permute-start | bytes 442376 | tf_op jit(solution)/shard_map/ppermute | solution.py:174
  86.3 4.4 %collective-permute-start.21 = (f32[136,128]{1,0:T(8,128)S(1)}, f32[136,128]{1,0:T(8,128)S(1)}, u32[]{:S(2)}, u32[]{:S(2)}) collective-permute-start(f32[136,128]{1,0:T(8,128)S(1)} %pad_maximum_fusion.1), channel_id=1, source_target_pairs={{0,1},{1,0},{2,3},{3,2},{4,5},{5,4},{6,7},{7,6},{8,9},{9,8},{10,11... | collective-permute-start | bytes 208904 | tf_op jit(solution)/shard_map/ppermute | solution.py:197
  88.0 12.8 %collective-permute-start.20 = (f32[512,128]{1,0:T(8,128)S(1)}, f32[512,128]{1,0:T(8,128)S(1)}, u32[]{:S(2)}, u32[]{:S(2)}) collective-permute-start(f32[512,128]{1,0:T(8,128)S(1)} %pad_maximum_fusion), channel_id=1, source_target_pairs={{0,16},{8,24},{16,0},{24,8},{1,17},{9,25},{17,1},{25,9},{2,18},{10... | collective-permute-start | bytes 786440 | tf_op jit(solution)/shard_map/ppermute | solution.py:174
  90.7 4.8 %collective-permute-start.22 = (f32[136,128]{1,0:T(8,128)S(1)}, f32[136,128]{1,0:T(8,128)S(1)}, u32[]{:S(2)}, u32[]{:S(2)}) collective-permute-start(f32[136,128]{1,0:T(8,128)S(1)} %fusion.3), channel_id=1, source_target_pairs={{0,2},{1,3},{2,0},{3,1},{4,6},{5,7},{6,4},{7,5},{8,10},{9,11},{10,... | collective-permute-start | bytes 208904 | tf_op jit(solution)/shard_map/ppermute | solution.py:197
  95.5 5.4 %collective-permute-start.23 = (f32[136,128]{1,0:T(8,128)S(1)}, f32[136,128]{1,0:T(8,128)S(1)}, u32[]{:S(2)}, u32[]{:S(2)}) collective-permute-start(f32[136,128]{1,0:T(8,128)S(1)} %add.36), channel_id=1, source_target_pairs={{0,4},{1,5},{2,6},{3,7},{4,0},{5,1},{6,2},{7,3},{8,12},{9,13},{10,... | collective-permute-start | bytes 208904 | tf_op jit(solution)/shard_map/ppermute | solution.py:197
  100.9 5.7 %collective-permute-start.24 = (f32[64,128]{1,0:T(8,128)S(1)}, f32[64,128]{1,0:T(8,128)S(1)}, u32[]{:S(2)}, u32[]{:S(2)}) collective-permute-start(f32[64,128]{1,0:T(8,128)S(1)} %slice.50), channel_id=1, source_target_pairs={{0,16},{8,24},{16,0},{24,8},{1,17},{9,25},{17,1},{25,9},{2,18},{10... | collective-permute-start | bytes 98312 | tf_op jit(solution)/shard_map/ppermute | solution.py:174

commit v7 on v6

--- a/solution.py
+++ b/solution.py
@@ -454,7 +454,11 @@
             image = diag[i] + coupled(slots, c, xh, xl, i)
             image_ref[i * blk:(i + 1) * blk, :] = image
             store_packed(joined, i, image)
-        part = exact(full_ref[...], image_ref[...], ((0,), (0,)))
+        left, right = split(full_ref[...]), split(image_ref[...])
+        part = sum(
+            lax.dot_general(left[a], right[b], (((0,), (0,)), ((), ())), preferred_element_type=F32)
+            for a, b in ((0, 0), (0, 1), (1, 0))
+        )
         piece = jnp.zeros((span, ncol), F32)
         for s in range(count):
             piece = piece + jnp.where(

time: 109 us -> 109 us (level)
  no operation moved by 1% of the time
where the time goes in v7:
time: 109 us; the launch traced here: 108 us
  starting transfers between devices  52.1 us (48%)
  waiting for transfers between devices  27.1 us (25%)
  Pallas kernels  26.5 us (24%)
  local copies, waits for them, and re-layouts  1.74 us (2%)
    ppermute x7, starting transfers between devices, pass_on(): return lax.ppermute(arrived, 'rows', pairs)  29.1 us
    ppermute x7, starting transfers between devices, swap(): return lax.ppermute(value, 'rows', [(i, i ^ 1) for i in range(nrows)])  10.6 us
    ppermute x7, waiting for transfers between devices, swap(): return lax.ppermute(value, 'rows', [(i, i ^ 1) for i in range(nrows)])  9.94 us
    ppermute x7, waiting for transfers between devices, pass_on(): return lax.ppermute(arrived, 'rows', pairs)  9.42 us
    ppermute x3, starting transfers between devices, sum_rows(): lax.ppermute(value, 'rows', [(i, i ^ step) for i in range(nrows)])  7.29 us
    ppermute x3, waiting for transfers between devices, sum_rows(): lax.ppermute(value, 'rows', [(i, i ^ step) for i in range(nrows)])  5.65 us
    pallas_call x1, Pallas kernels, per_device(): call(prepare, (sds((blk_dev, blk, ncol), F32), sds((packs * blk + blk_dev...  5.43 us
    pallas_call x1, Pallas kernels, per_device(): call(second_iterate, [sds((size, blk, wide), F32) for size in sizes] + [s...  4.55 us
  transfers between devices with their start and end apart: 25, of which 15 were waited for; matrix products, arithmetic and copies ran while one was open for 0% of the time, Pallas kernels for 11%

profile of v7, /device:TPU:0, one launch (start us, length us, event | category | flops | bytes accessed | tf_op | source)
XLA Modules:
  0.0 108.5 jit_solution(18366222323095917357)
XLA Ops:
  1.6 3.0 %collective-permute-start = (f32[512,128]{1,0:T(8,128)S(1)}, f32[512,128]{1,0:T(8,128)S(1)}, u32[]{:S(2)}, u32[]{:S(2)}) collective-permute-start(f32[512,128]{1,0:T(8,128)S(1)} %bitcast.1), channel_id=1, source_target_pairs={{0,1},{1,0},{2,3},{3,2},{4,5},{5,4},{6,7},{7,6},{8,9},{9,8},{10,11... | collective-permute-start | bytes 786440 | tf_op jit(solution)/shard_map/ppermute | solution.py:152
  5.3 5.4 %shard_map.76 = (f32[8,128,128]{2,1,0:T(8,128)S(1)}, f32[264,128]{1,0:T(8,128)S(1)}, bf16[8,128,256]{2,1,0:T(8,128)(2,1)S(1)}, bf16[8,128,256]{2,1,0:T(8,128)(2,1)S(1)}, bf16[8,256,1024]{2,1,0:T(8,128)(2,1)}) custom-call(f32[1024,128]{1,0:T(8,128)} %start_hbm.1, f32[8,128,128]{2,1,0:T(8,128)} %vec_hbm.1, f32[8,8,128,128]{3,2,1,0:T(8,128)} %coup_hbm.1, ...), custom_call_target="tpu_custom_call" | custom-call | flops 22000001024 | tf_op jit(solution)/shard_map/pallas_call | solution.py:250
  11.0 1.7 %collective-permute-start.1 = (f32[264,128]{1,0:T(8,128)S(1)}, f32[264,128]{1,0:T(8,128)S(1)}, u32[]{:S(2)}, u32[]{:S(2)}) collective-permute-start(f32[264,128]{1,0:T(8,128)S(1)} %get-tuple-element.30), channel_id=1, source_target_pairs={{0,1},{1,0},{2,3},{3,2},{4,5},{5,4},{6,7},{7,6},{8,9},{9,8},{10,11... | collective-permute-start | bytes 405512 | tf_op jit(solution)/shard_map/ppermute | solution.py:152
  12.7 3.5 %collective-permute-start.4 = (f32[512,128]{1,0:T(8,128)S(1)}, f32[512,128]{1,0:T(8,128)S(1)}, u32[]{:S(2)}, u32[]{:S(2)}) collective-permute-start(f32[512,128]{1,0:T(8,128)S(1)} %collective-permute-done.refs_4_), channel_id=1, source_target_pairs={{0,2},{2,4},{4,6},{3,1},{5,3},{7,5},{8,10},{10,12},{12,14},{11,9},... | collective-permute-start | bytes 786440 | tf_op jit(solution)/shard_map/ppermute | solution.py:158
  16.2 3.5 %collective-permute-start.3 = (f32[264,128]{1,0:T(8,128)S(1)}, f32[264,128]{1,0:T(8,128)S(1)}, u32[]{:S(2)}, u32[]{:S(2)}) collective-permute-start(f32[264,128]{1,0:T(8,128)S(1)} %collective-permute-done.1.refs_3_), channel_id=1, source_target_pairs={{0,2},{2,4},{4,6},{3,1},{5,3},{7,5},{8,10},{10,12},{12,14},{11,9},... | collective-permute-start | bytes 405512 | tf_op jit(solution)/shard_map/ppermute | solution.py:158
  19.8 2.2 %collective-permute-done.4.refs_9_ = f32[512,128]{1,0:T(8,128)S(1)} collective-permute-done((f32[512,128]{1,0:T(8,128)S(1)}, f32[512,128]{1,0:T(8,128)S(1)}, u32[]{:S(2)}, u32[]{:S(2)}) %collective-permute-start.4) | collective-permute-done | bytes 262176 | tf_op jit(solution)/shard_map/ppermute | solution.py:158
  22.0 1.4 %collective-permute-done.3.refs_8_ = f32[264,128]{1,0:T(8,128)S(1)} collective-permute-done((f32[264,128]{1,0:T(8,128)S(1)}, f32[264,128]{1,0:T(8,128)S(1)}, u32[]{:S(2)}, u32[]{:S(2)}) %collective-permute-start.3) | collective-permute-done | bytes 135200 | tf_op jit(solution)/shard_map/ppermute | solution.py:158
  23.5 1.7 %shard_map.77 = (bf16[2048,256]{1,0:T(8,128)(2,1)S(1)}, bf16[2048,256]{1,0:T(8,128)(2,1)S(1)}, f32[8,128,256]{2,1,0:T(8,128)S(1)}) custom-call(f32[8,128,128]{2,1,0:T(8,128)S(1)} %get-tuple-element.26.refs_0_.refs_6_.refs_17_, f32[8,128]{1,0:T(8,128)S(1)} %copy-done.1, bf16[8,128,256]{2,1,0:T(8,128)(2,1)S(1)} %get-tuple-element.27.refs_2_.refs_4_.refs_15_, ...), custom_call_target="tpu_custom_call" | custom-call | flops 2200000000 | tf_op jit(solution)/shard_map/pallas_call | solution.py:311
  25.2 4.6 %shard_map.78 = (f32[2,128,256]{2,1,0:T(8,128)S(1)}, f32[2,128,256]{2,1,0:T(8,128)S(1)}, f32[2,128,256]{2,1,0:T(8,128)S(1)}, f32[2,128,256]{2,1,0:T(8,128)S(1)}, f32[8,128,256]{2,1,0:T(8,128)S(1)}) custom-call(s32[8,8]{1,0:T(8,128)S(1)} %fusion.refs_0_.slots, bf16[2048,256]{1,0:T(8,128)(2,1)S(1)} %get-tuple-element.32.refs_1_, ...), custom_call_target="tpu_custom_call" | custom-call | flops 6600000000 | tf_op jit(solution)/shard_map/pallas_call | solution.py:357
  29.8 1.8 %collective-permute-start.6 = (f32[2,128,256]{2,1,0:T(8,128)S(1)}, f32[2,128,256]{2,1,0:T(8,128)S(1)}, u32[]{:S(2)}, u32[]{:S(2)}) collective-permute-start(f32[2,128,256]{2,1,0:T(8,128)S(1)} %get-tuple-element.38.refs_1_), channel_id=1, source_target_pairs={{0,1},{1,0},{2,3},{3,2},{4,5},{5,4},{6,7},{7,6},{8,9},{9,8},{10,11... | collective-permute-start | bytes 786440 | tf_op jit(solution)/shard_map/ppermute | solution.py:152
  31.9 1.7 %collective-permute-start.8 = (f32[2,128,256]{2,1,0:T(8,128)S(1)}, f32[2,128,256]{2,1,0:T(8,128)S(1)}, u32[]{:S(2)}, u32[]{:S(2)}) collective-permute-start(f32[2,128,256]{2,1,0:T(8,128)S(1)} %get-tuple-element.40.refs_3_), channel_id=1, source_target_pairs={{0,1},{1,0},{2,3},{3,2},{4,5},{5,4},{6,7},{7,6},{8,9},{9,8},{10,11... | collective-permute-start | bytes 786440 | tf_op jit(solution)/shard_map/ppermute | solution.py:152
  33.9 5.0 %collective-permute-done.6.refs_5_ = f32[2,128,256]{2,1,0:T(8,128)S(1)} collective-permute-done((f32[2,128,256]{2,1,0:T(8,128)S(1)}, f32[2,128,256]{2,1,0:T(8,128)S(1)}, u32[]{:S(2)}, u32[]{:S(2)}) %collective-permute-start.6) | collective-permute-done | bytes 262176 | tf_op jit(solution)/shard_map/ppermute | solution.py:152
  38.9 4.4 %collective-permute-start.10 = (f32[2,128,256]{2,1,0:T(8,128)S(1)}, f32[2,128,256]{2,1,0:T(8,128)S(1)}, u32[]{:S(2)}, u32[]{:S(2)}) collective-permute-start(f32[2,128,256]{2,1,0:T(8,128)S(1)} %collective-permute-done.6.refs_5_), channel_id=1, source_target_pairs={{0,2},{2,4},{4,6},{3,1},{5,3},{7,5},{8,10},{10,12},{12,14},{11,9},... | collective-permute-start | bytes 786440 | tf_op jit(solution)/shard_map/ppermute | solution.py:158
  44.5 4.4 %collective-permute-start.11 = (f32[2,128,256]{2,1,0:T(8,128)S(1)}, f32[2,128,256]{2,1,0:T(8,128)S(1)}, u32[]{:S(2)}, u32[]{:S(2)}) collective-permute-start(f32[2,128,256]{2,1,0:T(8,128)S(1)} %collective-permute-done.7.refs_6_), channel_id=1, source_target_pairs={{0,2},{2,4},{4,6},{3,1},{5,3},{7,5},{8,10},{10,12},{12,14},{11,9},... | collective-permute-start | bytes 786440 | tf_op jit(solution)/shard_map/ppermute | solution.py:158
  50.2 4.4 %collective-permute-start.12 = (f32[2,128,256]{2,1,0:T(8,128)S(1)}, f32[2,128,256]{2,1,0:T(8,128)S(1)}, u32[]{:S(2)}, u32[]{:S(2)}) collective-permute-start(f32[2,128,256]{2,1,0:T(8,128)S(1)} %collective-permute-done.8.refs_7_), channel_id=1, source_target_pairs={{0,2},{2,4},{4,6},{3,1},{5,3},{7,5},{8,10},{10,12},{12,14},{11,9},... | collective-permute-start | bytes 786440 | tf_op jit(solution)/shard_map/ppermute | solution.py:158
  55.4 4.4 %collective-permute-start.13 = (f32[2,128,256]{2,1,0:T(8,128)S(1)}, f32[2,128,256]{2,1,0:T(8,128)S(1)}, u32[]{:S(2)}, u32[]{:S(2)}) collective-permute-start(f32[2,128,256]{2,1,0:T(8,128)S(1)} %collective-permute-done.9.refs_8_), channel_id=1, source_target_pairs={{0,2},{2,4},{4,6},{3,1},{5,3},{7,5},{8,10},{10,12},{12,14},{11,9},... | collective-permute-start | bytes 786440 | tf_op jit(solution)/shard_map/ppermute | solution.py:158
  59.8 5.4 %collective-permute-done.13.refs_12_ = f32[2,128,256]{2,1,0:T(8,128)S(1)} collective-permute-done((f32[2,128,256]{2,1,0:T(8,128)S(1)}, f32[2,128,256]{2,1,0:T(8,128)S(1)}, u32[]{:S(2)}, u32[]{:S(2)}) %collective-permute-start.13) | collective-permute-done | bytes 262176 | tf_op jit(solution)/shard_map/ppermute | solution.py:158
  65.2 3.9 %shard_map.79 = (f32[256,128]{1,0:T(8,128)S(1)}, f32[8,128,128]{2,1,0:T(8,128)S(1)}) custom-call(s32[8,8]{1,0:T(8,128)S(1)} %fusion.refs_0_.slots, f32[2,128,256]{2,1,0:T(8,128)S(1)} %get-tuple-element.38.refs_1_, f32[2,128,256]{2,1,0:T(8,128)S(1)} %get-tuple-element.39.refs_2_, f32[2,128,256]{2,1,0:T(8,128)S(1)} %get-tuple-element.40.refs_3_, ...), custom_call_target="tpu_custom_call" | custom-call | flops 6600000000 | tf_op jit(solution)/shard_map/pallas_call | solution.py:391
  69.1 1.7 %collective-permute-start.17 = (f32[256,128]{1,0:T(8,128)S(1)}, f32[256,128]{1,0:T(8,128)S(1)}, u32[]{:S(2)}, u32[]{:S(2)}) collective-permute-start(f32[256,128]{1,0:T(8,128)S(1)} %get-tuple-element.43.refs_0_.own_f), channel_id=1, source_target_pairs={{0,1},{1,0},{2,3},{3,2},{4,5},{5,4},{6,7},{7,6},{8,9},{9,8},{10,11... | collective-permute-start | bytes 393224 | tf_op jit(solution)/shard_map/ppermute | solution.py:152
  70.9 1.5 %collective-permute-start.15 = (f32[256,128]{1,0:T(8,128)S(1)}, f32[256,128]{1,0:T(8,128)S(1)}, u32[]{:S(2)}, u32[]{:S(2)}) collective-permute-start(f32[256,128]{1,0:T(8,128)S(1)} %get-tuple-element.43.refs_0_.own_f), channel_id=1, source_target_pairs={{16,0},{24,8},{0,16},{8,24},{17,1},{25,9},{1,17},{9,25},{18,2},{26... | collective-permute-start | bytes 393224 | tf_op jit(solution)/shard_map/ppermute | solution.py:186
  72.7 1.4 %collective-permute-done.17.first_f = f32[256,128]{1,0:T(8,128)S(1)} collective-permute-done((f32[256,128]{1,0:T(8,128)S(1)}, f32[256,128]{1,0:T(8,128)S(1)}, u32[]{:S(2)}, u32[]{:S(2)}) %collective-permute-start.17) | collective-permute-done | bytes 131104 | tf_op jit(solution)/shard_map/ppermute | solution.py:152
  74.2 4.6 %collective-permute-start.18 = (f32[256,128]{1,0:T(8,128)S(1)}, f32[256,128]{1,0:T(8,128)S(1)}, u32[]{:S(2)}, u32[]{:S(2)}) collective-permute-start(f32[256,128]{1,0:T(8,128)S(1)} %collective-permute-done.17.first_f), channel_id=1, source_target_pairs={{0,2},{2,4},{4,6},{3,1},{5,3},{7,5},{8,10},{10,12},{12,14},{11,9},... | collective-permute-start | bytes 393224 | tf_op jit(solution)/shard_map/ppermute | solution.py:158
  81.1 3.6 %shard_map.81 = f32[288,128]{1,0:T(8,128)S(1)} custom-call(s32[8,8]{1,0:T(8,128)S(1)} %fusion.refs_0_.slots, f32[256,128]{1,0:T(8,128)S(1)} %get-tuple-element.43.refs_0_.own_f, f32[256,128]{1,0:T(8,128)S(1)} %collective-permute-done.17.first_f, f32[256,128]{1,0:T(8,128)S(1)} %collective-permute-done.18.second_f, ...), custom_call_target="tpu_custom_call" | custom-call | flops 4180000000 | tf_op jit(solution)/shard_map/pallas_call | solution.py:469
  86.1 1.7 %collective-permute-start.21 = (f32[136,128]{1,0:T(8,128)S(1)}, f32[136,128]{1,0:T(8,128)S(1)}, u32[]{:S(2)}, u32[]{:S(2)}) collective-permute-start(f32[136,128]{1,0:T(8,128)S(1)} %pad_maximum_fusion.1), channel_id=1, source_target_pairs={{0,1},{1,0},{2,3},{3,2},{4,5},{5,4},{6,7},{7,6},{8,9},{9,8},{10,11... | collective-permute-start | bytes 208904 | tf_op jit(solution)/shard_map/ppermute | solution.py:197
  87.9 1.6 %collective-permute-start.20 = (f32[512,128]{1,0:T(8,128)S(1)}, f32[512,128]{1,0:T(8,128)S(1)}, u32[]{:S(2)}, u32[]{:S(2)}) collective-permute-start(f32[512,128]{1,0:T(8,128)S(1)} %pad_maximum_fusion), channel_id=1, source_target_pairs={{0,16},{8,24},{16,0},{24,8},{1,17},{9,25},{17,1},{25,9},{2,18},{10... | collective-permute-start | bytes 786440 | tf_op jit(solution)/shard_map/ppermute | solution.py:174
  90.5 2.5 %collective-permute-start.22 = (f32[136,128]{1,0:T(8,128)S(1)}, f32[136,128]{1,0:T(8,128)S(1)}, u32[]{:S(2)}, u32[]{:S(2)}) collective-permute-start(f32[136,128]{1,0:T(8,128)S(1)} %fusion.3), channel_id=1, source_target_pairs={{0,2},{1,3},{2,0},{3,1},{4,6},{5,7},{6,4},{7,5},{8,10},{9,11},{10,... | collective-permute-start | bytes 208904 | tf_op jit(solution)/shard_map/ppermute | solution.py:197
  93.0 2.3 %collective-permute-done.22 = f32[136,128]{1,0:T(8,128)S(1)} collective-permute-done((f32[136,128]{1,0:T(8,128)S(1)}, f32[136,128]{1,0:T(8,128)S(1)}, u32[]{:S(2)}, u32[]{:S(2)}) %collective-permute-start.22) | collective-permute-done | bytes 69664 | tf_op jit(solution)/shard_map/ppermute | solution.py:197
  95.3 3.1 %collective-permute-start.23 = (f32[136,128]{1,0:T(8,128)S(1)}, f32[136,128]{1,0:T(8,128)S(1)}, u32[]{:S(2)}, u32[]{:S(2)}) collective-permute-start(f32[136,128]{1,0:T(8,128)S(1)} %add.36), channel_id=1, source_target_pairs={{0,4},{1,5},{2,6},{3,7},{4,0},{5,1},{6,2},{7,3},{8,12},{9,13},{10,... | collective-permute-start | bytes 208904 | tf_op jit(solution)/shard_map/ppermute | solution.py:197
  98.4 2.3 %collective-permute-done.23 = f32[136,128]{1,0:T(8,128)S(1)} collective-permute-done((f32[136,128]{1,0:T(8,128)S(1)}, f32[136,128]{1,0:T(8,128)S(1)}, u32[]{:S(2)}, u32[]{:S(2)}) %collective-permute-start.23) | collective-permute-done | bytes 69664 | tf_op jit(solution)/shard_map/ppermute | solution.py:197
  100.8 1.6 %collective-permute-start.24 = (f32[64,128]{1,0:T(8,128)S(1)}, f32[64,128]{1,0:T(8,128)S(1)}, u32[]{:S(2)}, u32[]{:S(2)}) collective-permute-start(f32[64,128]{1,0:T(8,128)S(1)} %slice.50), channel_id=1, source_target_pairs={{0,16},{8,24},{16,0},{24,8},{1,17},{9,25},{17,1},{25,9},{2,18},{10... | collective-permute-start | bytes 98312 | tf_op jit(solution)/shard_map/ppermute | solution.py:174
  102.4 4.1 %shard_map.82.refs_9_ = f32[128,128]{1,0:T(8,128)S(1)} custom-call(f32[136,128]{1,0:T(8,128)S(1)} %add.37.sums_ref), custom_call_target="tpu_custom_call" | custom-call | flops 550000000 | tf_op jit(solution)/shard_map/pallas_call | solution.py:523
  106.5 1.9 %shard_map.83 = (f32[1024,128]{1,0:T(8,128)}, f32[1024,128]{1,0:T(8,128)}, f32[128,128]{1,0:T(8,128)}) custom-call(f32[1024,128]{1,0:T(8,128)S(1)} %get-tuple-element.44.full_ref.refs_0_, f32[256,128]{1,0:T(8,128)S(1)} %slice.44.refs_1_, f32[256,128]{1,0:T(8,128)S(1)} %slice.45.refs_2_, f32[256,128]{1,0:T(8,128)S(1)} %get-tuple-element.50.refs_3_, ...), custom_call_target="tpu_custom_call" | custom-call | flops 3300000000 | tf_op jit(solution)/shard_map/pallas_call | solution.py:539
  (49 shorter events, 11.2 us)
Async XLA Ops:
  1.6 9.3 %collective-permute-start = (f32[512,128]{1,0:T(8,128)S(1)}, f32[512,128]{1,0:T(8,128)S(1)}, u32[]{:S(2)}, u32[]{:S(2)}) collective-permute-start(f32[512,128]{1,0:T(8,128)S(1)} %bitcast.1), channel_id=1, source_target_pairs={{0,1},{1,0},{2,3},{3,2},{4,5},{5,4},{6,7},{7,6},{8,9},{9,8},{10,11... | collective-permute-start | bytes 786440 | tf_op jit(solution)/shard_map/ppermute | solution.py:152
  4.7 0.7 copy-start
  5.3 18.1 %copy-start.3 = (s32[8,8]{1,0:T(8,128)S(1)}, s32[8,8]{1,0:T(8,128)}, u32[]{:S(2)}) copy-start(s32[8,8]{1,0:T(8,128)} %param.5) | copy-start | bytes 772
  5.3 18.2 %copy-start.1 = (f32[8,128]{1,0:T(8,128)S(1)}, f32[8,128]{1,0:T(8,128)}, u32[]{:S(2)}) copy-start(f32[8,128]{1,0:T(8,128)} %refs_19_.1) | copy-start | bytes 12292
  11.0 5.2 %collective-permute-start.1 = (f32[264,128]{1,0:T(8,128)S(1)}, f32[264,128]{1,0:T(8,128)S(1)}, u32[]{:S(2)}, u32[]{:S(2)}) collective-permute-start(f32[264,128]{1,0:T(8,128)S(1)} %get-tuple-element.30), channel_id=1, source_target_pairs={{0,1},{1,0},{2,3},{3,2},{4,5},{5,4},{6,7},{7,6},{8,9},{9,8},{10,11... | collective-permute-start | bytes 405512 | tf_op jit(solution)/shard_map/ppermute | solution.py:152
  12.7 9.3 %collective-permute-start.4 = (f32[512,128]{1,0:T(8,128)S(1)}, f32[512,128]{1,0:T(8,128)S(1)}, u32[]{:S(2)}, u32[]{:S(2)}) collective-permute-start(f32[512,128]{1,0:T(8,128)S(1)} %collective-permute-done.refs_4_), channel_id=1, source_target_pairs={{0,2},{2,4},{4,6},{3,1},{5,3},{7,5},{8,10},{10,12},{12,14},{11,9},... | collective-permute-start | bytes 786440 | tf_op jit(solution)/shard_map/ppermute | solution.py:158
  16.2 7.3 %collective-permute-start.3 = (f32[264,128]{1,0:T(8,128)S(1)}, f32[264,128]{1,0:T(8,128)S(1)}, u32[]{:S(2)}, u32[]{:S(2)}) collective-permute-start(f32[264,128]{1,0:T(8,128)S(1)} %collective-permute-done.1.refs_3_), channel_id=1, source_target_pairs={{0,2},{2,4},{4,6},{3,1},{5,3},{7,5},{8,10},{10,12},{12,14},{11,9},... | collective-permute-start | bytes 405512 | tf_op jit(solution)/shard_map/ppermute | solution.py:158
  19.7 3.8 %collective-permute-start.2 = (f32[512,128]{1,0:T(8,128)S(1)}, f32[512,128]{1,0:T(8,128)S(1)}, u32[]{:S(2)}, u32[]{:S(2)}) collective-permute-start(f32[512,128]{1,0:T(8,128)S(1)} %collective-permute-done.refs_4_), channel_id=1, source_target_pairs={{0,8},{8,0},{16,24},{24,16},{1,9},{9,1},{17,25},{25,17},{2,10},{10... | collective-permute-start | bytes 786440 | tf_op jit(solution)/shard_map/ppermute | solution.py:170
  19.8 5.4 %copy-start.2 = (bf16[8,256,1024]{2,1,0:T(8,128)(2,1)S(1)}, bf16[8,256,1024]{2,1,0:T(8,128)(2,1)}, u32[]{:S(2)}) copy-start(bf16[8,256,1024]{2,1,0:T(8,128)(2,1)} %get-tuple-element.34.refs_3_.refs_14_.c) | copy-start | bytes 12582916
  23.5 1.7 %collective-permute-start.5 = (f32[512,128]{1,0:T(8,128)S(1)}, f32[512,128]{1,0:T(8,128)S(1)}, u32[]{:S(2)}, u32[]{:S(2)}) collective-permute-start(f32[512,128]{1,0:T(8,128)S(1)} %collective-permute-done.4.refs_9_), channel_id=1, source_target_pairs={{0,8},{8,0},{16,24},{24,16},{1,9},{9,1},{17,25},{25,17},{2,10},{10... | collective-permute-start | bytes 786440 | tf_op jit(solution)/shard_map/ppermute | solution.py:170
  29.8 9.2 %collective-permute-start.6 = (f32[2,128,256]{2,1,0:T(8,128)S(1)}, f32[2,128,256]{2,1,0:T(8,128)S(1)}, u32[]{:S(2)}, u32[]{:S(2)}) collective-permute-start(f32[2,128,256]{2,1,0:T(8,128)S(1)} %get-tuple-element.38.refs_1_), channel_id=1, source_target_pairs={{0,1},{1,0},{2,3},{3,2},{4,5},{5,4},{6,7},{7,6},{8,9},{9,8},{10,11... | collective-permute-start | bytes 786440 | tf_op jit(solution)/shard_map/ppermute | solution.py:152
  31.5 13.0 %collective-permute-start.7 = (f32[2,128,256]{2,1,0:T(8,128)S(1)}, f32[2,128,256]{2,1,0:T(8,128)S(1)}, u32[]{:S(2)}, u32[]{:S(2)}) collective-permute-start(f32[2,128,256]{2,1,0:T(8,128)S(1)} %get-tuple-element.39.refs_2_), channel_id=1, source_target_pairs={{0,1},{1,0},{2,3},{3,2},{4,5},{5,4},{6,7},{7,6},{8,9},{9,8},{10,11... | collective-permute-start | bytes 786440 | tf_op jit(solution)/shard_map/ppermute | solution.py:152
  31.9 18.3 %collective-permute-start.8 = (f32[2,128,256]{2,1,0:T(8,128)S(1)}, f32[2,128,256]{2,1,0:T(8,128)S(1)}, u32[]{:S(2)}, u32[]{:S(2)}) collective-permute-start(f32[2,128,256]{2,1,0:T(8,128)S(1)} %get-tuple-element.40.refs_3_), channel_id=1, source_target_pairs={{0,1},{1,0},{2,3},{3,2},{4,5},{5,4},{6,7},{7,6},{8,9},{9,8},{10,11... | collective-permute-start | bytes 786440 | tf_op jit(solution)/shard_map/ppermute | solution.py:152
  33.5 21.9 %collective-permute-start.9 = (f32[2,128,256]{2,1,0:T(8,128)S(1)}, f32[2,128,256]{2,1,0:T(8,128)S(1)}, u32[]{:S(2)}, u32[]{:S(2)}) collective-permute-start(f32[2,128,256]{2,1,0:T(8,128)S(1)} %get-tuple-element.41.refs_4_), channel_id=1, source_target_pairs={{0,1},{1,0},{2,3},{3,2},{4,5},{5,4},{6,7},{7,6},{8,9},{9,8},{10,11... | collective-permute-start | bytes 786440 | tf_op jit(solution)/shard_map/ppermute | solution.py:152
  38.9 20.9 %collective-permute-start.10 = (f32[2,128,256]{2,1,0:T(8,128)S(1)}, f32[2,128,256]{2,1,0:T(8,128)S(1)}, u32[]{:S(2)}, u32[]{:S(2)}) collective-permute-start(f32[2,128,256]{2,1,0:T(8,128)S(1)} %collective-permute-done.6.refs_5_), channel_id=1, source_target_pairs={{0,2},{2,4},{4,6},{3,1},{5,3},{7,5},{8,10},{10,12},{12,14},{11,9},... | collective-permute-start | bytes 786440 | tf_op jit(solution)/shard_map/ppermute | solution.py:158
  44.5 15.3 %collective-permute-start.11 = (f32[2,128,256]{2,1,0:T(8,128)S(1)}, f32[2,128,256]{2,1,0:T(8,128)S(1)}, u32[]{:S(2)}, u32[]{:S(2)}) collective-permute-start(f32[2,128,256]{2,1,0:T(8,128)S(1)} %collective-permute-done.7.refs_6_), channel_id=1, source_target_pairs={{0,2},{2,4},{4,6},{3,1},{5,3},{7,5},{8,10},{10,12},{12,14},{11,9},... | collective-permute-start | bytes 786440 | tf_op jit(solution)/shard_map/ppermute | solution.py:158
  50.2 9.7 %collective-permute-start.12 = (f32[2,128,256]{2,1,0:T(8,128)S(1)}, f32[2,128,256]{2,1,0:T(8,128)S(1)}, u32[]{:S(2)}, u32[]{:S(2)}) collective-permute-start(f32[2,128,256]{2,1,0:T(8,128)S(1)} %collective-permute-done.8.refs_7_), channel_id=1, source_target_pairs={{0,2},{2,4},{4,6},{3,1},{5,3},{7,5},{8,10},{10,12},{12,14},{11,9},... | collective-permute-start | bytes 786440 | tf_op jit(solution)/shard_map/ppermute | solution.py:158
  55.4 9.8 %collective-permute-start.13 = (f32[2,128,256]{2,1,0:T(8,128)S(1)}, f32[2,128,256]{2,1,0:T(8,128)S(1)}, u32[]{:S(2)}, u32[]{:S(2)}) collective-permute-start(f32[2,128,256]{2,1,0:T(8,128)S(1)} %collective-permute-done.9.refs_8_), channel_id=1, source_target_pairs={{0,2},{2,4},{4,6},{3,1},{5,3},{7,5},{8,10},{10,12},{12,14},{11,9},... | collective-permute-start | bytes 786440 | tf_op jit(solution)/shard_map/ppermute | solution.py:158
  69.1 5.0 %collective-permute-start.17 = (f32[256,128]{1,0:T(8,128)S(1)}, f32[256,128]{1,0:T(8,128)S(1)}, u32[]{:S(2)}, u32[]{:S(2)}) collective-permute-start(f32[256,128]{1,0:T(8,128)S(1)} %get-tuple-element.43.refs_0_.own_f), channel_id=1, source_target_pairs={{0,1},{1,0},{2,3},{3,2},{4,5},{5,4},{6,7},{7,6},{8,9},{9,8},{10,11... | collective-permute-start | bytes 393224 | tf_op jit(solution)/shard_map/ppermute | solution.py:152
  70.9 7.9 %collective-permute-start.16 = (f32[256,128]{1,0:T(8,128)S(1)}, f32[256,128]{1,0:T(8,128)S(1)}, u32[]{:S(2)}, u32[]{:S(2)}) collective-permute-start(f32[256,128]{1,0:T(8,128)S(1)} %get-tuple-element.43.refs_0_.own_f), channel_id=1, source_target_pairs={{24,0},{16,8},{8,16},{0,24},{25,1},{17,9},{9,17},{1,25},{26,2},{18... | collective-permute-start | bytes 393224 | tf_op jit(solution)/shard_map/ppermute | solution.py:186
  70.9 8.6 %collective-permute-start.15 = (f32[256,128]{1,0:T(8,128)S(1)}, f32[256,128]{1,0:T(8,128)S(1)}, u32[]{:S(2)}, u32[]{:S(2)}) collective-permute-start(f32[256,128]{1,0:T(8,128)S(1)} %get-tuple-element.43.refs_0_.own_f), channel_id=1, source_target_pairs={{16,0},{24,8},{0,16},{8,24},{17,1},{25,9},{1,17},{9,25},{18,2},{26... | collective-permute-start | bytes 393224 | tf_op jit(solution)/shard_map/ppermute | solution.py:186
  72.4 7.1 %collective-permute-start.14 = (f32[256,128]{1,0:T(8,128)S(1)}, f32[256,128]{1,0:T(8,128)S(1)}, u32[]{:S(2)}, u32[]{:S(2)}) collective-permute-start(f32[256,128]{1,0:T(8,128)S(1)} %get-tuple-element.43.refs_0_.own_f), channel_id=1, source_target_pairs={{8,0},{0,8},{24,16},{16,24},{9,1},{1,9},{25,17},{17,25},{10,2},{2,... | collective-permute-start | bytes 393224 | tf_op jit(solution)/shard_map/ppermute | solution.py:186
  74.2 6.9 %collective-permute-start.18 = (f32[256,128]{1,0:T(8,128)S(1)}, f32[256,128]{1,0:T(8,128)S(1)}, u32[]{:S(2)}, u32[]{:S(2)}) collective-permute-start(f32[256,128]{1,0:T(8,128)S(1)} %collective-permute-done.17.first_f), channel_id=1, source_target_pairs={{0,2},{2,4},{4,6},{3,1},{5,3},{7,5},{8,10},{10,12},{12,14},{11,9},... | collective-permute-start | bytes 393224 | tf_op jit(solution)/shard_map/ppermute | solution.py:158
  84.7 1.4 %collective-permute-start.19 = (f32[288,128]{1,0:T(8,128)S(1)}, f32[288,128]{1,0:T(8,128)S(1)}, u32[]{:S(2)}, u32[]{:S(2)}) collective-permute-start(f32[288,128]{1,0:T(8,128)S(1)} %shard_map.81), channel_id=1, source_target_pairs={{0,8},{8,0},{16,24},{24,16},{1,9},{9,1},{17,25},{25,17},{2,10},{10... | collective-permute-start | bytes 442376 | tf_op jit(solution)/shard_map/ppermute | solution.py:174
  86.1 4.4 %collective-permute-start.21 = (f32[136,128]{1,0:T(8,128)S(1)}, f32[136,128]{1,0:T(8,128)S(1)}, u32[]{:S(2)}, u32[]{:S(2)}) collective-permute-start(f32[136,128]{1,0:T(8,128)S(1)} %pad_maximum_fusion.1), channel_id=1, source_target_pairs={{0,1},{1,0},{2,3},{3,2},{4,5},{5,4},{6,7},{7,6},{8,9},{9,8},{10,11... | collective-permute-start | bytes 208904 | tf_op jit(solution)/shard_map/ppermute | solution.py:197
  87.9 12.8 %collective-permute-start.20 = (f32[512,128]{1,0:T(8,128)S(1)}, f32[512,128]{1,0:T(8,128)S(1)}, u32[]{:S(2)}, u32[]{:S(2)}) collective-permute-start(f32[512,128]{1,0:T(8,128)S(1)} %pad_maximum_fusion), channel_id=1, source_target_pairs={{0,16},{8,24},{16,0},{24,8},{1,17},{9,25},{17,1},{25,9},{2,18},{10... | collective-permute-start | bytes 786440 | tf_op jit(solution)/shard_map/ppermute | solution.py:174
  90.5 4.8 %collective-permute-start.22 = (f32[136,128]{1,0:T(8,128)S(1)}, f32[136,128]{1,0:T(8,128)S(1)}, u32[]{:S(2)}, u32[]{:S(2)}) collective-permute-start(f32[136,128]{1,0:T(8,128)S(1)} %fusion.3), channel_id=1, source_target_pairs={{0,2},{1,3},{2,0},{3,1},{4,6},{5,7},{6,4},{7,5},{8,10},{9,11},{10,... | collective-permute-start | bytes 208904 | tf_op jit(solution)/shard_map/ppermute | solution.py:197
  95.3 5.4 %collective-permute-start.23 = (f32[136,128]{1,0:T(8,128)S(1)}, f32[136,128]{1,0:T(8,128)S(1)}, u32[]{:S(2)}, u32[]{:S(2)}) collective-permute-start(f32[136,128]{1,0:T(8,128)S(1)} %add.36), channel_id=1, source_target_pairs={{0,4},{1,5},{2,6},{3,7},{4,0},{5,1},{6,2},{7,3},{8,12},{9,13},{10,... | collective-permute-start | bytes 208904 | tf_op jit(solution)/shard_map/ppermute | solution.py:197
  100.8 5.7 %collective-permute-start.24 = (f32[64,128]{1,0:T(8,128)S(1)}, f32[64,128]{1,0:T(8,128)S(1)}, u32[]{:S(2)}, u32[]{:S(2)}) collective-permute-start(f32[64,128]{1,0:T(8,128)S(1)} %slice.50), channel_id=1, source_target_pairs={{0,16},{8,24},{16,0},{24,8},{1,17},{9,25},{17,1},{25,9},{2,18},{10... | collective-permute-start | bytes 98312 | tf_op jit(solution)/shard_map/ppermute | solution.py:174
